TPU v7x, 32 devices: a whole 2x2x4 slice. The times are simulated.
32 devices in a mesh: row: 8 (over y, x, core), col: 4 (over z).
Axes of the slice: x: 2, y: 2, z: 4, core: 2. Of those that a mesh axis runs over, the one named last changes fastest.
Arguments:
- laplacian: bfloat16 [8192, 8192], P('row', 'col')
- interp: bfloat16 [8192, 128], P('row'), may hold values from -0.375 to 0.375
- vectors: bfloat16 [32, 8192], P(None, 'row'), may hold values from -6 to 6
- pairs: int32 [32, 2], replicated, may hold values from 0 to 63, as said below
Outputs:
- coarse: bfloat16 [4096, 4096], P(('row', 'col'))
- coarse_vectors: bfloat16 [32, 4096], P(None, 'row')
Inputs may be any that keep to these rules, and one draw needn't show every extreme that they name: Row c holds (a, b), where a lies among the 8 fine tile rows of row index g = (c // 4) mod 4, that is a // 8 == g, and b // 8 == g + 4. Every fine tile row appears exactly once in pairs.
All inputs are finite; a program needn't handle non-finite values.
Results may differ from a plain program's by a relative error of at most 0.0058.
Values may be sent and summed in bfloat16 or wider, within the bound.
No kernel may reach another device: no remote copies, remote signals or barrier semaphores. Data moves between devices by JAX's collectives and lax.ppermute only.
A program may use at most 64 MiB of HBM per device.

v0:
```python
import jax
import jax.numpy as jnp
from jax import lax
from jax.sharding import PartitionSpec as P


def from_partner(block, axis, bit):
    count = lax.axis_size(axis)
    route = []
    for low in range(count):
        high = low | 1 << bit
        if high != low and high < count:
            route += [(low, high), (high, low)]
    return lax.ppermute(block, axis, route)


def on_device(laplacian, interp, vectors, pairs):
    tile_size = interp.shape[1]
    fine_rows = interp.shape[0] // tile_size
    fine_cols = laplacian.shape[1] // tile_size
    vector_count = vectors.shape[0]
    row_count = lax.axis_size("row")
    col_count = lax.axis_size("col")
    row_index = lax.axis_index("row")
    col_index = lax.axis_index("col")
    every_interp = lax.all_gather(interp, "row", axis=0, tiled=True)
    col_interp = lax.dynamic_slice_in_dim(
        every_interp, col_index * (fine_cols * tile_size), fine_cols * tile_size, 0
    )
    product = jnp.einsum(
        "xjy,jyb->xjb",
        laplacian.reshape(fine_rows * tile_size, fine_cols, tile_size),
        col_interp.reshape(fine_cols, tile_size, tile_size),
        preferred_element_type=jnp.float32,
    ).astype(jnp.bfloat16)
    row_blocks = interp.reshape(fine_rows, tile_size, tile_size)
    projected = jnp.einsum(
        "ixa,ixjb->iajb",
        row_blocks,
        product.reshape(fine_rows, tile_size, fine_cols, tile_size),
        preferred_element_type=jnp.float32,
    ).astype(jnp.bfloat16)
    projected = projected.reshape(fine_rows, tile_size, fine_cols * tile_size)
    restricted = jnp.einsum(
        "kix,ixa->kia",
        vectors.reshape(vector_count, fine_rows, tile_size),
        row_blocks,
        preferred_element_type=jnp.float32,
    ).astype(jnp.bfloat16)
    coarse_rows = fine_rows // 2
    upper_row = row_index >= row_count // 2
    partner_row = (row_index + row_count // 2) % row_count
    own_pairs = lax.dynamic_slice_in_dim(pairs, row_index * coarse_rows, coarse_rows, 0)
    local_rows = jnp.where(upper_row, own_pairs[:, 1], own_pairs[:, 0]) - row_index * fine_rows
    row_bit = row_count.bit_length() - 2
    mate_pairs = lax.dynamic_slice_in_dim(pairs, partner_row * coarse_rows, coarse_rows, 0)
    wanted = jnp.where(upper_row, mate_pairs[:, 1], mate_pairs[:, 0]) - row_index * fine_rows
    far_proj, far_vec = from_partner(
        (jnp.take(projected, wanted, axis=0), jnp.take(restricted, wanted, axis=1)), "row", row_bit
    )
    row_sum = jnp.take(projected, local_rows, axis=0).astype(jnp.float32) + far_proj.astype(
        jnp.float32
    )
    coarse_vectors = jnp.take(restricted, local_rows, axis=1).astype(jnp.float32) + far_vec.astype(
        jnp.float32
    )
    coarse_vectors = coarse_vectors.astype(jnp.bfloat16).reshape(
        vector_count, coarse_rows * tile_size
    )
    coarse_cols = fine_cols // 2
    summed = row_sum.reshape(coarse_rows * tile_size, fine_cols, tile_size)
    upper_col = col_index >= col_count // 2
    partner_col = (col_index + col_count // 2) % col_count
    col_pairs = lax.dynamic_slice_in_dim(pairs, col_index * coarse_cols, coarse_cols, 0)
    local_cols = jnp.where(upper_col, col_pairs[:, 1], col_pairs[:, 0]) - col_index * fine_cols
    col_bit = col_count.bit_length() - 2
    mate_cols = lax.dynamic_slice_in_dim(pairs, partner_col * coarse_cols, coarse_cols, 0)
    wanted_cols = jnp.where(upper_col, mate_cols[:, 1], mate_cols[:, 0]) - col_index * fine_cols
    far_cols = from_partner(jnp.take(summed, wanted_cols, axis=1), "col", col_bit)
    block = (jnp.take(summed, local_cols, axis=1) + far_cols).astype(jnp.bfloat16)
    block = block.reshape(coarse_rows * tile_size, coarse_cols * tile_size)
    coarse = lax.all_to_all(block, "col", split_axis=0, concat_axis=1, tiled=True)
    return (coarse, coarse_vectors)


def solution(mesh):
    placed = (P("row", "col"), P("row", None), P(None, "row"), P())
    return jax.shard_map(
        on_device,
        mesh=mesh,
        in_specs=placed,
        out_specs=(P(("row", "col"), None), P(None, "row")),
        check_vma=False,
    )
```

profile of v0, /device:TPU:0, one launch (start us, length us, event | category | flops | bytes accessed | tf_op | source)
XLA Modules:
  0.0 255.1 jit_solution(3137058183636399822)
XLA Ops:
  7.2 0.7 all-gather.2.cloned.1.call-update
  7.9 0.8 constant_dynamic-slice_fusion.3
  8.8 31.7 %all-gather.2.cloned.1.call-done = bf16[8192,128]{1,0:T(8,128)(2,1)} async-done(((bf16[1024,128]{1,0:T(8,128)(2,1)}), bf16[8192,128]{1,0:T(8,128)(2,1)}) %all-gather.2.cloned.1.call-update) | async-done | bytes 2097168 | tf_op jit(solution)/shard_map/all_gather | solution.py:26
  40.5 1.1 constant_dynamic-slice_fusion.4
  41.6 3.5 %convert_bitcast_fusion = bf16[16,16,8,8,128]{4,3,2,1,0:T(8,128)(2,1)S(1)} fusion(bf16[16,128,128]{2,1,0:T(8,128)(2,1)S(1)} %bitcast.86, bf16[1024,2048]{1,0:T(8,128)(2,1)} %param.10), kind=kOutput, calls=%fused_computation.13 | convolution fusion | flops 538968064 | bytes 8912896 | tf_op jit(solution)/shard_map/xjy,jyb->xjb/dot_general | solution.py:30
  45.2 3.2 %fusion.8 = bf16[8,16,128,128]{3,2,1,0:T(8,128)(2,1)} fusion(bf16[8,128,128,1]{2,1,3,0:T(8,128)(2,1)S(1)} %bitcast.84, bf16[16,16,8,8,128]{4,3,2,1,0:T(8,128)(2,1)S(1)} %convert_bitcast_fusion), kind=kOutput, calls=%fused_computation.14 | convolution fusion | flops 538968064 | bytes 8650752 | tf_op jit(solution)/shard_map/ixa,ixjb->iajb/dot_general | solution.py:37
  48.4 6.6 %copy.20 = bf16[8,128,2048]{2,1,0:T(8,128)(2,1)} copy(bf16[8,128,2048]{1,2,0:T(8,128)(2,1)} %bitcast.80) | data formatting | bytes 8388608 | tf_op jit(solution)/shard_map/reshape | solution.py:43
  55.0 2.9 %gather_fusion.1 = bf16[4,128,2048]{2,1,0:T(8,128)(2,1)S(1)} fusion(bf16[8,128,2048]{2,1,0:T(8,128)(2,1)} %copy.20, s32[1024]{0:T(1024)S(1)} %pad_clamp_fusion.2), kind=kCustom, calls=%fused_computation.3.clone | custom fusion | bytes 4194320 | tf_op jit(solution)/shard_map/jit(_take)/gather | solution.py:59
  57.9 1.6 broadcast_select_fusion
  59.5 1.4 collective-permute-start
  61.0 2.9 %gather_fusion = bf16[4,128,2048]{2,1,0:T(8,128)(2,1)S(1)} fusion(bf16[8,128,2048]{2,1,0:T(8,128)(2,1)} %copy.20, s32[1024]{0:T(1024)S(1)} %pad_clamp_fusion.3), kind=kCustom, calls=%fused_computation.clone | custom fusion | bytes 4194320 | tf_op jit(solution)/shard_map/jit(_take)/gather | solution.py:61
  63.9 43.7 %collective-permute-done = bf16[4,128,2048]{2,1,0:T(8,128)(2,1)} collective-permute-done((bf16[4,128,2048]{2,1,0:T(8,128)(2,1)}, bf16[4,128,2048]{2,1,0:T(8,128)(2,1)}, u32[]{:S(2)}, u32[]{:S(2)}) %collective-permute-start) | collective-permute-done | bytes 2097184 | tf_op jit(solution)/shard_map/ppermute | solution.py:14
  107.6 2.5 convert_add_fusion
  110.1 0.9 copy.35
  111.0 3.2 %copy.22 = f32[512,16,128]{2,0,1:T(8,128)} copy(f32[512,16,128]{2,1,0:T(8,128)S(1)} %bitcast.81) | data formatting | bytes 8388608 | tf_op jit(solution)/shard_map/reshape | solution.py:71
  114.3 2.9 %gather_fusion.3 = f32[8,512,128]{2,1,0:T(8,128)S(1)} fusion(f32[512,16,128]{2,0,1:T(8,128)} %copy.22, s32[1024]{0:T(1024)S(1)} %pad_clamp_fusion), kind=kCustom, calls=%fused_computation.4.clone | custom fusion | bytes 4194336 | tf_op jit(solution)/shard_map/jit(_take)/gather | solution.py:79
  117.2 1.6 select_bitcast_fusion
  118.8 2.4 collective-permute-start.1
  121.2 2.9 %gather_fusion.2 = f32[8,512,128]{2,1,0:T(8,128)S(1)} fusion(f32[512,16,128]{2,0,1:T(8,128)} %copy.22, s32[1024]{0:T(1024)S(1)} %pad_clamp_fusion.1), kind=kCustom, calls=%fused_computation.1.clone | custom fusion | bytes 4194336 | tf_op jit(solution)/shard_map/jit(_take)/gather | solution.py:80
  124.1 87.8 %collective-permute-done.1 = f32[512,8,128]{2,0,1:T(8,128)} collective-permute-done((f32[512,8,128]{2,0,1:T(8,128)}, f32[512,8,128]{2,0,1:T(8,128)}, u32[]{:S(2)}, u32[]{:S(2)}) %collective-permute-start.1) | collective-permute-done | bytes 2097184 | tf_op jit(solution)/shard_map/ppermute | solution.py:14
  211.9 1.9 fusion.11
  213.8 0.7 copy.24
  214.5 1.3 all_to_all.14
  215.8 4.6 %all-to-all-start = ((bf16[4,128,1024]{2,1,0:T(8,128)(2,1)}), bf16[4,128,1024]{2,1,0:T(8,128)(2,1)S(1)}, u32[]{:S(2)}, u32[]{:S(2)}) async-start(bf16[4,128,1024]{2,1,0:T(8,128)(2,1)} %all_to_all.14), calls=%async_computation | async-start | bytes 2097152 | tf_op jit(solution)/shard_map/all_to_all | solution.py:82
  220.5 0.6 gather_fusion.5
  221.2 1.3 collective-permute-start.2
  222.5 0.6 gather_fusion.4
  223.1 2.0 collective-permute-done.2
  225.1 0.7 copy_bitcast_fusion
  225.8 20.5 %all-to-all-done = bf16[4,128,1024]{2,1,0:T(8,128)(2,1)S(1)} async-done(((bf16[4,128,1024]{2,1,0:T(8,128)(2,1)}), bf16[4,128,1024]{2,1,0:T(8,128)(2,1)S(1)}, u32[]{:S(2)}, u32[]{:S(2)}) %all-to-all-start) | async-done | bytes 1048608 | tf_op jit(solution)/shard_map/all_to_all | solution.py:82
  246.3 0.7 copy.25
  246.9 1.3 copy.28
  (18 shorter events, 0.5 us)
Async XLA Ops:
  7.2 213.2 %copy-start = (bf16[32,1024]{1,0:T(8,128)(2,1)S(1)}, bf16[32,1024]{1,0:T(8,128)(2,1)}, u32[]{:S(2)}) copy-start(bf16[32,1024]{1,0:T(8,128)(2,1)} %param.12) | copy-start | bytes 196612
  7.2 33.4 %all-gather.2.cloned.1.call-start = ((), (), s32[]{:S(2)}) async-start(), calls=%async_computation.1 | async-start | bytes 2359296 | tf_op jit(solution)/shard_map/all_gather | solution.py:26
  41.6 3.6 %copy-start.1 = (bf16[1024,128]{1,0:T(8,128)(2,1)S(1)}, bf16[1024,128]{1,0:T(8,128)(2,1)}, u32[]{:S(2)}) copy-start(bf16[1024,128]{1,0:T(8,128)(2,1)} %param.11) | copy-start | bytes 786436
  57.9 3.0 %copy-start.2 = (s32[32,2]{0,1:T(2,128)S(1)}, s32[32,2]{0,1:T(2,128)}, u32[]{:S(2)}) copy-start(s32[32,2]{0,1:T(2,128)} %param.13) | copy-start | bytes 772
  59.5 48.1 %collective-permute-start = (bf16[4,128,2048]{2,1,0:T(8,128)(2,1)}, bf16[4,128,2048]{2,1,0:T(8,128)(2,1)}, u32[]{:S(2)}, u32[]{:S(2)}) collective-permute-start(bf16[4,128,2048]{2,1,0:T(8,128)(2,1)} %broadcast_select_fusion), channel_id=1, source_target_pairs={{0,16},{16,0},{4,20},{20,4},{8,24},{24,8},{12,28},{28,12},{1,17},{... | collective-permute-start | bytes 6291464 | tf_op jit(solution)/shard_map/ppermute | solution.py:14
  118.8 93.1 %collective-permute-start.1 = (f32[512,8,128]{2,0,1:T(8,128)}, f32[512,8,128]{2,0,1:T(8,128)}, u32[]{:S(2)}, u32[]{:S(2)}) collective-permute-start(f32[512,8,128]{2,0,1:T(8,128)} %select_bitcast_fusion), channel_id=1, source_target_pairs={{0,2},{2,0},{1,3},{3,1},{4,6},{6,4},{5,7},{7,5},{8,10},{10,8},{9,1... | collective-permute-start | bytes 6291464 | tf_op jit(solution)/shard_map/ppermute | solution.py:14
  215.8 30.5 %all-to-all-start = ((bf16[4,128,1024]{2,1,0:T(8,128)(2,1)}), bf16[4,128,1024]{2,1,0:T(8,128)(2,1)S(1)}, u32[]{:S(2)}, u32[]{:S(2)}) async-start(bf16[4,128,1024]{2,1,0:T(8,128)(2,1)} %all_to_all.14), calls=%async_computation | async-start | bytes 2097152 | tf_op jit(solution)/shard_map/all_to_all | solution.py:82
  221.2 3.9 %collective-permute-start.2 = (bf16[32,4,128]{2,0,1:T(8,128)(2,1)S(1)}, bf16[32,4,128]{2,0,1:T(8,128)(2,1)S(1)}, u32[]{:S(2)}, u32[]{:S(2)}) collective-permute-start(bf16[32,4,128]{2,0,1:T(8,128)(2,1)S(1)} %select_bitcast_fusion.1), channel_id=1, source_target_pairs={{0,16},{16,0},{4,20},{20,4},{8,24},{24,8},{12,28},{28,12},{1,17},{... | collective-permute-start | bytes 98312 | tf_op jit(solution)/shard_map/ppermute | solution.py:14
Sparse Core Ops, SparseCore 0:
  9.9 30.5 all-gather.1
where the time goes:
time: 256 us; the launch traced here: 255 us
  waiting for transfers between devices  186 us (73%)
  local copies, waits for them, and re-layouts  29.3 us (11%)
  between operations  14.2 us (6%)
  starting transfers between devices  9.78 us (4%)
  other arithmetic  8.46 us (3%)
  matrix products  6.95 us (3%)
    ppermute x3, waiting for transfers between devices, from_partner(): return lax.ppermute(block, axis, route)  134 us
    all_gather x1, waiting for transfers between devices, on_device(): every_interp = lax.all_gather(interp, 'row', axis=0, tiled=True)  31.7 us
    all_to_all x1, waiting for transfers between devices, on_device(): lax.all_to_all(block, 'col', split_axis=0, concat_axis=1, tiled=True)  20.5 us
    reshape x1, local copies, waits for them, and re-layouts, on_device(): projected = projected.reshape(fine_rows, tile_size, fine_cols * tile_size)  6.56 us
    ppermute x3, starting transfers between devices, from_partner(): return lax.ppermute(block, axis, route)  5.15 us
  transfers between devices with their start and end apart: 5, of which 5 were waited for; matrix products, arithmetic and copies ran while one was open for 3% of the time, Pallas kernels for 0%

commit v1 on v0

v1 whole, which is shorter than its diff:
```python
import functools

import jax
import jax.numpy as jnp
from jax import lax
from jax.experimental import pallas as pl
from jax.experimental.pallas import tpu as pltpu
from jax.sharding import PartitionSpec as P


def contract_rows(left, right):
    return lax.dot_general(
        left, right, (((0,), (0,)), ((), ())), preferred_element_type=jnp.float32
    )


def exchange(block, axis, flip):
    count = lax.axis_size(axis)
    return lax.ppermute(block, axis, [(i, i ^ flip) for i in range(count)])


def row_of(place, pairs, coarse_row, fine_rows, upper):
    return pairs[coarse_row, upper] - place[0] * fine_rows


def project(laplacian, interp, pairs, place, received, step, mine, width):
    tile = interp.shape[1]
    fine_rows = interp.shape[0] // tile
    coarse_rows = fine_rows // 2
    cols = laplacian.shape[1]
    half = lax.axis_size("row") // 2
    count = coarse_rows * tile // lax.axis_size("col")
    flip = 0 if mine else half

    def row_tile(pairs_ref, place_ref):
        row, col = place_ref[0], place_ref[1]
        coarse_row = (row ^ flip) * coarse_rows + (col ^ step) * count // tile
        return pairs_ref[coarse_row * 2 + row // half] - row * fine_rows

    def body(pairs_ref, place_ref, interp_ref, lap_ref, *refs):
        out_ref = refs[-1] if count == tile else refs[-2]
        result = contract_rows(interp_ref[...], lap_ref[...])
        if count != tile:
            whole_ref = refs[-1]
            whole_ref[...] = result
            begin = ((place_ref[1] ^ step) * count) % tile
            result = whole_ref[pl.ds(pl.multiple_of(begin, count), count), :]
        if received is not None:
            result = result + refs[0][...].astype(jnp.float32)
        out_ref[...] = result.astype(out_ref.dtype)

    in_specs = [
        pl.BlockSpec((tile, tile), lambda n, pr, pc: (row_tile(pr, pc), 0)),
        pl.BlockSpec((tile, width), lambda n, pr, pc: (row_tile(pr, pc), n)),
    ]
    operands = [interp, laplacian]
    if received is not None:
        in_specs.append(pl.BlockSpec((count, width), lambda n, pr, pc: (0, n)))
        operands.append(received)
    return pl.pallas_call(
        body,
        out_shape=jax.ShapeDtypeStruct((count, cols), jnp.bfloat16),
        grid_spec=pltpu.PrefetchScalarGridSpec(
            num_scalar_prefetch=2,
            grid=(cols // width,),
            in_specs=in_specs,
            out_specs=pl.BlockSpec((count, width), lambda n, pr, pc: (0, n)),
            scratch_shapes=[] if count == tile else [pltpu.VMEM((tile, width), jnp.float32)],
        ),
        cost_estimate=pl.CostEstimate(
            flops=2 * tile * tile * cols, bytes_accessed=6 * tile * cols, transcendentals=0
        ),
        name="project_mine" if mine else "project_partner",
    )(pairs, place, *operands)


def finish(near, far, every_interp, pairs, place, before, step, fine_cols):
    tile = every_interp.shape[1]
    count = near.shape[0]
    half = lax.axis_size("col") // 2
    coarse_cols = fine_cols // 2
    total = every_interp.shape[0] // 2

    def body(pairs_ref, place_ref, near_ref, far_ref, interp_ref, *refs):
        out_ref = refs[-1]
        col = place_ref[1]
        upper = col // half
        first = (pl.program_id(0) * half + (col ^ step) % half) * coarse_cols
        for k in range(coarse_cols):
            near_tile = pairs_ref[(first + k) * 2 + upper]
            far_tile = pairs_ref[(first + k) * 2 + 1 - upper]
            result = None
            for ref, j, owner in (
                (near_ref, near_tile, col ^ step),
                (far_ref, far_tile, col ^ step ^ half),
            ):
                start = pl.multiple_of((j - owner * fine_cols) * tile, tile)
                rows = pl.multiple_of(j * tile, tile)
                part = jnp.dot(
                    ref[:, pl.ds(start, tile)],
                    interp_ref[pl.ds(rows, tile), :],
                    preferred_element_type=jnp.float32,
                )
                result = part if result is None else result + part
            out_ref[:, k * tile : (k + 1) * tile] = result.astype(out_ref.dtype)

    whole = pl.BlockSpec(near.shape, lambda n, pr, pc: (0, 0))
    in_specs = [whole, whole, pl.BlockSpec(every_interp.shape, lambda n, pr, pc: (0, 0))]
    operands = [near, far, every_interp]
    aliases = {}
    if before is not None:
        in_specs.append(pl.BlockSpec(memory_space=pl.ANY))
        operands.append(before)
        aliases = {5: 0}
    return pl.pallas_call(
        body,
        out_shape=jax.ShapeDtypeStruct((count, total), jnp.bfloat16),
        grid_spec=pltpu.PrefetchScalarGridSpec(
            num_scalar_prefetch=2,
            grid=(2,),
            in_specs=in_specs,
            out_specs=pl.BlockSpec(
                (count, coarse_cols * tile),
                lambda n, pr, pc: (0, n * half + (pc[1] ^ step) % half),
            ),
        ),
        input_output_aliases=aliases,
        cost_estimate=pl.CostEstimate(
            flops=4 * count * tile * 2 * coarse_cols * tile,
            bytes_accessed=2 * every_interp.size,
            transcendentals=0,
        ),
        compiler_params=pltpu.CompilerParams(vmem_limit_bytes=40 * 1024 * 1024),
        name="finish",
    )(pairs, place, *operands)


def restrict(vectors, interp, pairs, place):
    tile = interp.shape[1]
    fine_rows = interp.shape[0] // tile
    coarse_rows = fine_rows // 2
    half = lax.axis_size("row") // 2

    def body(pairs_ref, place_ref, vec_ref, interp_ref, keep_ref, send_ref):
        row = place_ref[0]
        for out_ref, flip in ((keep_ref, 0), (send_ref, half)):
            for k in range(coarse_rows):
                i = pairs_ref[((row ^ flip) * coarse_rows + k) * 2 + row // half] - row * fine_rows
                at = pl.ds(pl.multiple_of(i * tile, tile), tile)
                out_ref[:, k * tile : (k + 1) * tile] = jnp.dot(
                    vec_ref[:, at], interp_ref[at, :], preferred_element_type=jnp.float32
                ).astype(out_ref.dtype)

    shape = jax.ShapeDtypeStruct((vectors.shape[0], coarse_rows * tile), jnp.bfloat16)
    return pl.pallas_call(
        body,
        out_shape=(shape, shape),
        in_specs=[
            pl.BlockSpec(memory_space=pltpu.SMEM),
            pl.BlockSpec(memory_space=pltpu.SMEM),
            pl.BlockSpec(memory_space=pltpu.VMEM),
            pl.BlockSpec(memory_space=pltpu.VMEM),
        ],
        out_specs=(pl.BlockSpec(memory_space=pltpu.VMEM),) * 2,
        name="restrict",
    )(pairs, place, vectors, interp)


def on_device(laplacian, interp, vectors, pairs):
    tile = interp.shape[1]
    fine_cols = laplacian.shape[1] // tile
    row_half = lax.axis_size("row") // 2
    col_count = lax.axis_size("col")
    col_half = col_count // 2
    width = min(512, laplacian.shape[1])
    place = jnp.stack([lax.axis_index("row"), lax.axis_index("col")]).astype(jnp.int32)
    pairs = pairs.reshape(-1)

    steps = list(range(col_half, col_count)) + list(range(col_half - 1, -1, -1))
    away = {}
    for step in steps:
        block = project(laplacian, interp, pairs, place, None, step, False, width)
        away[step] = exchange(block, "row", row_half)
    every_interp = lax.all_gather(interp, "row", axis=0, tiled=True)
    keep, send = restrict(vectors, interp, pairs, place)
    far_vec = exchange(send, "row", row_half)
    held = {}
    for step in steps:
        block = project(laplacian, interp, pairs, place, away[step], step, True, width)
        held[step] = exchange(block, "col", step) if step else block
    coarse_vectors = (keep.astype(jnp.float32) + far_vec.astype(jnp.float32)).astype(jnp.bfloat16)
    coarse = None
    for step in range(col_half):
        coarse = finish(
            held[step], held[step ^ col_half], every_interp, pairs, place, coarse, step, fine_cols
        )
    return (coarse, coarse_vectors)


def solution(mesh):
    placed = (P("row", "col"), P("row", None), P(None, "row"), P())
    return jax.shard_map(
        on_device,
        mesh=mesh,
        in_specs=placed,
        out_specs=(P(("row", "col"), None), P(None, "row")),
        check_vma=False,
    )
```

time: 256 us -> 95.3 us (0.37)
  waiting for transfers between devices: 186 us -> 14.6 us
  Pallas kernels: 0 us -> 40.6 us
  local copies, waits for them, and re-layouts: 29.3 us -> 7.25 us
  matrix products: 6.95 us -> 0 us
  other arithmetic: 8.46 us -> 2.03 us
  starting transfers between devices: 9.78 us -> 15.9 us
    ppermute x3 -> x8, waiting for transfers between devices: 134 us -> 13.9 us  [exchange(): return lax.ppermute(block, axis, [(i, i ^ flip) for i in range(count)])]
    pallas_call x0 -> x11, Pallas kernels: none -> 40.6 us  [the longest x8 34.9 us: project(): pl.pallas_call(body, out_shape=jax.ShapeDtypeStruct((count, cols), jnp.bf...]
    all_gather x1, waiting for transfers between devices: 31.7 us -> 0.01 us  [on_device(): every_interp = lax.all_gather(interp, 'row', axis=0, tiled=True)]
    all_to_all x1 -> x0, waiting for transfers between devices: 20.5 us -> none  [on_device(): lax.all_to_all(block, 'col', split_axis=0, concat_axis=1, tiled=True)]
    gather x6 -> x0, local copies, waits for them, and re-layouts: 12.6 us -> none  [the longest x1 2.87 us: on_device(): jnp.take(projected, local_rows, axis=0).astype(jnp.float32)]
    ppermute x3 -> x8, starting transfers between devices: 5.15 us -> 15.9 us  [exchange(): return lax.ppermute(block, axis, [(i, i ^ flip) for i in range(count)])]
    reshape x2 -> x1, local copies, waits for them, and re-layouts: 9.81 us -> 0.69 us  [on_device(): pairs = pairs.reshape(-1)]
    dot_general x3 -> x0, matrix products: 6.95 us -> none  [the longest x1 3.55 us: on_device(): jnp.einsum('xjy,jyb->xjb', laplacian.reshape(fine_rows * tile_size, fine_...]
  transfers between devices with their start and end apart: 5 -> 9, of which waited for: 5 -> 4; matrix products, arithmetic and copies ran while one was open for 3% -> 4% of each run, Pallas kernels for 0% -> 41%
where the time goes in v1:
time: 95.3 us; the launch traced here: 94.5 us
  Pallas kernels  40.6 us (43%)
  starting transfers between devices  15.9 us (17%)
  waiting for transfers between devices  14.6 us (15%)
  between operations  14.1 us (15%)
  local copies, waits for them, and re-layouts  7.25 us (8%)
  other arithmetic  2.03 us (2%)
    pallas_call x8, Pallas kernels, project(): pl.pallas_call(body, out_shape=jax.ShapeDtypeStruct((count, cols), jnp.bf...  34.9 us
    ppermute x8, starting transfers between devices, exchange(): return lax.ppermute(block, axis, [(i, i ^ flip) for i in range(count)])  15.9 us
    ppermute x8, waiting for transfers between devices, exchange(): return lax.ppermute(block, axis, [(i, i ^ flip) for i in range(count)])  13.9 us
    unnamed x19, local copies, waits for them, and re-layouts  6.56 us
    pallas_call x2, Pallas kernels, finish(): pl.pallas_call(body, out_shape=jax.ShapeDtypeStruct((count, total), jnp.b...  3.87 us
  transfers between devices with their start and end apart: 9, of which 4 were waited for; matrix products, arithmetic and copies ran while one was open for 4% of the time, Pallas kernels for 41%

profile of v1, /device:TPU:0, one launch (start us, length us, event | category | flops | bytes accessed | tf_op | source)
XLA Modules:
  0.0 94.5 jit_solution(3209837157842764329)
XLA Ops:
  7.2 0.7 all-gather.2.cloned.1.call-update
  7.9 0.8 copy.8
  8.7 0.7 reshape.7.pairs_ref
  9.3 0.6 pad_add_fusion.place_ref
  10.0 4.3 %project_partner.7 = bf16[128,2048]{1,0:T(8,128)(2,1)} custom-call(s32[64]{0:T(128)} %reshape.7.pairs_ref, s32[2]{0:T(128)} %pad_add_fusion.place_ref, bf16[1024,128]{1,0:T(8,128)(2,1)} %interp_ref.17, bf16[1024,2048]{1,0:T(8,128)(2,1)} %lap_ref.15), custom_call_target="tpu_custom_call" | custom-call | flops 67108864 | bytes 1572864 | tf_op jit(solution)/shard_map/project_partner/pallas_call | solution.py:60
  14.3 3.0 %collective-permute-start.5 = (bf16[128,2048]{1,0:T(8,128)(2,1)}, bf16[128,2048]{1,0:T(8,128)(2,1)S(1)}, u32[]{:S(2)}, u32[]{:S(2)}) collective-permute-start(bf16[128,2048]{1,0:T(8,128)(2,1)} %project_partner.7), channel_id=1, source_target_pairs={{0,16},{4,20},{8,24},{12,28},{16,0},{20,4},{24,8},{28,12},{1,17},{... | collective-permute-start | bytes 1572872 | tf_op jit(solution)/shard_map/ppermute | solution.py:19
  17.3 4.3 %project_partner.5 = bf16[128,2048]{1,0:T(8,128)(2,1)} custom-call(s32[64]{0:T(128)} %reshape.7.pairs_ref, s32[2]{0:T(128)} %pad_add_fusion.place_ref, bf16[1024,128]{1,0:T(8,128)(2,1)} %interp_ref.17, bf16[1024,2048]{1,0:T(8,128)(2,1)} %lap_ref.15), custom_call_target="tpu_custom_call" | custom-call | flops 67108864 | bytes 1572864 | tf_op jit(solution)/shard_map/project_partner/pallas_call | solution.py:60
  21.6 4.3 %project_partner.4 = bf16[128,2048]{1,0:T(8,128)(2,1)} custom-call(s32[64]{0:T(128)} %reshape.7.pairs_ref, s32[2]{0:T(128)} %pad_add_fusion.place_ref, bf16[1024,128]{1,0:T(8,128)(2,1)} %interp_ref.17, bf16[1024,2048]{1,0:T(8,128)(2,1)} %lap_ref.15), custom_call_target="tpu_custom_call" | custom-call | flops 67108864 | bytes 1572864 | tf_op jit(solution)/shard_map/project_partner/pallas_call | solution.py:60
  25.8 2.0 %collective-permute-start = (bf16[128,2048]{1,0:T(8,128)(2,1)}, bf16[128,2048]{1,0:T(8,128)(2,1)S(1)}, u32[]{:S(2)}, u32[]{:S(2)}) collective-permute-start(bf16[128,2048]{1,0:T(8,128)(2,1)} %project_partner.4), channel_id=1, source_target_pairs={{0,16},{4,20},{8,24},{12,28},{16,0},{20,4},{24,8},{28,12},{1,17},{... | collective-permute-start | bytes 1572872 | tf_op jit(solution)/shard_map/ppermute | solution.py:19
  27.8 4.3 %project_partner.6 = bf16[128,2048]{1,0:T(8,128)(2,1)} custom-call(s32[64]{0:T(128)} %reshape.7.pairs_ref, s32[2]{0:T(128)} %pad_add_fusion.place_ref, bf16[1024,128]{1,0:T(8,128)(2,1)} %interp_ref.17, bf16[1024,2048]{1,0:T(8,128)(2,1)} %lap_ref.15), custom_call_target="tpu_custom_call" | custom-call | flops 67108864 | bytes 1572864 | tf_op jit(solution)/shard_map/project_partner/pallas_call | solution.py:60
  32.2 0.9 collective-permute-done.5.refs_0_
  33.1 0.8 copy-done.8
  33.8 4.5 %project_mine.7 = bf16[128,2048]{1,0:T(8,128)(2,1)} custom-call(s32[64]{0:T(128)} %reshape.7.pairs_ref, s32[2]{0:T(128)} %pad_add_fusion.place_ref, bf16[1024,128]{1,0:T(8,128)(2,1)} %interp_ref.17, bf16[1024,2048]{1,0:T(8,128)(2,1)} %lap_ref.15, bf16[128,2048]{1,0:T(8,128)(2,1)} %copy-done.8), custom_call_target="tpu_custom_call" | custom-call | flops 67108864 | bytes 1572864 | tf_op jit(solution)/shard_map/project_mine/pallas_call | solution.py:60
  38.3 3.1 %collective-permute-start.6 = (bf16[128,2048]{1,0:T(8,128)(2,1)}, bf16[128,2048]{1,0:T(8,128)(2,1)S(1)}, u32[]{:S(2)}, u32[]{:S(2)}) collective-permute-start(bf16[128,2048]{1,0:T(8,128)(2,1)} %project_mine.7), channel_id=1, source_target_pairs={{0,2},{1,3},{2,0},{3,1},{4,6},{5,7},{6,4},{7,5},{8,10},{9,11},{10,... | collective-permute-start | bytes 1572872 | tf_op jit(solution)/shard_map/ppermute | solution.py:19
  41.4 8.5 %collective-permute-done.2.refs_0_ = bf16[128,2048]{1,0:T(8,128)(2,1)S(1)} collective-permute-done((bf16[128,2048]{1,0:T(8,128)(2,1)}, bf16[128,2048]{1,0:T(8,128)(2,1)S(1)}, u32[]{:S(2)}, u32[]{:S(2)}) %collective-permute-start.2) | collective-permute-done | bytes 524320 | tf_op jit(solution)/shard_map/ppermute | solution.py:19
  49.9 0.8 copy-done.7
  50.7 4.4 %project_mine.5 = bf16[128,2048]{1,0:T(8,128)(2,1)} custom-call(s32[64]{0:T(128)} %reshape.7.pairs_ref, s32[2]{0:T(128)} %pad_add_fusion.place_ref, bf16[1024,128]{1,0:T(8,128)(2,1)} %interp_ref.17, bf16[1024,2048]{1,0:T(8,128)(2,1)} %lap_ref.15, bf16[128,2048]{1,0:T(8,128)(2,1)} %copy-done.7), custom_call_target="tpu_custom_call" | custom-call | flops 67108864 | bytes 1572864 | tf_op jit(solution)/shard_map/project_mine/pallas_call | solution.py:60
  55.1 4.1 %collective-permute-start.3 = (bf16[128,2048]{1,0:T(8,128)(2,1)}, bf16[128,2048]{1,0:T(8,128)(2,1)S(1)}, u32[]{:S(2)}, u32[]{:S(2)}) collective-permute-start(bf16[128,2048]{1,0:T(8,128)(2,1)} %project_mine.5), channel_id=1, source_target_pairs={{0,3},{1,2},{2,1},{3,0},{4,7},{5,6},{6,5},{7,4},{8,11},{9,10},{10,... | collective-permute-start | bytes 1572872 | tf_op jit(solution)/shard_map/ppermute | solution.py:19
  59.2 1.9 %collective-permute-done.refs_0_ = bf16[128,2048]{1,0:T(8,128)(2,1)S(1)} collective-permute-done((bf16[128,2048]{1,0:T(8,128)(2,1)}, bf16[128,2048]{1,0:T(8,128)(2,1)S(1)}, u32[]{:S(2)}, u32[]{:S(2)}) %collective-permute-start) | collective-permute-done | bytes 524320 | tf_op jit(solution)/shard_map/ppermute | solution.py:19
  61.1 0.8 copy-done.6
  61.9 4.4 %project_mine.4 = bf16[128,2048]{1,0:T(8,128)(2,1)} custom-call(s32[64]{0:T(128)} %reshape.7.pairs_ref, s32[2]{0:T(128)} %pad_add_fusion.place_ref, bf16[1024,128]{1,0:T(8,128)(2,1)} %interp_ref.17, bf16[1024,2048]{1,0:T(8,128)(2,1)} %lap_ref.15, bf16[128,2048]{1,0:T(8,128)(2,1)} %copy-done.6), custom_call_target="tpu_custom_call" | custom-call | flops 67108864 | bytes 1572864 | tf_op jit(solution)/shard_map/project_mine/pallas_call | solution.py:60
  66.4 2.1 %collective-permute-start.1 = (bf16[128,2048]{1,0:T(8,128)(2,1)}, bf16[128,2048]{1,0:T(8,128)(2,1)S(1)}, u32[]{:S(2)}, u32[]{:S(2)}) collective-permute-start(bf16[128,2048]{1,0:T(8,128)(2,1)} %project_mine.4), channel_id=1, source_target_pairs={{0,1},{1,0},{2,3},{3,2},{4,5},{5,4},{6,7},{7,6},{8,9},{9,8},{10,11... | collective-permute-start | bytes 1572872 | tf_op jit(solution)/shard_map/ppermute | solution.py:19
  68.5 1.8 %restrict.1 = (bf16[32,512]{1,0:T(8,128)(2,1)}, bf16[32,512]{1,0:T(8,128)(2,1)}) custom-call(s32[64]{0:T(128)} %reshape.7.pairs_ref, s32[2]{0:T(128)} %pad_add_fusion.place_ref, bf16[32,1024]{1,0:T(8,128)(2,1)} %vec_ref.1, bf16[1024,128]{1,0:T(8,128)(2,1)} %interp_ref.17), custom_call_target="tpu_custom_call" | custom-call | tf_op jit(solution)/shard_map/restrict/pallas_call | solution.py:155
  70.3 1.5 %collective-permute-start.7 = (bf16[32,512]{1,0:T(8,128)(2,1)}, bf16[32,512]{1,0:T(8,128)(2,1)S(1)}, u32[]{:S(2)}, u32[]{:S(2)}) collective-permute-start(bf16[32,512]{1,0:T(8,128)(2,1)} %get-tuple-element.5), channel_id=1, source_target_pairs={{0,16},{4,20},{8,24},{12,28},{16,0},{20,4},{24,8},{28,12},{1,17},{... | collective-permute-start | bytes 98312 | tf_op jit(solution)/shard_map/ppermute | solution.py:19
  71.8 2.6 %collective-permute-done.7 = bf16[32,512]{1,0:T(8,128)(2,1)S(1)} collective-permute-done((bf16[32,512]{1,0:T(8,128)(2,1)}, bf16[32,512]{1,0:T(8,128)(2,1)S(1)}, u32[]{:S(2)}, u32[]{:S(2)}) %collective-permute-start.7) | collective-permute-done | bytes 32800 | tf_op jit(solution)/shard_map/ppermute | solution.py:19
  74.4 1.4 %add_convert_fusion = bf16[32,512]{1,0:T(8,128)(2,1)} fusion(bf16[32,512]{1,0:T(8,128)(2,1)S(1)} %collective-permute-done.7, bf16[32,512]{1,0:T(8,128)(2,1)} %get-tuple-element.4), kind=kLoop, calls=%fused_computation | loop fusion | flops 65536 | bytes 98304 | tf_op jit(solution)/shard_map/convert_element_type | solution.py:191
  75.8 0.8 copy-done.5
  76.6 4.5 %project_mine.6.near_ref = bf16[128,2048]{1,0:T(8,128)(2,1)} custom-call(s32[64]{0:T(128)} %reshape.7.pairs_ref, s32[2]{0:T(128)} %pad_add_fusion.place_ref, bf16[1024,128]{1,0:T(8,128)(2,1)} %interp_ref.17, bf16[1024,2048]{1,0:T(8,128)(2,1)} %lap_ref.15, bf16[128,2048]{1,0:T(8,128)(2,1)} %copy-done.5), custom_call_target="tpu_custom_call" | custom-call | flops 67108864 | bytes 1572864 | tf_op jit(solution)/shard_map/project_mine/pallas_call | solution.py:60
  81.1 1.6 %copy-done = bf16[8192,128]{1,0:T(8,128)(2,1)S(1)} copy-done((bf16[8192,128]{1,0:T(8,128)(2,1)S(1)}, bf16[8192,128]{1,0:T(8,128)(2,1)}, u32[]{:S(2)}) %copy-start) | copy-done | bytes 2097176
  82.7 1.0 %copy-done.2 = bf16[128,2048]{1,0:T(8,128)(2,1)S(1)} copy-done((bf16[128,2048]{1,0:T(8,128)(2,1)S(1)}, bf16[128,2048]{1,0:T(8,128)(2,1)}, u32[]{:S(2)}) %copy-start.2) | copy-done | bytes 524312
  83.8 1.9 %finish.2.refs_0_ = bf16[128,4096]{1,0:T(8,128)(2,1)} custom-call(s32[64]{0:T(128)S(1)} %copy-done.3, s32[2]{0:T(128)S(1)} %copy-done.4, bf16[128,2048]{1,0:T(8,128)(2,1)S(1)} %copy-done.2, bf16[128,2048]{1,0:T(8,128)(2,1)S(1)} %collective-permute-done.6.far_ref, bf16[8192,128]{1,0:T(8,128)(2,1)S(1)} %copy-done), custom_call_target="tpu_custom_call" | custom-call | flops 134217728 | bytes 2097152 | tf_op jit(solution)/shard_map/finish/pallas_call | solution.py:115
  85.7 1.9 %finish.3 = bf16[128,4096]{1,0:T(8,128)(2,1)} custom-call(s32[64]{0:T(128)S(1)} %copy-done.3, s32[2]{0:T(128)S(1)} %copy-done.4, bf16[128,2048]{1,0:T(8,128)(2,1)S(1)} %collective-permute-done.1.near_ref, bf16[128,2048]{1,0:T(8,128)(2,1)S(1)} %collective-permute-done.3.far_ref, bf16[8192,128]{1,0:T(8,128)(2,1)S(1)} %copy-done.1, ...), custom_call_target="tpu_custom_call", output_to_operand_aliasing={{}: (5, {})} | custom-call | flops 134217728 | bytes 2097152 | tf_op jit(solution)/shard_map/finish/pallas_call | solution.py:115
  (20 shorter events, 0.1 us)
Async XLA Ops:
  7.2 73.9 %all-gather.2.cloned.1.call-start = ((), (), s32[]{:S(2)}) async-start(), calls=%async_computation | async-start | bytes 2359296 | tf_op jit(solution)/shard_map/all_gather | solution.py:184
  14.3 18.7 %collective-permute-start.5 = (bf16[128,2048]{1,0:T(8,128)(2,1)}, bf16[128,2048]{1,0:T(8,128)(2,1)S(1)}, u32[]{:S(2)}, u32[]{:S(2)}) collective-permute-start(bf16[128,2048]{1,0:T(8,128)(2,1)} %project_partner.7), channel_id=1, source_target_pairs={{0,16},{4,20},{8,24},{12,28},{16,0},{20,4},{24,8},{28,12},{1,17},{... | collective-permute-start | bytes 1572872 | tf_op jit(solution)/shard_map/ppermute | solution.py:19
  21.5 28.4 %collective-permute-start.2 = (bf16[128,2048]{1,0:T(8,128)(2,1)}, bf16[128,2048]{1,0:T(8,128)(2,1)S(1)}, u32[]{:S(2)}, u32[]{:S(2)}) collective-permute-start(bf16[128,2048]{1,0:T(8,128)(2,1)} %project_partner.5), channel_id=1, source_target_pairs={{0,16},{4,20},{8,24},{12,28},{16,0},{20,4},{24,8},{28,12},{1,17},{... | collective-permute-start | bytes 1572872 | tf_op jit(solution)/shard_map/ppermute | solution.py:19
  25.8 35.3 %collective-permute-start = (bf16[128,2048]{1,0:T(8,128)(2,1)}, bf16[128,2048]{1,0:T(8,128)(2,1)S(1)}, u32[]{:S(2)}, u32[]{:S(2)}) collective-permute-start(bf16[128,2048]{1,0:T(8,128)(2,1)} %project_partner.4), channel_id=1, source_target_pairs={{0,16},{4,20},{8,24},{12,28},{16,0},{20,4},{24,8},{28,12},{1,17},{... | collective-permute-start | bytes 1572872 | tf_op jit(solution)/shard_map/ppermute | solution.py:19
  32.2 43.7 %collective-permute-start.4 = (bf16[128,2048]{1,0:T(8,128)(2,1)}, bf16[128,2048]{1,0:T(8,128)(2,1)S(1)}, u32[]{:S(2)}, u32[]{:S(2)}) collective-permute-start(bf16[128,2048]{1,0:T(8,128)(2,1)} %project_partner.6), channel_id=1, source_target_pairs={{0,16},{4,20},{8,24},{12,28},{16,0},{20,4},{24,8},{28,12},{1,17},{... | collective-permute-start | bytes 1572872 | tf_op jit(solution)/shard_map/ppermute | solution.py:19
  33.1 0.8 copy-start.8
  38.3 42.8 %collective-permute-start.6 = (bf16[128,2048]{1,0:T(8,128)(2,1)}, bf16[128,2048]{1,0:T(8,128)(2,1)S(1)}, u32[]{:S(2)}, u32[]{:S(2)}) collective-permute-start(bf16[128,2048]{1,0:T(8,128)(2,1)} %project_mine.7), channel_id=1, source_target_pairs={{0,2},{1,3},{2,0},{3,1},{4,6},{5,7},{6,4},{7,5},{8,10},{9,11},{10,... | collective-permute-start | bytes 1572872 | tf_op jit(solution)/shard_map/ppermute | solution.py:19
  49.9 0.8 copy-start.7
  55.1 30.6 %collective-permute-start.3 = (bf16[128,2048]{1,0:T(8,128)(2,1)}, bf16[128,2048]{1,0:T(8,128)(2,1)S(1)}, u32[]{:S(2)}, u32[]{:S(2)}) collective-permute-start(bf16[128,2048]{1,0:T(8,128)(2,1)} %project_mine.5), channel_id=1, source_target_pairs={{0,3},{1,2},{2,1},{3,0},{4,7},{5,6},{6,5},{7,4},{8,11},{9,10},{10,... | collective-permute-start | bytes 1572872 | tf_op jit(solution)/shard_map/ppermute | solution.py:19
  61.1 0.8 copy-start.6
  66.4 14.7 %copy-start.3 = (s32[64]{0:T(128)S(1)}, s32[64]{0:T(128)}, u32[]{:S(2)}) copy-start(s32[64]{0:T(128)} %reshape.7.pairs_ref) | copy-start | bytes 772
  66.4 14.7 %copy-start.4 = (s32[2]{0:T(128)S(1)}, s32[2]{0:T(128)}, u32[]{:S(2)}) copy-start(s32[2]{0:T(128)} %pad_add_fusion.place_ref) | copy-start | bytes 28
  66.4 19.3 %collective-permute-start.1 = (bf16[128,2048]{1,0:T(8,128)(2,1)}, bf16[128,2048]{1,0:T(8,128)(2,1)S(1)}, u32[]{:S(2)}, u32[]{:S(2)}) collective-permute-start(bf16[128,2048]{1,0:T(8,128)(2,1)} %project_mine.4), channel_id=1, source_target_pairs={{0,1},{1,0},{2,3},{3,2},{4,5},{5,4},{6,7},{7,6},{8,9},{9,8},{10,11... | collective-permute-start | bytes 1572872 | tf_op jit(solution)/shard_map/ppermute | solution.py:19
  70.3 4.1 %collective-permute-start.7 = (bf16[32,512]{1,0:T(8,128)(2,1)}, bf16[32,512]{1,0:T(8,128)(2,1)S(1)}, u32[]{:S(2)}, u32[]{:S(2)}) collective-permute-start(bf16[32,512]{1,0:T(8,128)(2,1)} %get-tuple-element.5), channel_id=1, source_target_pairs={{0,16},{4,20},{8,24},{12,28},{16,0},{20,4},{24,8},{28,12},{1,17},{... | collective-permute-start | bytes 98312 | tf_op jit(solution)/shard_map/ppermute | solution.py:19
  75.8 0.8 copy-start.5
  81.1 1.6 %copy-start = (bf16[8192,128]{1,0:T(8,128)(2,1)S(1)}, bf16[8192,128]{1,0:T(8,128)(2,1)}, u32[]{:S(2)}) copy-start(bf16[8192,128]{1,0:T(8,128)(2,1)} %all-gather.2.cloned.1.call-done.interp_ref) | copy-start | bytes 6291460
  82.7 1.0 %copy-start.2 = (bf16[128,2048]{1,0:T(8,128)(2,1)S(1)}, bf16[128,2048]{1,0:T(8,128)(2,1)}, u32[]{:S(2)}) copy-start(bf16[128,2048]{1,0:T(8,128)(2,1)} %project_mine.6.near_ref) | copy-start | bytes 1572868
  83.7 1.9 %copy-start.1 = (bf16[8192,128]{1,0:T(8,128)(2,1)S(1)}, bf16[8192,128]{1,0:T(8,128)(2,1)}, u32[]{:S(2)}) copy-start(bf16[8192,128]{1,0:T(8,128)(2,1)} %all-gather.2.cloned.1.call-done.interp_ref) | copy-start | bytes 6291460
Sparse Core Ops, SparseCore 0:
  9.9 39.2 all-gather.1

commit v2 on v1

v2 whole, which is shorter than its diff:
```python
import jax
import jax.numpy as jnp
from jax import lax
from jax.experimental import pallas as pl
from jax.experimental.pallas import tpu as pltpu
from jax.sharding import PartitionSpec as P


AHEAD = 2
HEAD = 1
GATHER = 1
VECTORS = 2
VECTORS_AT = '0a'
ZAFTER = {}
FINISH = 1000000000
JOBS = 2
WAITS = {'1a': ['z2a'], '0a': ['z3a', 'g2']}


def CHUNKS(half, count):
    chunks = [(half, 0, 8), (half, 8, 16)]
    for far, near in zip(range(half + 1, count), range(1, half)):
        chunks += [(far, 0, 16), (near, 0, 16)]
    return chunks + [(0, 0, 16)]


def estimate(flops=1000):
    return pl.CostEstimate(flops=flops, bytes_accessed=flops // 1000, transcendentals=0)


def in_hbm(value):
    return pltpu.with_memory_space_constraint(value, pltpu.HBM)


def contract_rows(left, right):
    return lax.dot_general(
        left, right, (((0,), (0,)), ((), ())), preferred_element_type=jnp.float32
    )


def exchange(block, axis, flip, name="p"):
    count = lax.axis_size(axis)
    with jax.named_scope(name):
        return lax.ppermute(block, axis, [(i, i ^ flip) for i in range(count)])
    return lax.ppermute(block, axis, [(i, i ^ flip) for i in range(count)])


def after(value, *earlier):
    return lax.optimization_barrier((value, *earlier))[0]


def project(laplacian, interp, pairs, jobs, *earlier, flops=1000):
    tile = interp.shape[1]
    fine_rows = interp.shape[0] // tile
    coarse_rows = fine_rows // 2
    cols = laplacian.shape[1]
    half = lax.axis_size("row") // 2
    count = coarse_rows * tile // lax.axis_size("col")
    outs = [
        jax.ShapeDtypeStruct((count, end - begin), dtype)
        for _, _, dtype, spans in jobs
        for begin, end in spans
    ]

    def body(pairs_ref, interp_ref, lap_ref, *refs):
        out_refs = list(refs[len(earlier) : len(earlier) + len(outs)])
        lap_buf, interp_buf, whole_ref, sems = refs[len(earlier) + len(outs) :]
        row, col = lax.axis_index("row"), lax.axis_index("col")
        copies = []
        for slot, (step, mine, _, _) in enumerate(jobs):
            owner = row if mine else row ^ half
            coarse_row = owner * coarse_rows + (col ^ step) * count // tile
            local = pairs_ref[row // half, coarse_row] - row * fine_rows
            at = pl.ds(pl.multiple_of(local * tile, tile), tile)
            for which, (ref, buf) in enumerate(((interp_ref, interp_buf), (lap_ref, lap_buf))):
                copy = pltpu.make_async_copy(ref.at[at, :], buf.at[slot], sems.at[which, slot])
                copy.start()
                copies.append(copy)
        for slot, (step, mine, _, spans) in enumerate(jobs):
            copies[2 * slot].wait()
            copies[2 * slot + 1].wait()
            left = interp_buf[slot]
            for begin, end in spans:
                out_ref = out_refs.pop(0)
                result = contract_rows(left, lap_buf[slot, :, begin:end])
                if count != tile:
                    whole_ref[:, : end - begin] = result
                    first = pl.multiple_of(((col ^ step) * count) % tile, count)
                    result = whole_ref[pl.ds(first, count), : end - begin]
                out_ref[...] = result.astype(out_ref.dtype)

    spare = (8, 128) if count == tile else (tile, cols)
    size = sum(out.size * out.dtype.itemsize for out in outs)
    size += len(jobs) * tile * (cols + tile) * 2 + spare[0] * spare[1] * 4
    return pl.pallas_call(
        body,
        out_shape=outs,
        in_specs=[pl.BlockSpec(memory_space=pltpu.SMEM)]
        + [pl.BlockSpec(memory_space=pl.ANY)] * (2 + len(earlier)),
        out_specs=[pl.BlockSpec(memory_space=pltpu.VMEM)] * len(outs),
        scratch_shapes=[
            pltpu.VMEM((len(jobs), tile, cols), jnp.bfloat16),
            pltpu.VMEM((len(jobs), tile, tile), jnp.bfloat16),
            pltpu.VMEM(spare, jnp.float32),
            pltpu.SemaphoreType.DMA((2, len(jobs))),
        ],
        compiler_params=pltpu.CompilerParams(vmem_limit_bytes=size + 4 * 1024 * 1024),
        cost_estimate=estimate(flops),
        name="project",
    )(in_hbm(pairs), in_hbm(interp), in_hbm(laplacian), *earlier)


def combine(own, begin, received, *earlier):
    end = begin + received.shape[1]

    def body(own_ref, received_ref, *refs):
        total = own_ref[:, begin:end].astype(jnp.float32) + received_ref[...].astype(jnp.float32)
        refs[-1][...] = total.astype(refs[-1].dtype)

    return pl.pallas_call(
        body,
        out_shape=jax.ShapeDtypeStruct(received.shape, jnp.bfloat16),
        in_specs=[pl.BlockSpec(memory_space=pltpu.VMEM)] * 2
        + [pl.BlockSpec(memory_space=pl.ANY)] * len(earlier),
        out_specs=pl.BlockSpec(memory_space=pltpu.VMEM),
        compiler_params=pltpu.CompilerParams(vmem_limit_bytes=8 * 1024 * 1024),
        cost_estimate=estimate(),
        name="combine",
    )(own, received, *earlier)


def gather_blocks(block, axis):
    blocks, flip = [block], lax.axis_size(axis) // 2
    while flip:
        blocks += [exchange(part, axis, flip, f"gather{flip}") for part in blocks]
        flip //= 2
    return blocks


def finish(jobs, interp_blocks, pairs, before, fine_cols, *earlier):
    tile = interp_blocks[0].shape[1]
    fine_rows = interp_blocks[0].shape[0] // tile
    count = jobs[0][0][0].shape[0]
    row_count = lax.axis_size("row")
    half = lax.axis_size("col") // 2
    coarse_cols = fine_cols // 2
    width = coarse_cols * tile
    total = row_count * fine_rows * tile // 2
    pieces = [
        (2 * n + which, part)
        for n, (near, far, _) in enumerate(jobs)
        for which, parts in enumerate((near, far))
        for part in parts
    ]
    sources = [*interp_blocks, *(part for _, part in pieces)]

    def body(pairs_ref, *refs):
        out_ref, wide, interp_buf, buf, sem, fetch = refs[-6:]
        row, col = lax.axis_index("row"), lax.axis_index("col")
        upper = col // half
        begins, fetches = [0] * (2 * len(jobs)), []
        for k, ref in enumerate(refs[: len(sources)]):
            if k < len(interp_blocks):
                target = interp_buf.at[k]
            else:
                which = pieces[k - len(interp_blocks)][0]
                begin = begins[which]
                begins[which] = begin + ref.shape[1]
                target = wide.at[which, :, begin : begins[which]]
            fetches.append(pltpu.make_async_copy(ref, target, fetch.at[k]))
        for copy in fetches:
            copy.start()
        for copy in fetches:
            copy.wait()
        copies = []
        for n, (_, _, step) in enumerate(jobs):
            for part in range(2):
                group = part * half + (col ^ step) % half
                for k in range(coarse_cols):
                    d = group * coarse_cols + k
                    result = None
                    for which, j, owner in (
                        (0, pairs_ref[upper, d], col ^ step),
                        (1, pairs_ref[1 - upper, d], col ^ step ^ half),
                    ):
                        start = pl.multiple_of((j - owner * fine_cols) * tile, tile)
                        source = (j // fine_rows) ^ row
                        place, bit = 0, row_count // 2
                        while bit:
                            place = place * 2 + source % 2
                            source, bit = source // 2, bit // 2
                        at = pl.multiple_of((j % fine_rows) * tile, tile)
                        product = jnp.dot(
                            wide[2 * n + which, :, pl.ds(start, tile)],
                            interp_buf[place, pl.ds(at, tile), :],
                            preferred_element_type=jnp.float32,
                        )
                        result = product if result is None else result + product
                    buf[2 * n + part, :, k * tile : (k + 1) * tile] = result.astype(buf.dtype)
                copy = pltpu.make_async_copy(
                    buf.at[2 * n + part],
                    out_ref.at[:, pl.ds(pl.multiple_of(group * width, width), width)],
                    sem.at[2 * n + part],
                )
                copy.start()
                copies.append(copy)
        for copy in copies:
            copy.wait()

    operands = [pairs, *sources]
    aliases = {}
    if before is not None:
        aliases = {len(operands): 0}
        operands.append(before)
    operands += earlier
    blocks = len(interp_blocks)
    size = blocks * fine_rows * tile * tile * 2 + 2 * len(jobs) * count * (fine_cols * tile + width) * 2
    return pl.pallas_call(
        body,
        out_shape=jax.ShapeDtypeStruct((count, total), jnp.bfloat16),
        in_specs=[pl.BlockSpec(memory_space=pltpu.SMEM)]
        + [pl.BlockSpec(memory_space=pl.ANY)] * (len(operands) - 1),
        out_specs=pl.BlockSpec(memory_space=pl.ANY),
        scratch_shapes=[
            pltpu.VMEM((2 * len(jobs), count, fine_cols * tile), jnp.bfloat16),
            pltpu.VMEM((blocks, fine_rows * tile, tile), jnp.bfloat16),
            pltpu.VMEM((2 * len(jobs), count, width), jnp.bfloat16),
            pltpu.SemaphoreType.DMA((2 * len(jobs),)),
            pltpu.SemaphoreType.DMA((len(sources),)),
        ],
        input_output_aliases=aliases,
        cost_estimate=estimate(FINISH),
        compiler_params=pltpu.CompilerParams(vmem_limit_bytes=size + 4 * 1024 * 1024),
        name="finish",
    )(*operands)


def restrict(vectors, interp, pairs, *earlier):
    tile = interp.shape[1]
    fine_rows = interp.shape[0] // tile
    coarse_rows = fine_rows // 2
    half = lax.axis_size("row") // 2

    def body(pairs_ref, vec_ref, interp_ref, *refs):
        keep_ref, send_ref = refs[-2:]
        row = lax.axis_index("row")
        for out_ref, flip in ((keep_ref, 0), (send_ref, half)):
            for k in range(coarse_rows):
                i = pairs_ref[row // half, (row ^ flip) * coarse_rows + k] - row * fine_rows
                at = pl.ds(pl.multiple_of(i * tile, tile), tile)
                out_ref[:, k * tile : (k + 1) * tile] = jnp.dot(
                    vec_ref[:, at], interp_ref[at, :], preferred_element_type=jnp.float32
                ).astype(out_ref.dtype)

    shape = jax.ShapeDtypeStruct((vectors.shape[0], coarse_rows * tile), jnp.bfloat16)
    return pl.pallas_call(
        body,
        out_shape=(shape, shape),
        in_specs=[
            pl.BlockSpec(memory_space=pltpu.SMEM),
            pl.BlockSpec(memory_space=pltpu.VMEM),
            pl.BlockSpec(memory_space=pltpu.VMEM),
        ]
        + [pl.BlockSpec(memory_space=pl.ANY)] * len(earlier),
        out_specs=(pl.BlockSpec(memory_space=pltpu.VMEM),) * 2,
        compiler_params=pltpu.CompilerParams(vmem_limit_bytes=4 * 1024 * 1024),
        cost_estimate=estimate(),
        name="restrict",
    )(pairs, vectors, interp, *earlier)


def on_device(laplacian, interp, vectors, pairs):
    tile = interp.shape[1]
    cols = laplacian.shape[1]
    fine_rows, fine_cols = interp.shape[0] // tile, cols // tile
    row_half = lax.axis_size("row") // 2
    col_count = lax.axis_size("col")
    col_half = col_count // 2
    pairs = pairs.T

    whole = [(0, cols)]
    order = CHUNKS(col_half, col_count)
    steps = list(dict.fromkeys(step for step, _, _ in order))
    spans = {
        step: [(lo * cols // 16, hi * cols // 16) for other, lo, hi in order if other == step]
        for step in steps
    }
    labels = [f"{step}{'abcdefgh'[spans[step].index((lo * cols // 16, hi * cols // 16))]}" for step, lo, hi in order]
    head = HEAD
    cut = sum(len(spans[step]) for step in steps[:head])
    sent = project(
        laplacian, interp, pairs, [(s, False, jnp.bfloat16, spans[s]) for s in steps[:head]]
    )
    sent += project(
        laplacian, interp, pairs, [(s, False, jnp.bfloat16, spans[s]) for s in steps[head:]], sent[0]
    )
    grouped = [(step, span) for step in steps for span in spans[step]]
    sent = dict(zip(grouped, sent))
    kept = project(
        laplacian, interp, pairs, [(s, True, jnp.float32, whole) for s in steps], sent[grouped[cut]]
    )
    kept = dict(zip(steps, kept))
    named, totals, held = {}, [kept[0]], {step: [] for step in steps}
    for k, (step, lo, hi) in enumerate(order):
        name, span = labels[k], (lo * cols // 16, hi * cols // 16)
        block = sent[step, span]
        if k >= AHEAD:
            block = after(block, totals[k + 1 - AHEAD])
        block = exchange(block, "row", row_half, "y" + name)
        waits = totals[-1:] + [named[w] for w in WAITS.get(name, ()) if w in named]
        if name == VECTORS_AT:
            coarse_vectors = combine(keep, 0, far_vec, totals[-1])
            waits.append(coarse_vectors)
        total = combine(kept[step], span[0], block, *waits)
        totals.append(total)
        if step:
            later = [named[w] for w in ZAFTER.get(name, ()) if w in named]
            total = exchange(after(total, *later) if later else total, "col", step, "z" + name)
        named["z" + name] = total
        held[step].append(total)
        if k == GATHER:
            interp_blocks = gather_blocks(after(interp, totals[-1]), "row")
            for place, value in enumerate(interp_blocks):
                named[f"g{place}"] = value
        if k == VECTORS:
            keep, send = restrict(vectors, interp, pairs, totals[-1])
            named["v"] = far_vec = exchange(send, "row", row_half, "vectors")
    if not VECTORS_AT:
        coarse_vectors = combine(keep, 0, far_vec, totals[-1])
    coarse = None
    jobs = [(held[step], held[step ^ col_half], step) for step in range(col_half)]
    for k in range(0, len(jobs), JOBS):
        coarse = finish(jobs[k : k + JOBS], interp_blocks, pairs, coarse, fine_cols)
    return (coarse, coarse_vectors)


def solution(mesh):
    placed = (P("row", "col"), P("row", None), P(None, "row"), P())
    return jax.shard_map(
        on_device,
        mesh=mesh,
        in_specs=placed,
        out_specs=(P(("row", "col"), None), P(None, "row")),
        check_vma=False,
    )
```

time: 95.3 us -> 72.7 us (0.76)
  Pallas kernels: 40.6 us -> 13.4 us
  waiting for transfers between devices: 14.6 us -> 30.7 us
  between operations: 14.1 us -> 0.73 us
  starting transfers between devices: 15.9 us -> 26.4 us
  local copies, waits for them, and re-layouts: 7.25 us -> 0.78 us
  other arithmetic: 2.03 us -> 0 us
    pallas_call x8 -> x9, Pallas kernels: 34.9 us -> 9.23 us  [the longest x3 8.18 us: project(): pl.pallas_call(body, out_shape=outs, in_specs=[pl.BlockSpec(memory_space=...]
    ppermute x8 -> x17, waiting for transfers between devices: 13.9 us -> 30.7 us  [exchange(): return lax.ppermute(block, axis, [(i, i ^ flip) for i in range(count)])]
    ppermute x8 -> x17, starting transfers between devices: 15.9 us -> 26.4 us  [exchange(): return lax.ppermute(block, axis, [(i, i ^ flip) for i in range(count)])]
    unnamed x19 -> x8, local copies, waits for them, and re-layouts: 6.56 us -> 0.78 us
    convert_element_type x1 -> x0, other arithmetic: 1.38 us -> none  [on_device(): (keep.astype(jnp.float32) + far_vec.astype(jnp.float32)).astype(jnp.bfloa...]
    pallas_call x1, Pallas kernels: 1.82 us -> 0.75 us  [restrict(): pl.pallas_call(body, out_shape=(shape, shape), in_specs=[pl.BlockSpec(mem...]
    pallas_call x2 -> x1, Pallas kernels: 3.87 us -> 3.38 us  [finish(): pl.pallas_call(body, out_shape=jax.ShapeDtypeStruct((count, total), jnp.b...]
  transfers between devices with their start and end apart: 9 -> 17, of which waited for: 4 -> 7; matrix products, arithmetic and copies ran while one was open for 4% -> 0% of each run, Pallas kernels for 41% -> 11%
where the time goes in v2:
time: 72.7 us; the launch traced here: 71.9 us
  waiting for transfers between devices  30.7 us (42%)
  starting transfers between devices  26.4 us (36%)
  Pallas kernels  13.4 us (18%)
  local copies, waits for them, and re-layouts  0.78 us (1%)
  between operations  0.73 us (1%)
    ppermute x17, waiting for transfers between devices, exchange(): return lax.ppermute(block, axis, [(i, i ^ flip) for i in range(count)])  30.7 us
    ppermute x17, starting transfers between devices, exchange(): return lax.ppermute(block, axis, [(i, i ^ flip) for i in range(count)])  26.4 us
    pallas_call x3, Pallas kernels, project(): pl.pallas_call(body, out_shape=outs, in_specs=[pl.BlockSpec(memory_space=...  8.18 us
    pallas_call x1, Pallas kernels, finish(): pl.pallas_call(body, out_shape=jax.ShapeDtypeStruct((count, total), jnp.b...  3.38 us
  transfers between devices with their start and end apart: 17, of which 7 were waited for; matrix products, arithmetic and copies ran while one was open for 0% of the time, Pallas kernels for 11%

profile of v2, /device:TPU:0, one launch (start us, length us, event | category | flops | bytes accessed | tf_op | source)
XLA Modules:
  0.0 71.9 jit_solution(15559543111445707331)
XLA Ops:
  0.6 2.1 %project.3 = (bf16[128,1024]{1,0:T(8,128)(2,1)S(1)}, bf16[128,1024]{1,0:T(8,128)(2,1)S(1)}) custom-call(s32[2,32]{1,0:T(2,128)} %bitcast.1, bf16[1024,128]{1,0:T(8,128)(2,1)} %refs_0_, bf16[1024,2048]{1,0:T(8,128)(2,1)} %lap_ref.5), custom_call_target="tpu_custom_call" | custom-call | flops 1000 | bytes 1 | tf_op jit(solution)/shard_map/project/pallas_call | solution.py:95
  2.8 3.0 %collective-permute-start.1 = (bf16[128,1024]{1,0:T(8,128)(2,1)S(1)}, bf16[128,1024]{1,0:T(8,128)(2,1)S(1)}, u32[]{:S(2)}, u32[]{:S(2)}) collective-permute-start(bf16[128,1024]{1,0:T(8,128)(2,1)S(1)} %get-tuple-element.17.refs_0_), channel_id=1, source_target_pairs={{0,16},{4,20},{8,24},{12,28},{16,0},{20,4},{24,8},{28,12},{1,17},{... | collective-permute-start | bytes 786440 | tf_op jit(solution)/shard_map/y2a/ppermute | solution.py:44
  5.8 0.1 collective-permute-start
  5.9 2.8 %project.4 = (bf16[128,2048]{1,0:T(8,128)(2,1)S(1)}, bf16[128,2048]{1,0:T(8,128)(2,1)S(1)}, bf16[128,2048]{1,0:T(8,128)(2,1)S(1)}) custom-call(s32[2,32]{1,0:T(2,128)} %bitcast.2, bf16[1024,128]{1,0:T(8,128)(2,1)} %refs_0_, bf16[1024,2048]{1,0:T(8,128)(2,1)} %lap_ref.5, bf16[128,1024]{1,0:T(8,128)(2,1)S(1)} %get-tuple-element.17.refs_0_), custom_call_target="tpu_custom_call" | custom-call | flops 1000 | bytes 1 | tf_op jit(solution)/shard_map/project/pallas_call | solution.py:95
  8.7 3.3 %project.5 = (f32[128,2048]{1,0:T(8,128)S(1)}, f32[128,2048]{1,0:T(8,128)S(1)}, f32[128,2048]{1,0:T(8,128)S(1)}, f32[128,2048]{1,0:T(8,128)S(1)}) custom-call(s32[2,32]{1,0:T(2,128)} %bitcast.3, bf16[1024,128]{1,0:T(8,128)(2,1)} %refs_0_, bf16[1024,2048]{1,0:T(8,128)(2,1)} %lap_ref.5, bf16[128,2048]{1,0:T(8,128)(2,1)S(1)} %get-tuple-element.25.refs_0_), custom_call_target="tpu_custom_call" | custom-call | flops 1000 | bytes 1 | tf_op jit(solution)/shard_map/project/pallas_call | solution.py:95
  12.0 1.0 %collective-permute-done.1.received_ref = bf16[128,1024]{1,0:T(8,128)(2,1)S(1)} collective-permute-done((bf16[128,1024]{1,0:T(8,128)(2,1)S(1)}, bf16[128,1024]{1,0:T(8,128)(2,1)S(1)}, u32[]{:S(2)}, u32[]{:S(2)}) %collective-permute-start.1) | collective-permute-done | bytes 262176 | tf_op jit(solution)/shard_map/y2a/ppermute | solution.py:44
  13.0 2.1 %collective-permute-start.9 = (bf16[128,2048]{1,0:T(8,128)(2,1)S(1)}, bf16[128,2048]{1,0:T(8,128)(2,1)S(1)}, u32[]{:S(2)}, u32[]{:S(2)}) collective-permute-start(bf16[128,2048]{1,0:T(8,128)(2,1)S(1)} %get-tuple-element.25.refs_0_), channel_id=1, source_target_pairs={{0,16},{4,20},{8,24},{12,28},{16,0},{20,4},{24,8},{28,12},{1,17},{... | collective-permute-start | bytes 1572872 | tf_op jit(solution)/shard_map/y3a/ppermute | solution.py:44
  15.1 3.4 %collective-permute-done.received_ref = bf16[128,1024]{1,0:T(8,128)(2,1)S(1)} collective-permute-done((bf16[128,1024]{1,0:T(8,128)(2,1)S(1)}, bf16[128,1024]{1,0:T(8,128)(2,1)S(1)}, u32[]{:S(2)}, u32[]{:S(2)}) %collective-permute-start) | collective-permute-done | bytes 262176 | tf_op jit(solution)/shard_map/y2b/ppermute | solution.py:44
  18.6 2.1 %collective-permute-start.11 = (bf16[128,2048]{1,0:T(8,128)(2,1)S(1)}, bf16[128,2048]{1,0:T(8,128)(2,1)S(1)}, u32[]{:S(2)}, u32[]{:S(2)}) collective-permute-start(bf16[128,2048]{1,0:T(8,128)(2,1)S(1)} %get-tuple-element.29), channel_id=1, source_target_pairs={{0,16},{4,20},{8,24},{12,28},{16,0},{20,4},{24,8},{28,12},{1,17},{... | collective-permute-start | bytes 1572872 | tf_op jit(solution)/shard_map/y1a/ppermute | solution.py:44
  20.7 2.6 %collective-permute-start.12 = (bf16[128,1024]{1,0:T(8,128)(2,1)S(1)}, bf16[128,1024]{1,0:T(8,128)(2,1)S(1)}, u32[]{:S(2)}, u32[]{:S(2)}) collective-permute-start(bf16[128,1024]{1,0:T(8,128)(2,1)S(1)} %combine.6.refs_0_), channel_id=1, source_target_pairs={{0,2},{1,3},{2,0},{3,1},{4,6},{5,7},{6,4},{7,5},{8,10},{9,11},{10,... | collective-permute-start | bytes 786440 | tf_op jit(solution)/shard_map/z2a/ppermute | solution.py:44
  23.3 0.5 collective-permute-start.2
  23.8 6.0 %collective-permute-done.9.received_ref = bf16[128,2048]{1,0:T(8,128)(2,1)S(1)} collective-permute-done((bf16[128,2048]{1,0:T(8,128)(2,1)S(1)}, bf16[128,2048]{1,0:T(8,128)(2,1)S(1)}, u32[]{:S(2)}, u32[]{:S(2)}) %collective-permute-start.9) | collective-permute-done | bytes 524320 | tf_op jit(solution)/shard_map/y3a/ppermute | solution.py:44
  29.8 0.1 combine.8.refs_0_
  29.9 2.1 %collective-permute-start.10 = (bf16[128,2048]{1,0:T(8,128)(2,1)S(1)}, bf16[128,2048]{1,0:T(8,128)(2,1)S(1)}, u32[]{:S(2)}, u32[]{:S(2)}) collective-permute-start(bf16[128,2048]{1,0:T(8,128)(2,1)S(1)} %get-tuple-element.26), channel_id=1, source_target_pairs={{0,16},{4,20},{8,24},{12,28},{16,0},{20,4},{24,8},{28,12},{1,17},{... | collective-permute-start | bytes 1572872 | tf_op jit(solution)/shard_map/y0a/ppermute | solution.py:44
  32.0 3.6 %collective-permute-start.13 = (bf16[128,2048]{1,0:T(8,128)(2,1)S(1)}, bf16[128,2048]{1,0:T(8,128)(2,1)S(1)}, u32[]{:S(2)}, u32[]{:S(2)}) collective-permute-start(bf16[128,2048]{1,0:T(8,128)(2,1)S(1)} %combine.8.refs_0_), channel_id=1, source_target_pairs={{0,3},{1,2},{2,1},{3,0},{4,7},{5,6},{6,5},{7,4},{8,11},{9,10},{10,... | collective-permute-start | bytes 1572872 | tf_op jit(solution)/shard_map/z3a/ppermute | solution.py:44
  35.6 1.5 %collective-permute-start.3 = (bf16[1024,128]{1,0:T(8,128)(2,1)S(1)}, bf16[1024,128]{1,0:T(8,128)(2,1)S(1)}, u32[]{:S(2)}, u32[]{:S(2)}) collective-permute-start(bf16[1024,128]{1,0:T(8,128)(2,1)S(1)} %copy-done), channel_id=1, source_target_pairs={{0,8},{4,12},{8,0},{12,4},{16,24},{20,28},{24,16},{28,20},{1,9},{5... | collective-permute-start | bytes 786440 | tf_op jit(solution)/shard_map/gather2/ppermute | solution.py:44
  37.1 9.5 %collective-permute-done.2.refs_1_ = bf16[1024,128]{1,0:T(8,128)(2,1)S(1)} collective-permute-done((bf16[1024,128]{1,0:T(8,128)(2,1)S(1)}, bf16[1024,128]{1,0:T(8,128)(2,1)S(1)}, u32[]{:S(2)}, u32[]{:S(2)}) %collective-permute-start.2) | collective-permute-done | bytes 262176 | tf_op jit(solution)/shard_map/gather4/ppermute | solution.py:44
  46.6 2.0 %collective-permute-start.4 = (bf16[1024,128]{1,0:T(8,128)(2,1)S(1)}, bf16[1024,128]{1,0:T(8,128)(2,1)S(1)}, u32[]{:S(2)}, u32[]{:S(2)}) collective-permute-start(bf16[1024,128]{1,0:T(8,128)(2,1)S(1)} %collective-permute-done.2.refs_1_), channel_id=1, source_target_pairs={{0,8},{4,12},{8,0},{12,4},{16,24},{20,28},{24,16},{28,20},{1,9},{5... | collective-permute-start | bytes 786440 | tf_op jit(solution)/shard_map/gather2/ppermute | solution.py:44
  48.7 0.1 combine.9.refs_0_
  48.8 1.6 %collective-permute-start.16 = (bf16[128,2048]{1,0:T(8,128)(2,1)S(1)}, bf16[128,2048]{1,0:T(8,128)(2,1)S(1)}, u32[]{:S(2)}, u32[]{:S(2)}) collective-permute-start(bf16[128,2048]{1,0:T(8,128)(2,1)S(1)} %combine.9.refs_0_), channel_id=1, source_target_pairs={{0,1},{1,0},{2,3},{3,2},{4,5},{5,4},{6,7},{7,6},{8,9},{9,8},{10,11... | collective-permute-start | bytes 1572872 | tf_op jit(solution)/shard_map/z1a/ppermute | solution.py:44
  50.4 0.8 %restrict.1 = (bf16[32,512]{1,0:T(8,128)(2,1)S(1)}, bf16[32,512]{1,0:T(8,128)(2,1)S(1)}) custom-call(s32[2,32]{1,0:T(2,128)S(1)} %bitcast.4, bf16[32,1024]{1,0:T(8,128)(2,1)S(1)} %copy-done.2, bf16[1024,128]{1,0:T(8,128)(2,1)S(1)} %copy-done, bf16[128,2048]{1,0:T(8,128)(2,1)S(1)} %combine.8.refs_0_), custom_call_target="tpu_custom_call" | custom-call | flops 1000 | bytes 1 | tf_op jit(solution)/shard_map/restrict/pallas_call | solution.py:256
  51.2 1.6 %collective-permute-start.14 = (bf16[32,512]{1,0:T(8,128)(2,1)S(1)}, bf16[32,512]{1,0:T(8,128)(2,1)S(1)}, u32[]{:S(2)}, u32[]{:S(2)}) collective-permute-start(bf16[32,512]{1,0:T(8,128)(2,1)S(1)} %get-tuple-element.31), channel_id=1, source_target_pairs={{0,16},{4,20},{8,24},{12,28},{16,0},{20,4},{24,8},{28,12},{1,17},{... | collective-permute-start | bytes 98312 | tf_op jit(solution)/shard_map/vectors/ppermute | solution.py:44
  52.8 2.9 %collective-permute-done.4.refs_3_ = bf16[1024,128]{1,0:T(8,128)(2,1)S(1)} collective-permute-done((bf16[1024,128]{1,0:T(8,128)(2,1)S(1)}, bf16[1024,128]{1,0:T(8,128)(2,1)S(1)}, u32[]{:S(2)}, u32[]{:S(2)}) %collective-permute-start.4) | collective-permute-done | bytes 262176 | tf_op jit(solution)/shard_map/gather2/ppermute | solution.py:44
  55.6 2.8 %collective-permute-start.15 = (bf16[128,1024]{1,0:T(8,128)(2,1)S(1)}, bf16[128,1024]{1,0:T(8,128)(2,1)S(1)}, u32[]{:S(2)}, u32[]{:S(2)}) collective-permute-start(bf16[128,1024]{1,0:T(8,128)(2,1)S(1)} %combine.7.refs_0_), channel_id=1, source_target_pairs={{0,2},{1,3},{2,0},{3,1},{4,6},{5,7},{6,4},{7,5},{8,10},{9,11},{10,... | collective-permute-start | bytes 786440 | tf_op jit(solution)/shard_map/z2b/ppermute | solution.py:44
  58.5 0.5 collective-permute-start.7
  59.0 0.1 collective-permute-start.8
  59.1 0.6 combine.10.refs_3_
  59.7 0.8 %copy-done.1 = bf16[32,512]{1,0:T(8,128)(2,1)S(1)} copy-done((bf16[32,512]{1,0:T(8,128)(2,1)S(1)}, bf16[32,512]{1,0:T(8,128)(2,1)}, u32[]{:S(2)}) %copy-start.1) | copy-done | bytes 32792
  60.5 0.1 combine.11.refs_8_
  60.6 7.1 %collective-permute-done.15.refs_10_ = bf16[128,1024]{1,0:T(8,128)(2,1)S(1)} collective-permute-done((bf16[128,1024]{1,0:T(8,128)(2,1)S(1)}, bf16[128,1024]{1,0:T(8,128)(2,1)S(1)}, u32[]{:S(2)}, u32[]{:S(2)}) %collective-permute-start.15) | collective-permute-done | bytes 262176 | tf_op jit(solution)/shard_map/z2b/ppermute | solution.py:44
  67.7 0.9 %collective-permute-done.16.refs_11_ = bf16[128,2048]{1,0:T(8,128)(2,1)S(1)} collective-permute-done((bf16[128,2048]{1,0:T(8,128)(2,1)S(1)}, bf16[128,2048]{1,0:T(8,128)(2,1)S(1)}, u32[]{:S(2)}, u32[]{:S(2)}) %collective-permute-start.16) | collective-permute-done | bytes 524320 | tf_op jit(solution)/shard_map/z1a/ppermute | solution.py:44
  68.5 3.4 %finish.1 = bf16[128,4096]{1,0:T(8,128)(2,1)} custom-call(s32[2,32]{1,0:T(2,128)S(1)} %bitcast.5, bf16[1024,128]{1,0:T(8,128)(2,1)S(1)} %copy-done, bf16[1024,128]{1,0:T(8,128)(2,1)S(1)} %collective-permute-done.2.refs_1_, bf16[1024,128]{1,0:T(8,128)(2,1)S(1)} %collective-permute-done.3.refs_2_, bf16[1024,128]{1,0:T(8,128)(2,1)S(1)} %collective-permute-done.4.refs_3_, ...), custom_call_target="tpu_custom_call" | custom-call | flops 1000000000 | bytes 1000000 | tf_op jit(solution)/shard_map/finish/pallas_call | solution.py:218
  (21 shorter events, 0.2 us)
Async XLA Ops:
  2.8 10.2 %collective-permute-start.1 = (bf16[128,1024]{1,0:T(8,128)(2,1)S(1)}, bf16[128,1024]{1,0:T(8,128)(2,1)S(1)}, u32[]{:S(2)}, u32[]{:S(2)}) collective-permute-start(bf16[128,1024]{1,0:T(8,128)(2,1)S(1)} %get-tuple-element.17.refs_0_), channel_id=1, source_target_pairs={{0,16},{4,20},{8,24},{12,28},{16,0},{20,4},{24,8},{28,12},{1,17},{... | collective-permute-start | bytes 786440 | tf_op jit(solution)/shard_map/y2a/ppermute | solution.py:44
  5.8 12.8 %collective-permute-start = (bf16[128,1024]{1,0:T(8,128)(2,1)S(1)}, bf16[128,1024]{1,0:T(8,128)(2,1)S(1)}, u32[]{:S(2)}, u32[]{:S(2)}) collective-permute-start(bf16[128,1024]{1,0:T(8,128)(2,1)S(1)} %get-tuple-element.20), channel_id=1, source_target_pairs={{0,16},{4,20},{8,24},{12,28},{16,0},{20,4},{24,8},{28,12},{1,17},{... | collective-permute-start | bytes 786440 | tf_op jit(solution)/shard_map/y2b/ppermute | solution.py:44
  8.7 14.6 %copy-start = (bf16[1024,128]{1,0:T(8,128)(2,1)S(1)}, bf16[1024,128]{1,0:T(8,128)(2,1)}, u32[]{:S(2)}) copy-start(bf16[1024,128]{1,0:T(8,128)(2,1)} %refs_0_) | copy-start | bytes 786436
  13.0 37.4 %copy-start.2 = (bf16[32,1024]{1,0:T(8,128)(2,1)S(1)}, bf16[32,1024]{1,0:T(8,128)(2,1)}, u32[]{:S(2)}) copy-start(bf16[32,1024]{1,0:T(8,128)(2,1)} %vec_ref.1) | copy-start | bytes 196612
  13.0 37.4 %copy-start.3 = (s32[32,2]{0,1:T(2,128)S(1)}, s32[32,2]{0,1:T(2,128)}, u32[]{:S(2)}) copy-start(s32[32,2]{0,1:T(2,128)} %param.7) | copy-start | bytes 772
  13.0 16.8 %collective-permute-start.9 = (bf16[128,2048]{1,0:T(8,128)(2,1)S(1)}, bf16[128,2048]{1,0:T(8,128)(2,1)S(1)}, u32[]{:S(2)}, u32[]{:S(2)}) collective-permute-start(bf16[128,2048]{1,0:T(8,128)(2,1)S(1)} %get-tuple-element.25.refs_0_), channel_id=1, source_target_pairs={{0,16},{4,20},{8,24},{12,28},{16,0},{20,4},{24,8},{28,12},{1,17},{... | collective-permute-start | bytes 1572872 | tf_op jit(solution)/shard_map/y3a/ppermute | solution.py:44
  18.6 28.0 %collective-permute-start.11 = (bf16[128,2048]{1,0:T(8,128)(2,1)S(1)}, bf16[128,2048]{1,0:T(8,128)(2,1)S(1)}, u32[]{:S(2)}, u32[]{:S(2)}) collective-permute-start(bf16[128,2048]{1,0:T(8,128)(2,1)S(1)} %get-tuple-element.29), channel_id=1, source_target_pairs={{0,16},{4,20},{8,24},{12,28},{16,0},{20,4},{24,8},{28,12},{1,17},{... | collective-permute-start | bytes 1572872 | tf_op jit(solution)/shard_map/y1a/ppermute | solution.py:44
  20.7 14.9 %collective-permute-start.12 = (bf16[128,1024]{1,0:T(8,128)(2,1)S(1)}, bf16[128,1024]{1,0:T(8,128)(2,1)S(1)}, u32[]{:S(2)}, u32[]{:S(2)}) collective-permute-start(bf16[128,1024]{1,0:T(8,128)(2,1)S(1)} %combine.6.refs_0_), channel_id=1, source_target_pairs={{0,2},{1,3},{2,0},{3,1},{4,6},{5,7},{6,4},{7,5},{8,10},{9,11},{10,... | collective-permute-start | bytes 786440 | tf_op jit(solution)/shard_map/z2a/ppermute | solution.py:44
  23.3 23.3 %collective-permute-start.2 = (bf16[1024,128]{1,0:T(8,128)(2,1)S(1)}, bf16[1024,128]{1,0:T(8,128)(2,1)S(1)}, u32[]{:S(2)}, u32[]{:S(2)}) collective-permute-start(bf16[1024,128]{1,0:T(8,128)(2,1)S(1)} %copy-done), channel_id=1, source_target_pairs={{0,16},{4,20},{8,24},{12,28},{16,0},{20,4},{24,8},{28,12},{1,17},{... | collective-permute-start | bytes 786440 | tf_op jit(solution)/shard_map/gather4/ppermute | solution.py:44
  29.9 28.6 %collective-permute-start.10 = (bf16[128,2048]{1,0:T(8,128)(2,1)S(1)}, bf16[128,2048]{1,0:T(8,128)(2,1)S(1)}, u32[]{:S(2)}, u32[]{:S(2)}) collective-permute-start(bf16[128,2048]{1,0:T(8,128)(2,1)S(1)} %get-tuple-element.26), channel_id=1, source_target_pairs={{0,16},{4,20},{8,24},{12,28},{16,0},{20,4},{24,8},{28,12},{1,17},{... | collective-permute-start | bytes 1572872 | tf_op jit(solution)/shard_map/y0a/ppermute | solution.py:44
  32.0 27.0 %collective-permute-start.13 = (bf16[128,2048]{1,0:T(8,128)(2,1)S(1)}, bf16[128,2048]{1,0:T(8,128)(2,1)S(1)}, u32[]{:S(2)}, u32[]{:S(2)}) collective-permute-start(bf16[128,2048]{1,0:T(8,128)(2,1)S(1)} %combine.8.refs_0_), channel_id=1, source_target_pairs={{0,3},{1,2},{2,1},{3,0},{4,7},{5,6},{6,5},{7,4},{8,11},{9,10},{10,... | collective-permute-start | bytes 1572872 | tf_op jit(solution)/shard_map/z3a/ppermute | solution.py:44
  35.6 13.2 %collective-permute-start.3 = (bf16[1024,128]{1,0:T(8,128)(2,1)S(1)}, bf16[1024,128]{1,0:T(8,128)(2,1)S(1)}, u32[]{:S(2)}, u32[]{:S(2)}) collective-permute-start(bf16[1024,128]{1,0:T(8,128)(2,1)S(1)} %copy-done), channel_id=1, source_target_pairs={{0,8},{4,12},{8,0},{12,4},{16,24},{20,28},{24,16},{28,20},{1,9},{5... | collective-permute-start | bytes 786440 | tf_op jit(solution)/shard_map/gather2/ppermute | solution.py:44
  46.6 4.6 %collective-permute-start.5 = (bf16[1024,128]{1,0:T(8,128)(2,1)S(1)}, bf16[1024,128]{1,0:T(8,128)(2,1)S(1)}, u32[]{:S(2)}, u32[]{:S(2)}) collective-permute-start(bf16[1024,128]{1,0:T(8,128)(2,1)S(1)} %copy-done), channel_id=1, source_target_pairs={{0,4},{4,0},{8,12},{12,8},{16,20},{20,16},{24,28},{28,24},{1,5},{5... | collective-permute-start | bytes 786440 | tf_op jit(solution)/shard_map/gather1/ppermute | solution.py:44
  46.6 9.0 %collective-permute-start.4 = (bf16[1024,128]{1,0:T(8,128)(2,1)S(1)}, bf16[1024,128]{1,0:T(8,128)(2,1)S(1)}, u32[]{:S(2)}, u32[]{:S(2)}) collective-permute-start(bf16[1024,128]{1,0:T(8,128)(2,1)S(1)} %collective-permute-done.2.refs_1_), channel_id=1, source_target_pairs={{0,8},{4,12},{8,0},{12,4},{16,24},{20,28},{24,16},{28,20},{1,9},{5... | collective-permute-start | bytes 786440 | tf_op jit(solution)/shard_map/gather2/ppermute | solution.py:44
  48.8 19.7 %collective-permute-start.16 = (bf16[128,2048]{1,0:T(8,128)(2,1)S(1)}, bf16[128,2048]{1,0:T(8,128)(2,1)S(1)}, u32[]{:S(2)}, u32[]{:S(2)}) collective-permute-start(bf16[128,2048]{1,0:T(8,128)(2,1)S(1)} %combine.9.refs_0_), channel_id=1, source_target_pairs={{0,1},{1,0},{2,3},{3,2},{4,5},{5,4},{6,7},{7,6},{8,9},{9,8},{10,11... | collective-permute-start | bytes 1572872 | tf_op jit(solution)/shard_map/z1a/ppermute | solution.py:44
  51.2 7.3 %collective-permute-start.14 = (bf16[32,512]{1,0:T(8,128)(2,1)S(1)}, bf16[32,512]{1,0:T(8,128)(2,1)S(1)}, u32[]{:S(2)}, u32[]{:S(2)}) collective-permute-start(bf16[32,512]{1,0:T(8,128)(2,1)S(1)} %get-tuple-element.31), channel_id=1, source_target_pairs={{0,16},{4,20},{8,24},{12,28},{16,0},{20,4},{24,8},{28,12},{1,17},{... | collective-permute-start | bytes 98312 | tf_op jit(solution)/shard_map/vectors/ppermute | solution.py:44
  55.6 12.0 %collective-permute-start.15 = (bf16[128,1024]{1,0:T(8,128)(2,1)S(1)}, bf16[128,1024]{1,0:T(8,128)(2,1)S(1)}, u32[]{:S(2)}, u32[]{:S(2)}) collective-permute-start(bf16[128,1024]{1,0:T(8,128)(2,1)S(1)} %combine.7.refs_0_), channel_id=1, source_target_pairs={{0,2},{1,3},{2,0},{3,1},{4,6},{5,7},{6,4},{7,5},{8,10},{9,11},{10,... | collective-permute-start | bytes 786440 | tf_op jit(solution)/shard_map/z2b/ppermute | solution.py:44
  58.5 9.2 %collective-permute-start.6 = (bf16[1024,128]{1,0:T(8,128)(2,1)S(1)}, bf16[1024,128]{1,0:T(8,128)(2,1)S(1)}, u32[]{:S(2)}, u32[]{:S(2)}) collective-permute-start(bf16[1024,128]{1,0:T(8,128)(2,1)S(1)} %collective-permute-done.2.refs_1_), channel_id=1, source_target_pairs={{0,4},{4,0},{8,12},{12,8},{16,20},{20,16},{24,28},{28,24},{1,5},{5... | collective-permute-start | bytes 786440 | tf_op jit(solution)/shard_map/gather1/ppermute | solution.py:44
  58.5 9.2 %collective-permute-start.7 = (bf16[1024,128]{1,0:T(8,128)(2,1)S(1)}, bf16[1024,128]{1,0:T(8,128)(2,1)S(1)}, u32[]{:S(2)}, u32[]{:S(2)}) collective-permute-start(bf16[1024,128]{1,0:T(8,128)(2,1)S(1)} %collective-permute-done.3.refs_2_), channel_id=1, source_target_pairs={{0,4},{4,0},{8,12},{12,8},{16,20},{20,16},{24,28},{28,24},{1,5},{5... | collective-permute-start | bytes 786440 | tf_op jit(solution)/shard_map/gather1/ppermute | solution.py:44
  59.0 8.7 %collective-permute-start.8 = (bf16[1024,128]{1,0:T(8,128)(2,1)S(1)}, bf16[1024,128]{1,0:T(8,128)(2,1)S(1)}, u32[]{:S(2)}, u32[]{:S(2)}) collective-permute-start(bf16[1024,128]{1,0:T(8,128)(2,1)S(1)} %collective-permute-done.4.refs_3_), channel_id=1, source_target_pairs={{0,4},{4,0},{8,12},{12,8},{16,20},{20,16},{24,28},{28,24},{1,5},{5... | collective-permute-start | bytes 786440 | tf_op jit(solution)/shard_map/gather1/ppermute | solution.py:44
  59.7 0.8 %copy-start.1 = (bf16[32,512]{1,0:T(8,128)(2,1)S(1)}, bf16[32,512]{1,0:T(8,128)(2,1)}, u32[]{:S(2)}) copy-start(bf16[32,512]{1,0:T(8,128)(2,1)} %combine.10.refs_3_) | copy-start | bytes 98308

commit v3 on v2

--- a/solution.py
+++ b/solution.py
@@ -6,22 +6,31 @@
 from jax.sharding import PartitionSpec as P
 
 
-AHEAD = 2
+YAFTER = {'3a': ['2a'], '1a': ['2b'], '1b': ['3a'], '3b': ['1a'], '0a': ['1b'], '0b': ['3b']}
 HEAD = 1
-GATHER = 1
-VECTORS = 2
-VECTORS_AT = '0a'
+GATHER = '2b'
+VECTORS = '1b'
+VECTORS_AT = ''
 ZAFTER = {}
-FINISH = 1000000000
+FINISH = 1000
 JOBS = 2
-WAITS = {'1a': ['z2a'], '0a': ['z3a', 'g2']}
-
-
-def CHUNKS(half, count):
-    chunks = [(half, 0, 8), (half, 8, 16)]
-    for far, near in zip(range(half + 1, count), range(1, half)):
-        chunks += [(far, 0, 16), (near, 0, 16)]
-    return chunks + [(0, 0, 16)]
+ASSEMBLE_Y = ''
+VECTORS_Y = ''
+PFLOPS = (1000, 1000)
+CFLOPS = 1000
+ASSEMBLE_AT = ''
+VECFLOPS = 1000
+VECDEP = -1
+ASSEMBLE = 100000000
+WAITS = {'3a': ['z2a'], '1b': ['g1', 'z2b', 'g2'], '0a': ['z3a', 'z1b', 'v', 'z3b'], '0b': ['g3', 'z1a']}
+
+
+TOKENS = [('h', 0, 8), ('h', 8, 16), ('f', 0, 8), ('n', 0, 8), ('n', 8, 16), ('f', 8, 16), ('0', 0, 8), ('0', 8, 16)]
+
+
+def chunks_of(half, count):
+    kinds = {"h": [half], "f": range(half + 1, count), "n": range(1, half), "0": [0]}
+    return [(step, lo, hi) for kind, lo, hi in TOKENS for step in kinds[kind]]
 
 
 def estimate(flops=1000):
@@ -54,6 +63,7 @@
     fine_rows = interp.shape[0] // tile
     coarse_rows = fine_rows // 2
     cols = laplacian.shape[1]
+    coarse_cols = cols // tile // 2
     half = lax.axis_size("row") // 2
     count = coarse_rows * tile // lax.axis_size("col")
     outs = [
@@ -66,6 +76,12 @@
         out_refs = list(refs[len(earlier) : len(earlier) + len(outs)])
         lap_buf, interp_buf, whole_ref, sems = refs[len(earlier) + len(outs) :]
         row, col = lax.axis_index("row"), lax.axis_index("col")
+        col_half = lax.axis_size("col") // 2
+        sources = []
+        for p in range(cols // tile):
+            group = p // coarse_cols * col_half + col % col_half
+            j = pairs_ref[col // col_half, group * coarse_cols + p % coarse_cols]
+            sources.append(pl.multiple_of((j - col * 2 * coarse_cols) * tile, tile))
         copies = []
         for slot, (step, mine, _, _) in enumerate(jobs):
             owner = row if mine else row ^ half
@@ -82,14 +98,19 @@
             left = interp_buf[slot]
             for begin, end in spans:
                 out_ref = out_refs.pop(0)
-                result = contract_rows(left, lap_buf[slot, :, begin:end])
-                if count != tile:
-                    whole_ref[:, : end - begin] = result
-                    first = pl.multiple_of(((col ^ step) * count) % tile, count)
-                    result = whole_ref[pl.ds(first, count), : end - begin]
-                out_ref[...] = result.astype(out_ref.dtype)
-
-    spare = (8, 128) if count == tile else (tile, cols)
+                for at in range(begin, end, 2 * tile):
+                    right = [
+                        lap_buf[slot, :, pl.ds(source, tile)]
+                        for source in sources[at // tile : at // tile + 2]
+                    ]
+                    result = contract_rows(left, jnp.concatenate(right, axis=1))
+                    if count != tile:
+                        whole_ref[...] = result
+                        first = pl.multiple_of(((col ^ step) * count) % tile, count)
+                        result = whole_ref[pl.ds(first, count), :]
+                    out_ref[:, at - begin : at - begin + 2 * tile] = result.astype(out_ref.dtype)
+
+    spare = (8, 128) if count == tile else (tile, 2 * tile)
     size = sum(out.size * out.dtype.itemsize for out in outs)
     size += len(jobs) * tile * (cols + tile) * 2 + spare[0] * spare[1] * 4
     return pl.pallas_call(
@@ -110,7 +131,7 @@
     )(in_hbm(pairs), in_hbm(interp), in_hbm(laplacian), *earlier)
 
 
-def combine(own, begin, received, *earlier):
+def combine(own, begin, received, *earlier, flops=1000):
     end = begin + received.shape[1]
 
     def body(own_ref, received_ref, *refs):
@@ -124,7 +145,7 @@
         + [pl.BlockSpec(memory_space=pl.ANY)] * len(earlier),
         out_specs=pl.BlockSpec(memory_space=pltpu.VMEM),
         compiler_params=pltpu.CompilerParams(vmem_limit_bytes=8 * 1024 * 1024),
-        cost_estimate=estimate(),
+        cost_estimate=estimate(flops),
         name="combine",
     )(own, received, *earlier)
 
@@ -137,66 +158,89 @@
     return blocks
 
 
-def finish(jobs, interp_blocks, pairs, before, fine_cols, *earlier):
-    tile = interp_blocks[0].shape[1]
-    fine_rows = interp_blocks[0].shape[0] // tile
-    count = jobs[0][0][0].shape[0]
-    row_count = lax.axis_size("row")
-    half = lax.axis_size("col") // 2
-    coarse_cols = fine_cols // 2
-    width = coarse_cols * tile
-    total = row_count * fine_rows * tile // 2
-    pieces = [
-        (2 * n + which, part)
-        for n, (near, far, _) in enumerate(jobs)
-        for which, parts in enumerate((near, far))
-        for part in parts
-    ]
-    sources = [*interp_blocks, *(part for _, part in pieces)]
+def assemble(blocks, pairs, fine_cols, *earlier):
+    rows, tile = blocks[0].shape
+    fine_rows, row_count = rows // tile, lax.axis_size("row")
+    coarse_cols, half = fine_cols // 2, lax.axis_size("col") // 2
 
     def body(pairs_ref, *refs):
-        out_ref, wide, interp_buf, buf, sem, fetch = refs[-6:]
+        out_ref, buf, fetch = refs[-3:]
         row, col = lax.axis_index("row"), lax.axis_index("col")
-        upper = col // half
-        begins, fetches = [0] * (2 * len(jobs)), []
-        for k, ref in enumerate(refs[: len(sources)]):
-            if k < len(interp_blocks):
-                target = interp_buf.at[k]
-            else:
-                which = pieces[k - len(interp_blocks)][0]
-                begin = begins[which]
-                begins[which] = begin + ref.shape[1]
-                target = wide.at[which, :, begin : begins[which]]
-            fetches.append(pltpu.make_async_copy(ref, target, fetch.at[k]))
+        fetches = [
+            pltpu.make_async_copy(ref, buf.at[pl.ds(k * rows, rows), :], fetch.at[k])
+            for k, ref in enumerate(refs[: len(blocks)])
+        ]
         for copy in fetches:
             copy.start()
         for copy in fetches:
             copy.wait()
-        copies = []
-        for n, (_, _, step) in enumerate(jobs):
+        upper = col // half
+        for step in range(half):
+            for p in range(fine_cols):
+                group = p // coarse_cols * half + (col ^ step) % half
+                d = group * coarse_cols + p % coarse_cols
+                for which, j in enumerate((pairs_ref[upper, d], pairs_ref[1 - upper, d])):
+                    source = (j // fine_rows) ^ row
+                    place, bit = 0, row_count // 2
+                    while bit:
+                        place = place * 2 + source % 2
+                        source, bit = source // 2, bit // 2
+                    at = pl.multiple_of((place * fine_rows + j % fine_rows) * tile, tile)
+                    begin = ((step * fine_cols + p) * 2 + which) * tile
+                    out_ref[begin : begin + tile, :] = buf[pl.ds(at, tile), :]
+
+    return pl.pallas_call(
+        body,
+        out_shape=jax.ShapeDtypeStruct((len(blocks) * rows, tile), blocks[0].dtype),
+        in_specs=[pl.BlockSpec(memory_space=pltpu.SMEM)]
+        + [pl.BlockSpec(memory_space=pl.ANY)] * (len(blocks) + len(earlier)),
+        out_specs=pl.BlockSpec(memory_space=pltpu.VMEM),
+        scratch_shapes=[
+            pltpu.VMEM((len(blocks) * rows, tile), blocks[0].dtype),
+            pltpu.SemaphoreType.DMA((len(blocks),)),
+        ],
+        cost_estimate=estimate(ASSEMBLE),
+        compiler_params=pltpu.CompilerParams(
+            vmem_limit_bytes=len(blocks) * rows * tile * 4 + 4 * 1024 * 1024
+        ),
+        name="assemble",
+    )(in_hbm(pairs), *blocks, *earlier)
+
+
+def finish(jobs, paired_interp, before, fine_cols, *earlier):
+    tile = paired_interp.shape[1]
+    count = jobs[0][0][0].shape[0]
+    half = lax.axis_size("col") // 2
+    coarse_cols = fine_cols // 2
+    width = coarse_cols * tile
+    total = paired_interp.shape[0] // 2
+    pieces = [part for near, far, _ in jobs for part in (*near, *far)]
+
+    def tile_of(refs, p):
+        begin = p * tile
+        for ref in refs:
+            if begin < ref.shape[1]:
+                return ref[:, begin : begin + tile]
+            begin -= ref.shape[1]
+
+    def body(interp_ref, *refs):
+        out_ref, buf, sem = refs[-3:]
+        col = lax.axis_index("col")
+        copies, taken = [], 0
+        for n, (near, far, step) in enumerate(jobs):
+            near_refs = refs[taken : taken + len(near)]
+            far_refs = refs[taken + len(near) : taken + len(near) + len(far)]
+            taken += len(near) + len(far)
             for part in range(2):
+                for k in range(coarse_cols):
+                    p = part * coarse_cols + k
+                    left = jnp.concatenate([tile_of(near_refs, p), tile_of(far_refs, p)], axis=1)
+                    at = (step * fine_cols + p) * 2 * tile
+                    result = jnp.dot(
+                        left, interp_ref[at : at + 2 * tile, :], preferred_element_type=jnp.float32
+                    )
+                    buf[2 * n + part, :, k * tile : (k + 1) * tile] = result.astype(buf.dtype)
                 group = part * half + (col ^ step) % half
-                for k in range(coarse_cols):
-                    d = group * coarse_cols + k
-                    result = None
-                    for which, j, owner in (
-                        (0, pairs_ref[upper, d], col ^ step),
-                        (1, pairs_ref[1 - upper, d], col ^ step ^ half),
-                    ):
-                        start = pl.multiple_of((j - owner * fine_cols) * tile, tile)
-                        source = (j // fine_rows) ^ row
-                        place, bit = 0, row_count // 2
-                        while bit:
-                            place = place * 2 + source % 2
-                            source, bit = source // 2, bit // 2
-                        at = pl.multiple_of((j % fine_rows) * tile, tile)
-                        product = jnp.dot(
-                            wide[2 * n + which, :, pl.ds(start, tile)],
-                            interp_buf[place, pl.ds(at, tile), :],
-                            preferred_element_type=jnp.float32,
-                        )
-                        result = product if result is None else result + product
-                    buf[2 * n + part, :, k * tile : (k + 1) * tile] = result.astype(buf.dtype)
                 copy = pltpu.make_async_copy(
                     buf.at[2 * n + part],
                     out_ref.at[:, pl.ds(pl.multiple_of(group * width, width), width)],
@@ -207,26 +251,23 @@
         for copy in copies:
             copy.wait()
 
-    operands = [pairs, *sources]
+    operands = [paired_interp, *pieces]
+    in_specs = [pl.BlockSpec(memory_space=pltpu.VMEM)] * len(operands)
     aliases = {}
     if before is not None:
         aliases = {len(operands): 0}
         operands.append(before)
     operands += earlier
-    blocks = len(interp_blocks)
-    size = blocks * fine_rows * tile * tile * 2 + 2 * len(jobs) * count * (fine_cols * tile + width) * 2
+    in_specs += [pl.BlockSpec(memory_space=pl.ANY)] * (len(operands) - len(in_specs))
+    size = paired_interp.size * 2 + 2 * len(jobs) * count * (fine_cols * tile + width) * 2
     return pl.pallas_call(
         body,
         out_shape=jax.ShapeDtypeStruct((count, total), jnp.bfloat16),
-        in_specs=[pl.BlockSpec(memory_space=pltpu.SMEM)]
-        + [pl.BlockSpec(memory_space=pl.ANY)] * (len(operands) - 1),
+        in_specs=in_specs,
         out_specs=pl.BlockSpec(memory_space=pl.ANY),
         scratch_shapes=[
-            pltpu.VMEM((2 * len(jobs), count, fine_cols * tile), jnp.bfloat16),
-            pltpu.VMEM((blocks, fine_rows * tile, tile), jnp.bfloat16),
             pltpu.VMEM((2 * len(jobs), count, width), jnp.bfloat16),
             pltpu.SemaphoreType.DMA((2 * len(jobs),)),
-            pltpu.SemaphoreType.DMA((len(sources),)),
         ],
         input_output_aliases=aliases,
         cost_estimate=estimate(FINISH),
@@ -279,7 +320,7 @@
     pairs = pairs.T
 
     whole = [(0, cols)]
-    order = CHUNKS(col_half, col_count)
+    order = chunks_of(col_half, col_count)
     steps = list(dict.fromkeys(step for step, _, _ in order))
     spans = {
         step: [(lo * cols // 16, hi * cols // 16) for other, lo, hi in order if other == step]
@@ -292,45 +333,58 @@
         laplacian, interp, pairs, [(s, False, jnp.bfloat16, spans[s]) for s in steps[:head]]
     )
     sent += project(
-        laplacian, interp, pairs, [(s, False, jnp.bfloat16, spans[s]) for s in steps[head:]], sent[0]
+        laplacian, interp, pairs, [(s, False, jnp.bfloat16, spans[s]) for s in steps[head:]], sent[0], flops=PFLOPS[0]
     )
     grouped = [(step, span) for step in steps for span in spans[step]]
     sent = dict(zip(grouped, sent))
     kept = project(
-        laplacian, interp, pairs, [(s, True, jnp.float32, whole) for s in steps], sent[grouped[cut]]
+        laplacian, interp, pairs, [(s, True, jnp.float32, whole) for s in steps], sent[grouped[cut]], flops=PFLOPS[1]
     )
     kept = dict(zip(steps, kept))
     named, totals, held = {}, [kept[0]], {step: [] for step in steps}
+    interp_blocks = keep = None
     for k, (step, lo, hi) in enumerate(order):
         name, span = labels[k], (lo * cols // 16, hi * cols // 16)
         block = sent[step, span]
-        if k >= AHEAD:
-            block = after(block, totals[k + 1 - AHEAD])
+        if name in YAFTER:
+            block = after(block, *(named["t" + w] for w in YAFTER[name] if "t" + w in named))
+        if name == ASSEMBLE_Y:
+            paired_interp = assemble(interp_blocks, pairs, fine_cols)
+            block = after(block, paired_interp)
+        if name == VECTORS_Y:
+            coarse_vectors = combine(keep, 0, far_vec, totals[-1])
+            block = after(block, coarse_vectors)
         block = exchange(block, "row", row_half, "y" + name)
         waits = totals[-1:] + [named[w] for w in WAITS.get(name, ()) if w in named]
+        if name == ASSEMBLE_AT:
+            paired_interp = assemble(interp_blocks, pairs, fine_cols, *totals[-1:])
+            waits.append(paired_interp)
         if name == VECTORS_AT:
             coarse_vectors = combine(keep, 0, far_vec, totals[-1])
-            waits.append(coarse_vectors)
-        total = combine(kept[step], span[0], block, *waits)
+            waits.append(in_hbm(coarse_vectors))
+        total = combine(kept[step], span[0], block, *waits, flops=CFLOPS)
         totals.append(total)
+        named["t" + name] = total
         if step:
             later = [named[w] for w in ZAFTER.get(name, ()) if w in named]
             total = exchange(after(total, *later) if later else total, "col", step, "z" + name)
         named["z" + name] = total
         held[step].append(total)
-        if k == GATHER:
+        if name == GATHER or (k + 1 == len(order) and interp_blocks is None):
             interp_blocks = gather_blocks(after(interp, totals[-1]), "row")
             for place, value in enumerate(interp_blocks):
                 named[f"g{place}"] = value
-        if k == VECTORS:
+        if name == VECTORS or (k + 1 == len(order) and keep is None):
             keep, send = restrict(vectors, interp, pairs, totals[-1])
             named["v"] = far_vec = exchange(send, "row", row_half, "vectors")
-    if not VECTORS_AT:
-        coarse_vectors = combine(keep, 0, far_vec, totals[-1])
+    if VECTORS_AT not in labels and VECTORS_Y not in labels:
+        coarse_vectors = combine(keep, 0, far_vec, totals[VECDEP], flops=VECFLOPS)
     coarse = None
+    if ASSEMBLE_AT not in labels and ASSEMBLE_Y not in labels:
+        paired_interp = assemble(interp_blocks, pairs, fine_cols)
     jobs = [(held[step], held[step ^ col_half], step) for step in range(col_half)]
     for k in range(0, len(jobs), JOBS):
-        coarse = finish(jobs[k : k + JOBS], interp_blocks, pairs, coarse, fine_cols)
+        coarse = finish(jobs[k : k + JOBS], paired_interp, coarse, fine_cols)
     return (coarse, coarse_vectors)
 
 

time: 72.7 us -> 68.8 us (0.946)
  waiting for transfers between devices: 30.7 us -> 25.9 us
  starting transfers between devices: 26.4 us -> 27.9 us
  local copies, waits for them, and re-layouts: 0.78 us -> 0.01 us
    ppermute x17 -> x22, waiting for transfers between devices: 30.7 us -> 25.9 us  [exchange(): return lax.ppermute(block, axis, [(i, i ^ flip) for i in range(count)])]
    pallas_call x0 -> x1, Pallas kernels: none -> 2.34 us  [assemble(): pl.pallas_call(body, out_shape=jax.ShapeDtypeStruct((len(blocks) * rows,...]
    pallas_call x1, Pallas kernels: 3.38 us -> 1.43 us  [finish(): pl.pallas_call(body, out_shape=jax.ShapeDtypeStruct((count, total), jnp.b...]
    ppermute x17 -> x22, starting transfers between devices: 26.4 us -> 27.9 us  [exchange(): return lax.ppermute(block, axis, [(i, i ^ flip) for i in range(count)])]
    unnamed x8 -> x6, local copies, waits for them, and re-layouts: 0.78 us -> 0.01 us
  transfers between devices with their start and end apart: 17 -> 22, of which waited for: 7 -> 11; matrix products, arithmetic and copies ran while one was open for 0% -> 0% of each run, Pallas kernels for 11% -> 11%
where the time goes in v3:
time: 68.8 us; the launch traced here: 68.6 us
  starting transfers between devices  27.9 us (41%)
  waiting for transfers between devices  25.9 us (38%)
  Pallas kernels  14 us (20%)
  between operations  0.76 us (1%)
    ppermute x22, starting transfers between devices, exchange(): return lax.ppermute(block, axis, [(i, i ^ flip) for i in range(count)])  27.9 us
    ppermute x22, waiting for transfers between devices, exchange(): return lax.ppermute(block, axis, [(i, i ^ flip) for i in range(count)])  25.9 us
    pallas_call x3, Pallas kernels, project(): pl.pallas_call(body, out_shape=outs, in_specs=[pl.BlockSpec(memory_space=...  8.37 us
    pallas_call x1, Pallas kernels, assemble(): pl.pallas_call(body, out_shape=jax.ShapeDtypeStruct((len(blocks) * rows,...  2.34 us
    pallas_call x1, Pallas kernels, finish(): pl.pallas_call(body, out_shape=jax.ShapeDtypeStruct((count, total), jnp.b...  1.43 us
  transfers between devices with their start and end apart: 22, of which 11 were waited for; matrix products, arithmetic and copies ran while one was open for 0% of the time, Pallas kernels for 11%

profile of v3, /device:TPU:0, one launch (start us, length us, event | category | flops | bytes accessed | tf_op | source)
XLA Modules:
  0.0 68.6 jit_solution(12060717478177880890)
XLA Ops:
  0.6 2.2 %project.3 = (bf16[128,1024]{1,0:T(8,128)(2,1)S(1)}, bf16[128,1024]{1,0:T(8,128)(2,1)S(1)}) custom-call(s32[2,32]{1,0:T(2,128)} %bitcast.1, bf16[1024,128]{1,0:T(8,128)(2,1)} %interp_ref.7, bf16[1024,2048]{1,0:T(8,128)(2,1)} %lap_ref.5), custom_call_target="tpu_custom_call" | custom-call | flops 1000 | bytes 1 | tf_op jit(solution)/shard_map/project/pallas_call | solution.py:116
  2.8 3.0 %collective-permute-start.1 = (bf16[128,1024]{1,0:T(8,128)(2,1)S(1)}, bf16[128,1024]{1,0:T(8,128)(2,1)S(1)}, u32[]{:S(2)}, u32[]{:S(2)}) collective-permute-start(bf16[128,1024]{1,0:T(8,128)(2,1)S(1)} %get-tuple-element.23.refs_0_), channel_id=1, source_target_pairs={{0,16},{4,20},{8,24},{12,28},{16,0},{20,4},{24,8},{28,12},{1,17},{... | collective-permute-start | bytes 786440 | tf_op jit(solution)/shard_map/y2a/ppermute | solution.py:53
  5.9 2.9 %project.4 = (bf16[128,1024]{1,0:T(8,128)(2,1)S(1)}, bf16[128,1024]{1,0:T(8,128)(2,1)S(1)}, bf16[128,1024]{1,0:T(8,128)(2,1)S(1)}, bf16[128,1024]{1,0:T(8,128)(2...) custom-call(s32[2,32]{1,0:T(2,128)} %bitcast.2, bf16[1024,128]{1,0:T(8,128)(2,1)} %interp_ref.7, ...), custom_call_target="tpu_custom_call" | custom-call | flops 1000 | bytes 1 | tf_op jit(solution)/shard_map/project/pallas_call | solution.py:116
  8.8 3.3 %project.5 = (f32[128,2048]{1,0:T(8,128)S(1)}, f32[128,2048]{1,0:T(8,128)S(1)}, f32[128,2048]{1,0:T(8,128)S(1)}, f32[128,2048]{1,0:T(8,128)S(1)}) custom-call(s32[2,32]{1,0:T(2,128)} %bitcast.3, bf16[1024,128]{1,0:T(8,128)(2,1)} %interp_ref.7, bf16[1024,2048]{1,0:T(8,128)(2,1)} %lap_ref.5, bf16[128,1024]{1,0:T(8,128)(2,1)S(1)} %get-tuple-element.33.refs_0_), custom_call_target="tpu_custom_call" | custom-call | flops 1000 | bytes 1 | tf_op jit(solution)/shard_map/project/pallas_call | solution.py:116
  12.1 0.8 %collective-permute-done.1.received_ref = bf16[128,1024]{1,0:T(8,128)(2,1)S(1)} collective-permute-done((bf16[128,1024]{1,0:T(8,128)(2,1)S(1)}, bf16[128,1024]{1,0:T(8,128)(2,1)S(1)}, u32[]{:S(2)}, u32[]{:S(2)}) %collective-permute-start.1) | collective-permute-done | bytes 262176 | tf_op jit(solution)/shard_map/y2a/ppermute | solution.py:53
  13.0 3.2 %collective-permute-start.10 = (bf16[128,1024]{1,0:T(8,128)(2,1)S(1)}, bf16[128,1024]{1,0:T(8,128)(2,1)S(1)}, u32[]{:S(2)}, u32[]{:S(2)}) collective-permute-start(bf16[128,1024]{1,0:T(8,128)(2,1)S(1)} %combine.9.refs_0_), channel_id=1, source_target_pairs={{0,2},{1,3},{2,0},{3,1},{4,6},{5,7},{6,4},{7,5},{8,10},{9,11},{10,... | collective-permute-start | bytes 786440 | tf_op jit(solution)/shard_map/z2a/ppermute | solution.py:53
  16.2 1.5 %collective-permute-start.9 = (bf16[128,1024]{1,0:T(8,128)(2,1)S(1)}, bf16[128,1024]{1,0:T(8,128)(2,1)S(1)}, u32[]{:S(2)}, u32[]{:S(2)}) collective-permute-start(bf16[128,1024]{1,0:T(8,128)(2,1)S(1)} %get-tuple-element.33.refs_0_), channel_id=1, source_target_pairs={{0,16},{4,20},{8,24},{12,28},{16,0},{20,4},{24,8},{28,12},{1,17},{... | collective-permute-start | bytes 786440 | tf_op jit(solution)/shard_map/y3a/ppermute | solution.py:53
  17.8 0.8 %collective-permute-done.received_ref = bf16[128,1024]{1,0:T(8,128)(2,1)S(1)} collective-permute-done((bf16[128,1024]{1,0:T(8,128)(2,1)S(1)}, bf16[128,1024]{1,0:T(8,128)(2,1)S(1)}, u32[]{:S(2)}, u32[]{:S(2)}) %collective-permute-start) | collective-permute-done | bytes 262176 | tf_op jit(solution)/shard_map/y2b/ppermute | solution.py:53
  18.6 2.0 %collective-permute-start.12 = (bf16[128,1024]{1,0:T(8,128)(2,1)S(1)}, bf16[128,1024]{1,0:T(8,128)(2,1)S(1)}, u32[]{:S(2)}, u32[]{:S(2)}) collective-permute-start(bf16[128,1024]{1,0:T(8,128)(2,1)S(1)} %get-tuple-element.36), channel_id=1, source_target_pairs={{0,16},{4,20},{8,24},{12,28},{16,0},{20,4},{24,8},{28,12},{1,17},{... | collective-permute-start | bytes 786440 | tf_op jit(solution)/shard_map/y1a/ppermute | solution.py:53
  20.7 1.9 %collective-permute-start.3 = (bf16[1024,128]{1,0:T(8,128)(2,1)S(1)}, bf16[1024,128]{1,0:T(8,128)(2,1)S(1)}, u32[]{:S(2)}, u32[]{:S(2)}) collective-permute-start(bf16[1024,128]{1,0:T(8,128)(2,1)S(1)} %copy-done), channel_id=1, source_target_pairs={{0,8},{4,12},{8,0},{12,4},{16,24},{20,28},{24,16},{28,20},{1,9},{5... | collective-permute-start | bytes 786440 | tf_op jit(solution)/shard_map/gather2/ppermute | solution.py:53
  22.6 2.9 %collective-permute-done.9.received_ref = bf16[128,1024]{1,0:T(8,128)(2,1)S(1)} collective-permute-done((bf16[128,1024]{1,0:T(8,128)(2,1)S(1)}, bf16[128,1024]{1,0:T(8,128)(2,1)S(1)}, u32[]{:S(2)}, u32[]{:S(2)}) %collective-permute-start.9) | collective-permute-done | bytes 262176 | tf_op jit(solution)/shard_map/y3a/ppermute | solution.py:53
  25.5 1.9 %collective-permute-start.13 = (bf16[128,1024]{1,0:T(8,128)(2,1)S(1)}, bf16[128,1024]{1,0:T(8,128)(2,1)S(1)}, u32[]{:S(2)}, u32[]{:S(2)}) collective-permute-start(bf16[128,1024]{1,0:T(8,128)(2,1)S(1)} %combine.10.refs_0_), channel_id=1, source_target_pairs={{0,2},{1,3},{2,0},{3,1},{4,6},{5,7},{6,4},{7,5},{8,10},{9,11},{10,... | collective-permute-start | bytes 786440 | tf_op jit(solution)/shard_map/z2b/ppermute | solution.py:53
  27.3 2.8 %collective-permute-done.10.refs_1_.refs_2_ = bf16[128,1024]{1,0:T(8,128)(2,1)S(1)} collective-permute-done((bf16[128,1024]{1,0:T(8,128)(2,1)S(1)}, bf16[128,1024]{1,0:T(8,128)(2,1)S(1)}, u32[]{:S(2)}, u32[]{:S(2)}) %collective-permute-start.10) | collective-permute-done | bytes 262176 | tf_op jit(solution)/shard_map/z2a/ppermute | solution.py:53
  30.2 0.9 %collective-permute-done.12.received_ref = bf16[128,1024]{1,0:T(8,128)(2,1)S(1)} collective-permute-done((bf16[128,1024]{1,0:T(8,128)(2,1)S(1)}, bf16[128,1024]{1,0:T(8,128)(2,1)S(1)}, u32[]{:S(2)}, u32[]{:S(2)}) %collective-permute-start.12) | collective-permute-done | bytes 262176 | tf_op jit(solution)/shard_map/y1a/ppermute | solution.py:53
  31.2 1.6 %collective-permute-start.11 = (bf16[128,1024]{1,0:T(8,128)(2,1)S(1)}, bf16[128,1024]{1,0:T(8,128)(2,1)S(1)}, u32[]{:S(2)}, u32[]{:S(2)}) collective-permute-start(bf16[128,1024]{1,0:T(8,128)(2,1)S(1)} %get-tuple-element.34), channel_id=1, source_target_pairs={{0,16},{4,20},{8,24},{12,28},{16,0},{20,4},{24,8},{28,12},{1,17},{... | collective-permute-start | bytes 786440 | tf_op jit(solution)/shard_map/y1b/ppermute | solution.py:53
  33.2 3.5 %collective-permute-done.2.refs_1_ = bf16[1024,128]{1,0:T(8,128)(2,1)S(1)} collective-permute-done((bf16[1024,128]{1,0:T(8,128)(2,1)S(1)}, bf16[1024,128]{1,0:T(8,128)(2,1)S(1)}, u32[]{:S(2)}, u32[]{:S(2)}) %collective-permute-start.2) | collective-permute-done | bytes 262176 | tf_op jit(solution)/shard_map/gather4/ppermute | solution.py:53
  36.7 1.7 %collective-permute-start.16 = (bf16[128,1024]{1,0:T(8,128)(2,1)S(1)}, bf16[128,1024]{1,0:T(8,128)(2,1)S(1)}, u32[]{:S(2)}, u32[]{:S(2)}) collective-permute-start(bf16[128,1024]{1,0:T(8,128)(2,1)S(1)} %combine.11.refs_0_), channel_id=1, source_target_pairs={{0,3},{1,2},{2,1},{3,0},{4,7},{5,6},{6,5},{7,4},{8,11},{9,10},{10,... | collective-permute-start | bytes 786440 | tf_op jit(solution)/shard_map/z3a/ppermute | solution.py:53
  38.4 0.7 %collective-permute-start.21 = (bf16[128,1024]{1,0:T(8,128)(2,1)S(1)}, bf16[128,1024]{1,0:T(8,128)(2,1)S(1)}, u32[]{:S(2)}, u32[]{:S(2)}) collective-permute-start(bf16[128,1024]{1,0:T(8,128)(2,1)S(1)} %combine.12.refs_0_), channel_id=1, source_target_pairs={{0,1},{1,0},{2,3},{3,2},{4,5},{5,4},{6,7},{7,6},{8,9},{9,8},{10,11... | collective-permute-start | bytes 786440 | tf_op jit(solution)/shard_map/z1a/ppermute | solution.py:53
  39.1 2.3 %collective-permute-done.13.refs_2_.refs_3_ = bf16[128,1024]{1,0:T(8,128)(2,1)S(1)} collective-permute-done((bf16[128,1024]{1,0:T(8,128)(2,1)S(1)}, bf16[128,1024]{1,0:T(8,128)(2,1)S(1)}, u32[]{:S(2)}, u32[]{:S(2)}) %collective-permute-start.13) | collective-permute-done | bytes 262176 | tf_op jit(solution)/shard_map/z2b/ppermute | solution.py:53
  41.4 1.5 %collective-permute-start.4 = (bf16[1024,128]{1,0:T(8,128)(2,1)S(1)}, bf16[1024,128]{1,0:T(8,128)(2,1)S(1)}, u32[]{:S(2)}, u32[]{:S(2)}) collective-permute-start(bf16[1024,128]{1,0:T(8,128)(2,1)S(1)} %collective-permute-done.2.refs_1_), channel_id=1, source_target_pairs={{0,8},{4,12},{8,0},{12,4},{16,24},{20,28},{24,16},{28,20},{1,9},{5... | collective-permute-start | bytes 786440 | tf_op jit(solution)/shard_map/gather2/ppermute | solution.py:53
  43.0 2.8 %collective-permute-done.15.received_ref = bf16[128,1024]{1,0:T(8,128)(2,1)S(1)} collective-permute-done((bf16[128,1024]{1,0:T(8,128)(2,1)S(1)}, bf16[128,1024]{1,0:T(8,128)(2,1)S(1)}, u32[]{:S(2)}, u32[]{:S(2)}) %collective-permute-start.15) | collective-permute-done | bytes 262176 | tf_op jit(solution)/shard_map/y3b/ppermute | solution.py:53
  45.9 4.1 %collective-permute-start.19 = (bf16[128,1024]{1,0:T(8,128)(2,1)S(1)}, bf16[128,1024]{1,0:T(8,128)(2,1)S(1)}, u32[]{:S(2)}, u32[]{:S(2)}) collective-permute-start(bf16[128,1024]{1,0:T(8,128)(2,1)S(1)} %combine.14.refs_0_), channel_id=1, source_target_pairs={{0,3},{1,2},{2,1},{3,0},{4,7},{5,6},{6,5},{7,4},{8,11},{9,10},{10,... | collective-permute-start | bytes 786440 | tf_op jit(solution)/shard_map/z3b/ppermute | solution.py:53
  50.0 1.5 %collective-permute-start.14 = (bf16[128,1024]{1,0:T(8,128)(2,1)S(1)}, bf16[128,1024]{1,0:T(8,128)(2,1)S(1)}, u32[]{:S(2)}, u32[]{:S(2)}) collective-permute-start(bf16[128,1024]{1,0:T(8,128)(2,1)S(1)} %get-tuple-element.37), channel_id=1, source_target_pairs={{0,16},{4,20},{8,24},{12,28},{16,0},{20,4},{24,8},{28,12},{1,17},{... | collective-permute-start | bytes 786440 | tf_op jit(solution)/shard_map/y0a/ppermute | solution.py:53
  51.5 0.8 %restrict.1 = (bf16[32,512]{1,0:T(8,128)(2,1)S(1)}, bf16[32,512]{1,0:T(8,128)(2,1)S(1)}) custom-call(s32[2,32]{1,0:T(2,128)S(1)} %bitcast.5, bf16[32,1024]{1,0:T(8,128)(2,1)S(1)} %copy-done.1, bf16[1024,128]{1,0:T(8,128)(2,1)S(1)} %copy-done, bf16[128,1024]{1,0:T(8,128)(2,1)S(1)} %combine.13.refs_0_), custom_call_target="tpu_custom_call" | custom-call | flops 1000 | bytes 1 | tf_op jit(solution)/shard_map/restrict/pallas_call | solution.py:297
  52.3 0.6 collective-permute-start.18
  52.9 4.8 %collective-permute-done.18.refs_3_.received_ref = bf16[32,512]{1,0:T(8,128)(2,1)S(1)} collective-permute-done((bf16[32,512]{1,0:T(8,128)(2,1)S(1)}, bf16[32,512]{1,0:T(8,128)(2,1)S(1)}, u32[]{:S(2)}, u32[]{:S(2)}) %collective-permute-start.18) | collective-permute-done | bytes 32800 | tf_op jit(solution)/shard_map/vectors/ppermute | solution.py:53
  57.7 1.5 %collective-permute-start.20 = (bf16[128,1024]{1,0:T(8,128)(2,1)S(1)}, bf16[128,1024]{1,0:T(8,128)(2,1)S(1)}, u32[]{:S(2)}, u32[]{:S(2)}) collective-permute-start(bf16[128,1024]{1,0:T(8,128)(2,1)S(1)} %get-tuple-element.42), channel_id=1, source_target_pairs={{0,16},{4,20},{8,24},{12,28},{16,0},{20,4},{24,8},{28,12},{1,17},{... | collective-permute-start | bytes 786440 | tf_op jit(solution)/shard_map/y0b/ppermute | solution.py:53
  59.7 1.5 %collective-permute-done.17.refs_2_.refs_5_ = bf16[128,1024]{1,0:T(8,128)(2,1)S(1)} collective-permute-done((bf16[128,1024]{1,0:T(8,128)(2,1)S(1)}, bf16[128,1024]{1,0:T(8,128)(2,1)S(1)}, u32[]{:S(2)}, u32[]{:S(2)}) %collective-permute-start.17) | collective-permute-done | bytes 262176 | tf_op jit(solution)/shard_map/z1b/ppermute | solution.py:53
  61.3 2.8 %collective-permute-done.20.received_ref = bf16[128,1024]{1,0:T(8,128)(2,1)S(1)} collective-permute-done((bf16[128,1024]{1,0:T(8,128)(2,1)S(1)}, bf16[128,1024]{1,0:T(8,128)(2,1)S(1)}, u32[]{:S(2)}, u32[]{:S(2)}) %collective-permute-start.20) | collective-permute-done | bytes 262176 | tf_op jit(solution)/shard_map/y0b/ppermute | solution.py:53
  64.2 2.3 %assemble.1.interp_ref = bf16[8192,128]{1,0:T(8,128)(2,1)S(1)} custom-call(s32[2,32]{1,0:T(2,128)} %bitcast.4, bf16[1024,128]{1,0:T(8,128)(2,1)S(1)} %copy-done, bf16[1024,128]{1,0:T(8,128)(2,1)S(1)} %collective-permute-done.2.refs_1_, bf16[1024,128]{1,0:T(8,128)(2,1)S(1)} %collective-permute-done.3.refs_2_.refs_3_, ...), custom_call_target="tpu_custom_call" | custom-call | flops 100000000 | bytes 100000 | tf_op jit(solution)/shard_map/assemble/pallas_call | solution.py:192
  66.5 0.6 combine.17
  67.1 1.4 %finish.1 = bf16[128,4096]{1,0:T(8,128)(2,1)} custom-call(bf16[8192,128]{1,0:T(8,128)(2,1)S(1)} %assemble.1.interp_ref, bf16[128,1024]{1,0:T(8,128)(2,1)S(1)} %combine.15.refs_0_, bf16[128,1024]{1,0:T(8,128)(2,1)S(1)} %combine.16.refs_1_.refs_0_, bf16[128,1024]{1,0:T(8,128)(2,1)S(1)} %collective-permute-done.10.refs_1_.refs_2_, ...), custom_call_target="tpu_custom_call" | custom-call | flops 1000 | bytes 1 | tf_op jit(solution)/shard_map/finish/pallas_call | solution.py:263
  (33 shorter events, 1.7 us)
Async XLA Ops:
  2.8 10.2 %collective-permute-start.1 = (bf16[128,1024]{1,0:T(8,128)(2,1)S(1)}, bf16[128,1024]{1,0:T(8,128)(2,1)S(1)}, u32[]{:S(2)}, u32[]{:S(2)}) collective-permute-start(bf16[128,1024]{1,0:T(8,128)(2,1)S(1)} %get-tuple-element.23.refs_0_), channel_id=1, source_target_pairs={{0,16},{4,20},{8,24},{12,28},{16,0},{20,4},{24,8},{28,12},{1,17},{... | collective-permute-start | bytes 786440 | tf_op jit(solution)/shard_map/y2a/ppermute | solution.py:53
  5.8 12.8 %collective-permute-start = (bf16[128,1024]{1,0:T(8,128)(2,1)S(1)}, bf16[128,1024]{1,0:T(8,128)(2,1)S(1)}, u32[]{:S(2)}, u32[]{:S(2)}) collective-permute-start(bf16[128,1024]{1,0:T(8,128)(2,1)S(1)} %get-tuple-element.26), channel_id=1, source_target_pairs={{0,16},{4,20},{8,24},{12,28},{16,0},{20,4},{24,8},{28,12},{1,17},{... | collective-permute-start | bytes 786440 | tf_op jit(solution)/shard_map/y2b/ppermute | solution.py:53
  8.8 11.8 %copy-start = (bf16[1024,128]{1,0:T(8,128)(2,1)S(1)}, bf16[1024,128]{1,0:T(8,128)(2,1)}, u32[]{:S(2)}) copy-start(bf16[1024,128]{1,0:T(8,128)(2,1)} %interp_ref.7) | copy-start | bytes 786436
  13.0 17.1 %collective-permute-start.10 = (bf16[128,1024]{1,0:T(8,128)(2,1)S(1)}, bf16[128,1024]{1,0:T(8,128)(2,1)S(1)}, u32[]{:S(2)}, u32[]{:S(2)}) collective-permute-start(bf16[128,1024]{1,0:T(8,128)(2,1)S(1)} %combine.9.refs_0_), channel_id=1, source_target_pairs={{0,2},{1,3},{2,0},{3,1},{4,6},{5,7},{6,4},{7,5},{8,10},{9,11},{10,... | collective-permute-start | bytes 786440 | tf_op jit(solution)/shard_map/z2a/ppermute | solution.py:53
  16.2 9.2 %collective-permute-start.9 = (bf16[128,1024]{1,0:T(8,128)(2,1)S(1)}, bf16[128,1024]{1,0:T(8,128)(2,1)S(1)}, u32[]{:S(2)}, u32[]{:S(2)}) collective-permute-start(bf16[128,1024]{1,0:T(8,128)(2,1)S(1)} %get-tuple-element.33.refs_0_), channel_id=1, source_target_pairs={{0,16},{4,20},{8,24},{12,28},{16,0},{20,4},{24,8},{28,12},{1,17},{... | collective-permute-start | bytes 786440 | tf_op jit(solution)/shard_map/y3a/ppermute | solution.py:53
  18.6 12.5 %collective-permute-start.12 = (bf16[128,1024]{1,0:T(8,128)(2,1)S(1)}, bf16[128,1024]{1,0:T(8,128)(2,1)S(1)}, u32[]{:S(2)}, u32[]{:S(2)}) collective-permute-start(bf16[128,1024]{1,0:T(8,128)(2,1)S(1)} %get-tuple-element.36), channel_id=1, source_target_pairs={{0,16},{4,20},{8,24},{12,28},{16,0},{20,4},{24,8},{28,12},{1,17},{... | collective-permute-start | bytes 786440 | tf_op jit(solution)/shard_map/y1a/ppermute | solution.py:53
  20.6 16.1 %collective-permute-start.2 = (bf16[1024,128]{1,0:T(8,128)(2,1)S(1)}, bf16[1024,128]{1,0:T(8,128)(2,1)S(1)}, u32[]{:S(2)}, u32[]{:S(2)}) collective-permute-start(bf16[1024,128]{1,0:T(8,128)(2,1)S(1)} %copy-done), channel_id=1, source_target_pairs={{0,16},{4,20},{8,24},{12,28},{16,0},{20,4},{24,8},{28,12},{1,17},{... | collective-permute-start | bytes 786440 | tf_op jit(solution)/shard_map/gather4/ppermute | solution.py:53
  20.7 17.7 %collective-permute-start.3 = (bf16[1024,128]{1,0:T(8,128)(2,1)S(1)}, bf16[1024,128]{1,0:T(8,128)(2,1)S(1)}, u32[]{:S(2)}, u32[]{:S(2)}) collective-permute-start(bf16[1024,128]{1,0:T(8,128)(2,1)S(1)} %copy-done), channel_id=1, source_target_pairs={{0,8},{4,12},{8,0},{12,4},{16,24},{20,28},{24,16},{28,20},{1,9},{5... | collective-permute-start | bytes 786440 | tf_op jit(solution)/shard_map/gather2/ppermute | solution.py:53
  25.5 15.9 %collective-permute-start.13 = (bf16[128,1024]{1,0:T(8,128)(2,1)S(1)}, bf16[128,1024]{1,0:T(8,128)(2,1)S(1)}, u32[]{:S(2)}, u32[]{:S(2)}) collective-permute-start(bf16[128,1024]{1,0:T(8,128)(2,1)S(1)} %combine.10.refs_0_), channel_id=1, source_target_pairs={{0,2},{1,3},{2,0},{3,1},{4,6},{5,7},{6,4},{7,5},{8,10},{9,11},{10,... | collective-permute-start | bytes 786440 | tf_op jit(solution)/shard_map/z2b/ppermute | solution.py:53
  30.1 21.4 %copy-start.1 = (bf16[32,1024]{1,0:T(8,128)(2,1)S(1)}, bf16[32,1024]{1,0:T(8,128)(2,1)}, u32[]{:S(2)}) copy-start(bf16[32,1024]{1,0:T(8,128)(2,1)} %vec_ref.1) | copy-start | bytes 196612
  30.1 21.4 %copy-start.2 = (s32[32,2]{0,1:T(2,128)S(1)}, s32[32,2]{0,1:T(2,128)}, u32[]{:S(2)}) copy-start(s32[32,2]{0,1:T(2,128)} %param.7) | copy-start | bytes 772
  31.2 11.8 %collective-permute-start.11 = (bf16[128,1024]{1,0:T(8,128)(2,1)S(1)}, bf16[128,1024]{1,0:T(8,128)(2,1)S(1)}, u32[]{:S(2)}, u32[]{:S(2)}) collective-permute-start(bf16[128,1024]{1,0:T(8,128)(2,1)S(1)} %get-tuple-element.34), channel_id=1, source_target_pairs={{0,16},{4,20},{8,24},{12,28},{16,0},{20,4},{24,8},{28,12},{1,17},{... | collective-permute-start | bytes 786440 | tf_op jit(solution)/shard_map/y1b/ppermute | solution.py:53
  32.7 13.1 %collective-permute-start.15 = (bf16[128,1024]{1,0:T(8,128)(2,1)S(1)}, bf16[128,1024]{1,0:T(8,128)(2,1)S(1)}, u32[]{:S(2)}, u32[]{:S(2)}) collective-permute-start(bf16[128,1024]{1,0:T(8,128)(2,1)S(1)} %get-tuple-element.39), channel_id=1, source_target_pairs={{0,16},{4,20},{8,24},{12,28},{16,0},{20,4},{24,8},{28,12},{1,17},{... | collective-permute-start | bytes 786440 | tf_op jit(solution)/shard_map/y3b/ppermute | solution.py:53
  36.7 14.8 %collective-permute-start.16 = (bf16[128,1024]{1,0:T(8,128)(2,1)S(1)}, bf16[128,1024]{1,0:T(8,128)(2,1)S(1)}, u32[]{:S(2)}, u32[]{:S(2)}) collective-permute-start(bf16[128,1024]{1,0:T(8,128)(2,1)S(1)} %combine.11.refs_0_), channel_id=1, source_target_pairs={{0,3},{1,2},{2,1},{3,0},{4,7},{5,6},{6,5},{7,4},{8,11},{9,10},{10,... | collective-permute-start | bytes 786440 | tf_op jit(solution)/shard_map/z3a/ppermute | solution.py:53
  38.4 13.9 %collective-permute-start.21 = (bf16[128,1024]{1,0:T(8,128)(2,1)S(1)}, bf16[128,1024]{1,0:T(8,128)(2,1)S(1)}, u32[]{:S(2)}, u32[]{:S(2)}) collective-permute-start(bf16[128,1024]{1,0:T(8,128)(2,1)S(1)} %combine.12.refs_0_), channel_id=1, source_target_pairs={{0,1},{1,0},{2,3},{3,2},{4,5},{5,4},{6,7},{7,6},{8,9},{9,8},{10,11... | collective-permute-start | bytes 786440 | tf_op jit(solution)/shard_map/z1a/ppermute | solution.py:53
  41.4 11.5 %collective-permute-start.4 = (bf16[1024,128]{1,0:T(8,128)(2,1)S(1)}, bf16[1024,128]{1,0:T(8,128)(2,1)S(1)}, u32[]{:S(2)}, u32[]{:S(2)}) collective-permute-start(bf16[1024,128]{1,0:T(8,128)(2,1)S(1)} %collective-permute-done.2.refs_1_), channel_id=1, source_target_pairs={{0,8},{4,12},{8,0},{12,4},{16,24},{20,28},{24,16},{28,20},{1,9},{5... | collective-permute-start | bytes 786440 | tf_op jit(solution)/shard_map/gather2/ppermute | solution.py:53
  45.9 13.3 %collective-permute-start.19 = (bf16[128,1024]{1,0:T(8,128)(2,1)S(1)}, bf16[128,1024]{1,0:T(8,128)(2,1)S(1)}, u32[]{:S(2)}, u32[]{:S(2)}) collective-permute-start(bf16[128,1024]{1,0:T(8,128)(2,1)S(1)} %combine.14.refs_0_), channel_id=1, source_target_pairs={{0,3},{1,2},{2,1},{3,0},{4,7},{5,6},{6,5},{7,4},{8,11},{9,10},{10,... | collective-permute-start | bytes 786440 | tf_op jit(solution)/shard_map/z3b/ppermute | solution.py:53
  50.0 9.2 %collective-permute-start.14 = (bf16[128,1024]{1,0:T(8,128)(2,1)S(1)}, bf16[128,1024]{1,0:T(8,128)(2,1)S(1)}, u32[]{:S(2)}, u32[]{:S(2)}) collective-permute-start(bf16[128,1024]{1,0:T(8,128)(2,1)S(1)} %get-tuple-element.37), channel_id=1, source_target_pairs={{0,16},{4,20},{8,24},{12,28},{16,0},{20,4},{24,8},{28,12},{1,17},{... | collective-permute-start | bytes 786440 | tf_op jit(solution)/shard_map/y0a/ppermute | solution.py:53
  51.5 9.7 %collective-permute-start.17 = (bf16[128,1024]{1,0:T(8,128)(2,1)S(1)}, bf16[128,1024]{1,0:T(8,128)(2,1)S(1)}, u32[]{:S(2)}, u32[]{:S(2)}) collective-permute-start(bf16[128,1024]{1,0:T(8,128)(2,1)S(1)} %combine.13.refs_0_), channel_id=1, source_target_pairs={{0,1},{1,0},{2,3},{3,2},{4,5},{5,4},{6,7},{7,6},{8,9},{9,8},{10,11... | collective-permute-start | bytes 786440 | tf_op jit(solution)/shard_map/z1b/ppermute | solution.py:53
  52.3 5.4 %collective-permute-start.18 = (bf16[32,512]{1,0:T(8,128)(2,1)S(1)}, bf16[32,512]{1,0:T(8,128)(2,1)S(1)}, u32[]{:S(2)}, u32[]{:S(2)}) collective-permute-start(bf16[32,512]{1,0:T(8,128)(2,1)S(1)} %get-tuple-element.40), channel_id=1, source_target_pairs={{0,16},{4,20},{8,24},{12,28},{16,0},{20,4},{24,8},{28,12},{1,17},{... | collective-permute-start | bytes 98312 | tf_op jit(solution)/shard_map/vectors/ppermute | solution.py:53
  52.9 11.3 %collective-permute-start.5 = (bf16[1024,128]{1,0:T(8,128)(2,1)S(1)}, bf16[1024,128]{1,0:T(8,128)(2,1)S(1)}, u32[]{:S(2)}, u32[]{:S(2)}) collective-permute-start(bf16[1024,128]{1,0:T(8,128)(2,1)S(1)} %copy-done), channel_id=1, source_target_pairs={{0,4},{4,0},{8,12},{12,8},{16,20},{20,16},{24,28},{28,24},{1,5},{5... | collective-permute-start | bytes 786440 | tf_op jit(solution)/shard_map/gather1/ppermute | solution.py:53
  57.7 6.4 %collective-permute-start.20 = (bf16[128,1024]{1,0:T(8,128)(2,1)S(1)}, bf16[128,1024]{1,0:T(8,128)(2,1)S(1)}, u32[]{:S(2)}, u32[]{:S(2)}) collective-permute-start(bf16[128,1024]{1,0:T(8,128)(2,1)S(1)} %get-tuple-element.42), channel_id=1, source_target_pairs={{0,16},{4,20},{8,24},{12,28},{16,0},{20,4},{24,8},{28,12},{1,17},{... | collective-permute-start | bytes 786440 | tf_op jit(solution)/shard_map/y0b/ppermute | solution.py:53
  59.2 4.9 %collective-permute-start.6 = (bf16[1024,128]{1,0:T(8,128)(2,1)S(1)}, bf16[1024,128]{1,0:T(8,128)(2,1)S(1)}, u32[]{:S(2)}, u32[]{:S(2)}) collective-permute-start(bf16[1024,128]{1,0:T(8,128)(2,1)S(1)} %collective-permute-done.2.refs_1_), channel_id=1, source_target_pairs={{0,4},{4,0},{8,12},{12,8},{16,20},{20,16},{24,28},{28,24},{1,5},{5... | collective-permute-start | bytes 786440 | tf_op jit(solution)/shard_map/gather1/ppermute | solution.py:53
  59.2 4.9 %collective-permute-start.7 = (bf16[1024,128]{1,0:T(8,128)(2,1)S(1)}, bf16[1024,128]{1,0:T(8,128)(2,1)S(1)}, u32[]{:S(2)}, u32[]{:S(2)}) collective-permute-start(bf16[1024,128]{1,0:T(8,128)(2,1)S(1)} %collective-permute-done.3.refs_2_.refs_3_), channel_id=1, source_target_pairs={{0,4},{4,0},{8,12},{12,8},{16,20},{20,16},{24,28},{28,24},{1,5},{5... | collective-permute-start | bytes 786440 | tf_op jit(solution)/shard_map/gather1/ppermute | solution.py:53
  61.3 2.9 %collective-permute-start.8 = (bf16[1024,128]{1,0:T(8,128)(2,1)S(1)}, bf16[1024,128]{1,0:T(8,128)(2,1)S(1)}, u32[]{:S(2)}, u32[]{:S(2)}) collective-permute-start(bf16[1024,128]{1,0:T(8,128)(2,1)S(1)} %collective-permute-done.4.refs_3_.refs_1_), channel_id=1, source_target_pairs={{0,4},{4,0},{8,12},{12,8},{16,20},{20,16},{24,28},{28,24},{1,5},{5... | collective-permute-start | bytes 786440 | tf_op jit(solution)/shard_map/gather1/ppermute | solution.py:53

commit v4 on v3

--- a/solution.py
+++ b/solution.py
@@ -8,20 +8,14 @@
 
 YAFTER = {'3a': ['2a'], '1a': ['2b'], '1b': ['3a'], '3b': ['1a'], '0a': ['1b'], '0b': ['3b']}
 HEAD = 1
+CORE_PARTS = 4
 GATHER = '2b'
 VECTORS = '1b'
-VECTORS_AT = ''
 ZAFTER = {}
 FINISH = 1000
-JOBS = 2
-ASSEMBLE_Y = ''
-VECTORS_Y = ''
 PFLOPS = (1000, 1000)
 CFLOPS = 1000
-ASSEMBLE_AT = ''
-VECFLOPS = 1000
-VECDEP = -1
-ASSEMBLE = 100000000
+ASSEMBLE = 1000
 WAITS = {'3a': ['z2a'], '1b': ['g1', 'z2b', 'g2'], '0a': ['z3a', 'z1b', 'v', 'z3b'], '0b': ['g3', 'z1a']}
 
 
@@ -152,7 +146,7 @@
 
 def gather_blocks(block, axis):
     blocks, flip = [block], lax.axis_size(axis) // 2
-    while flip:
+    while flip > 1:
         blocks += [exchange(part, axis, flip, f"gather{flip}") for part in blocks]
         flip //= 2
     return blocks
@@ -161,10 +155,10 @@
 def assemble(blocks, pairs, fine_cols, *earlier):
     rows, tile = blocks[0].shape
     fine_rows, row_count = rows // tile, lax.axis_size("row")
-    coarse_cols, half = fine_cols // 2, lax.axis_size("col") // 2
+    coarse_rows, coarse_cols, half = fine_rows // 2, fine_cols // 2, lax.axis_size("col") // 2
 
     def body(pairs_ref, *refs):
-        out_ref, buf, fetch = refs[-3:]
+        out_refs, (buf, fetch) = refs[-2 - CORE_PARTS : -2], refs[-2:]
         row, col = lax.axis_index("row"), lax.axis_index("col")
         fetches = [
             pltpu.make_async_copy(ref, buf.at[pl.ds(k * rows, rows), :], fetch.at[k])
@@ -174,27 +168,34 @@
             copy.start()
         for copy in fetches:
             copy.wait()
-        upper = col // half
+        upper, slot = col // half, 0
         for step in range(half):
-            for p in range(fine_cols):
-                group = p // coarse_cols * half + (col ^ step) % half
-                d = group * coarse_cols + p % coarse_cols
-                for which, j in enumerate((pairs_ref[upper, d], pairs_ref[1 - upper, d])):
-                    source = (j // fine_rows) ^ row
-                    place, bit = 0, row_count // 2
-                    while bit:
-                        place = place * 2 + source % 2
-                        source, bit = source // 2, bit // 2
-                    at = pl.multiple_of((place * fine_rows + j % fine_rows) * tile, tile)
-                    begin = ((step * fine_cols + p) * 2 + which) * tile
-                    out_ref[begin : begin + tile, :] = buf[pl.ds(at, tile), :]
-
-    return pl.pallas_call(
-        body,
-        out_shape=jax.ShapeDtypeStruct((len(blocks) * rows, tile), blocks[0].dtype),
+            for part in range(2):
+                group = part * half + (col ^ step) % half
+                for first in range(0, coarse_cols, 2 * coarse_rows):
+                    for k in range(coarse_rows):
+                        d = group * coarse_cols + first + row % 2 * coarse_rows + k
+                        for j in (pairs_ref[upper, d], pairs_ref[1 - upper, d]):
+                            source = ((j // fine_rows) ^ row) // 2
+                            place, bit = 0, row_count // 4
+                            while bit:
+                                place = place * 2 + source % 2
+                                source, bit = source // 2, bit // 2
+                            at = (place * fine_rows + j % fine_rows) * tile
+                            out_ref, begin = out_refs[slot // length], slot % length * tile
+                            out_ref[begin : begin + tile, :] = buf[
+                                pl.ds(pl.multiple_of(at, tile), tile), :
+                            ]
+                            slot += 1
+
+    length = half * coarse_cols * 2 // CORE_PARTS
+
+    return pl.pallas_call(
+        body,
+        out_shape=[jax.ShapeDtypeStruct((length * tile, tile), blocks[0].dtype)] * CORE_PARTS,
         in_specs=[pl.BlockSpec(memory_space=pltpu.SMEM)]
         + [pl.BlockSpec(memory_space=pl.ANY)] * (len(blocks) + len(earlier)),
-        out_specs=pl.BlockSpec(memory_space=pltpu.VMEM),
+        out_specs=[pl.BlockSpec(memory_space=pltpu.VMEM)] * CORE_PARTS,
         scratch_shapes=[
             pltpu.VMEM((len(blocks) * rows, tile), blocks[0].dtype),
             pltpu.SemaphoreType.DMA((len(blocks),)),
@@ -207,13 +208,13 @@
     )(in_hbm(pairs), *blocks, *earlier)
 
 
-def finish(jobs, paired_interp, before, fine_cols, *earlier):
-    tile = paired_interp.shape[1]
+def finish(jobs, paired, other_paired, own_vec, far_vec, fine_cols, fine_rows):
+    part_rows, tile = paired[0].shape
     count = jobs[0][0][0].shape[0]
     half = lax.axis_size("col") // 2
-    coarse_cols = fine_cols // 2
+    coarse_rows, coarse_cols = fine_rows // 2, fine_cols // 2
     width = coarse_cols * tile
-    total = paired_interp.shape[0] // 2
+    total = lax.axis_size("row") * fine_rows * tile // 2
     pieces = [part for near, far, _ in jobs for part in (*near, *far)]
 
     def tile_of(refs, p):
@@ -223,10 +224,14 @@
                 return ref[:, begin : begin + tile]
             begin -= ref.shape[1]
 
-    def body(interp_ref, *refs):
-        out_ref, buf, sem = refs[-3:]
-        col = lax.axis_index("col")
-        copies, taken = [], 0
+    def body(own_ref, far_ref, *refs):
+        paired_refs, other_refs, refs = refs[:CORE_PARTS], refs[CORE_PARTS : 2 * CORE_PARTS], refs[2 * CORE_PARTS :]
+        out_ref, vec_ref, buf, vec_buf, sem = refs[-5:]
+        row, col = lax.axis_index("row"), lax.axis_index("col")
+        vec = own_ref[...].astype(jnp.float32) + far_ref[...].astype(jnp.float32)
+        vec_buf[...] = vec.astype(vec_buf.dtype)
+        copies, taken, slot = [pltpu.make_async_copy(vec_buf, vec_ref, sem.at[0])], 0, 0
+        copies[0].start()
         for n, (near, far, step) in enumerate(jobs):
             near_refs = refs[taken : taken + len(near)]
             far_refs = refs[taken + len(near) : taken + len(near) + len(far)]
@@ -235,41 +240,43 @@
                 for k in range(coarse_cols):
                     p = part * coarse_cols + k
                     left = jnp.concatenate([tile_of(near_refs, p), tile_of(far_refs, p)], axis=1)
-                    at = (step * fine_cols + p) * 2 * tile
-                    result = jnp.dot(
-                        left, interp_ref[at : at + 2 * tile, :], preferred_element_type=jnp.float32
+                    place = k // (2 * coarse_rows) * coarse_rows + k % coarse_rows
+                    at = (slot + place) * 2 * tile
+                    which, at = at // part_rows, at % part_rows
+                    right = jnp.where(
+                        row % 2 == k // coarse_rows % 2,
+                        paired_refs[which][at : at + 2 * tile, :],
+                        other_refs[which][at : at + 2 * tile, :],
                     )
+                    result = jnp.dot(left, right, preferred_element_type=jnp.float32)
                     buf[2 * n + part, :, k * tile : (k + 1) * tile] = result.astype(buf.dtype)
+                slot += coarse_cols // 2
                 group = part * half + (col ^ step) % half
                 copy = pltpu.make_async_copy(
                     buf.at[2 * n + part],
                     out_ref.at[:, pl.ds(pl.multiple_of(group * width, width), width)],
-                    sem.at[2 * n + part],
+                    sem.at[1 + 2 * n + part],
                 )
                 copy.start()
                 copies.append(copy)
         for copy in copies:
             copy.wait()
 
-    operands = [paired_interp, *pieces]
-    in_specs = [pl.BlockSpec(memory_space=pltpu.VMEM)] * len(operands)
-    aliases = {}
-    if before is not None:
-        aliases = {len(operands): 0}
-        operands.append(before)
-    operands += earlier
-    in_specs += [pl.BlockSpec(memory_space=pl.ANY)] * (len(operands) - len(in_specs))
-    size = paired_interp.size * 2 + 2 * len(jobs) * count * (fine_cols * tile + width) * 2
-    return pl.pallas_call(
-        body,
-        out_shape=jax.ShapeDtypeStruct((count, total), jnp.bfloat16),
-        in_specs=in_specs,
-        out_specs=pl.BlockSpec(memory_space=pl.ANY),
+    operands = [own_vec, far_vec, *paired, *other_paired, *pieces]
+    size = CORE_PARTS * paired[0].size * 4 + 2 * len(jobs) * count * (fine_cols * tile + width) * 2
+    return pl.pallas_call(
+        body,
+        out_shape=(
+            jax.ShapeDtypeStruct((count, total), jnp.bfloat16),
+            jax.ShapeDtypeStruct(own_vec.shape, jnp.bfloat16),
+        ),
+        in_specs=[pl.BlockSpec(memory_space=pltpu.VMEM)] * len(operands),
+        out_specs=(pl.BlockSpec(memory_space=pl.ANY),) * 2,
         scratch_shapes=[
             pltpu.VMEM((2 * len(jobs), count, width), jnp.bfloat16),
-            pltpu.SemaphoreType.DMA((2 * len(jobs),)),
+            pltpu.VMEM(own_vec.shape, jnp.bfloat16),
+            pltpu.SemaphoreType.DMA((1 + 2 * len(jobs),)),
         ],
-        input_output_aliases=aliases,
         cost_estimate=estimate(FINISH),
         compiler_params=pltpu.CompilerParams(vmem_limit_bytes=size + 4 * 1024 * 1024),
         name="finish",
@@ -342,26 +349,14 @@
     )
     kept = dict(zip(steps, kept))
     named, totals, held = {}, [kept[0]], {step: [] for step in steps}
-    interp_blocks = keep = None
+    paired = keep = None
     for k, (step, lo, hi) in enumerate(order):
         name, span = labels[k], (lo * cols // 16, hi * cols // 16)
         block = sent[step, span]
         if name in YAFTER:
             block = after(block, *(named["t" + w] for w in YAFTER[name] if "t" + w in named))
-        if name == ASSEMBLE_Y:
-            paired_interp = assemble(interp_blocks, pairs, fine_cols)
-            block = after(block, paired_interp)
-        if name == VECTORS_Y:
-            coarse_vectors = combine(keep, 0, far_vec, totals[-1])
-            block = after(block, coarse_vectors)
         block = exchange(block, "row", row_half, "y" + name)
         waits = totals[-1:] + [named[w] for w in WAITS.get(name, ()) if w in named]
-        if name == ASSEMBLE_AT:
-            paired_interp = assemble(interp_blocks, pairs, fine_cols, *totals[-1:])
-            waits.append(paired_interp)
-        if name == VECTORS_AT:
-            coarse_vectors = combine(keep, 0, far_vec, totals[-1])
-            waits.append(in_hbm(coarse_vectors))
         total = combine(kept[step], span[0], block, *waits, flops=CFLOPS)
         totals.append(total)
         named["t" + name] = total
@@ -370,22 +365,19 @@
             total = exchange(after(total, *later) if later else total, "col", step, "z" + name)
         named["z" + name] = total
         held[step].append(total)
-        if name == GATHER or (k + 1 == len(order) and interp_blocks is None):
-            interp_blocks = gather_blocks(after(interp, totals[-1]), "row")
-            for place, value in enumerate(interp_blocks):
+        if name == GATHER or (k + 1 == len(order) and paired is None):
+            blocks = gather_blocks(after(interp, totals[-1]), "row")
+            for place, value in enumerate(blocks):
                 named[f"g{place}"] = value
+            paired = assemble(blocks, pairs, fine_cols)
+            other_paired = [exchange(part, "row", 1, "core") for part in paired]
+            for place, value in enumerate(other_paired):
+                named[f"p{place}"] = value
         if name == VECTORS or (k + 1 == len(order) and keep is None):
             keep, send = restrict(vectors, interp, pairs, totals[-1])
             named["v"] = far_vec = exchange(send, "row", row_half, "vectors")
-    if VECTORS_AT not in labels and VECTORS_Y not in labels:
-        coarse_vectors = combine(keep, 0, far_vec, totals[VECDEP], flops=VECFLOPS)
-    coarse = None
-    if ASSEMBLE_AT not in labels and ASSEMBLE_Y not in labels:
-        paired_interp = assemble(interp_blocks, pairs, fine_cols)
     jobs = [(held[step], held[step ^ col_half], step) for step in range(col_half)]
-    for k in range(0, len(jobs), JOBS):
-        coarse = finish(jobs[k : k + JOBS], paired_interp, coarse, fine_cols)
-    return (coarse, coarse_vectors)
+    return finish(jobs, paired, other_paired, keep, far_vec, fine_cols, fine_rows)
 
 
 def solution(mesh):

time: 68.8 us -> 66.9 us (0.972)
  waiting for transfers between devices: 25.9 us -> 22 us
  starting transfers between devices: 27.9 us -> 31.2 us
  Pallas kernels: 14 us -> 12.7 us
    ppermute x22, waiting for transfers between devices: 25.9 us -> 22 us  [exchange(): return lax.ppermute(block, axis, [(i, i ^ flip) for i in range(count)])]
    ppermute x22, starting transfers between devices: 27.9 us -> 31.2 us  [exchange(): return lax.ppermute(block, axis, [(i, i ^ flip) for i in range(count)])]
  transfers between devices with their start and end apart: 22 -> 22, of which waited for: 11 -> 11; matrix products, arithmetic and copies ran while one was open for 0% -> 0% of each run, Pallas kernels for 11% -> 13%
where the time goes in v4:
time: 66.9 us; the launch traced here: 66.7 us
  starting transfers between devices  31.2 us (47%)
  waiting for transfers between devices  22 us (33%)
  Pallas kernels  12.7 us (19%)
  between operations  0.77 us (1%)
    ppermute x22, starting transfers between devices, exchange(): return lax.ppermute(block, axis, [(i, i ^ flip) for i in range(count)])  31.2 us
    ppermute x22, waiting for transfers between devices, exchange(): return lax.ppermute(block, axis, [(i, i ^ flip) for i in range(count)])  22 us
    pallas_call x3, Pallas kernels, project(): pl.pallas_call(body, out_shape=outs, in_specs=[pl.BlockSpec(memory_space=...  8.37 us
    pallas_call x1, Pallas kernels, finish(): pl.pallas_call(body, out_shape=(jax.ShapeDtypeStruct((count, total), jnp....  1.63 us
    pallas_call x1, Pallas kernels, assemble(): pl.pallas_call(body, out_shape=[jax.ShapeDtypeStruct((length * tile, tile...  1.49 us
  transfers between devices with their start and end apart: 22, of which 11 were waited for; matrix products, arithmetic and copies ran while one was open for 0% of the time, Pallas kernels for 13%

profile of v4, /device:TPU:0, one launch (start us, length us, event | category | flops | bytes accessed | tf_op | source)
XLA Modules:
  0.0 66.7 jit_solution(8097122488827294471)
XLA Ops:
  0.6 2.2 %project.3 = (bf16[128,1024]{1,0:T(8,128)(2,1)S(1)}, bf16[128,1024]{1,0:T(8,128)(2,1)S(1)}) custom-call(s32[2,32]{1,0:T(2,128)} %bitcast.1, bf16[1024,128]{1,0:T(8,128)(2,1)} %refs_0_, bf16[1024,2048]{1,0:T(8,128)(2,1)} %lap_ref.5), custom_call_target="tpu_custom_call" | custom-call | flops 1000 | bytes 1 | tf_op jit(solution)/shard_map/project/pallas_call | solution.py:110
  2.8 3.0 %collective-permute-start = (bf16[128,1024]{1,0:T(8,128)(2,1)S(1)}, bf16[128,1024]{1,0:T(8,128)(2,1)S(1)}, u32[]{:S(2)}, u32[]{:S(2)}) collective-permute-start(bf16[128,1024]{1,0:T(8,128)(2,1)S(1)} %get-tuple-element.27.refs_0_), channel_id=1, source_target_pairs={{0,16},{4,20},{8,24},{12,28},{16,0},{20,4},{24,8},{28,12},{1,17},{... | collective-permute-start | bytes 786440 | tf_op jit(solution)/shard_map/y2a/ppermute | solution.py:47
  5.9 2.9 %project.4 = (bf16[128,1024]{1,0:T(8,128)(2,1)S(1)}, bf16[128,1024]{1,0:T(8,128)(2,1)S(1)}, bf16[128,1024]{1,0:T(8,128)(2,1)S(1)}, bf16[128,1024]{1,0:T(8,128)(2...) custom-call(s32[2,32]{1,0:T(2,128)} %bitcast.2, bf16[1024,128]{1,0:T(8,128)(2,1)} %refs_0_, ...), custom_call_target="tpu_custom_call" | custom-call | flops 1000 | bytes 1 | tf_op jit(solution)/shard_map/project/pallas_call | solution.py:110
  8.8 3.3 %project.5 = (f32[128,2048]{1,0:T(8,128)S(1)}, f32[128,2048]{1,0:T(8,128)S(1)}, f32[128,2048]{1,0:T(8,128)S(1)}, f32[128,2048]{1,0:T(8,128)S(1)}) custom-call(s32[2,32]{1,0:T(2,128)} %bitcast.3, bf16[1024,128]{1,0:T(8,128)(2,1)} %refs_0_, bf16[1024,2048]{1,0:T(8,128)(2,1)} %lap_ref.5, bf16[128,1024]{1,0:T(8,128)(2,1)S(1)} %get-tuple-element.34.refs_0_), custom_call_target="tpu_custom_call" | custom-call | flops 1000 | bytes 1 | tf_op jit(solution)/shard_map/project/pallas_call | solution.py:110
  12.1 0.8 %collective-permute-done.received_ref = bf16[128,1024]{1,0:T(8,128)(2,1)S(1)} collective-permute-done((bf16[128,1024]{1,0:T(8,128)(2,1)S(1)}, bf16[128,1024]{1,0:T(8,128)(2,1)S(1)}, u32[]{:S(2)}, u32[]{:S(2)}) %collective-permute-start) | collective-permute-done | bytes 262176 | tf_op jit(solution)/shard_map/y2a/ppermute | solution.py:47
  13.0 2.1 %collective-permute-start.1 = (bf16[128,1024]{1,0:T(8,128)(2,1)S(1)}, bf16[128,1024]{1,0:T(8,128)(2,1)S(1)}, u32[]{:S(2)}, u32[]{:S(2)}) collective-permute-start(bf16[128,1024]{1,0:T(8,128)(2,1)S(1)} %get-tuple-element.34.refs_0_), channel_id=1, source_target_pairs={{0,16},{4,20},{8,24},{12,28},{16,0},{20,4},{24,8},{28,12},{1,17},{... | collective-permute-start | bytes 786440 | tf_op jit(solution)/shard_map/y3a/ppermute | solution.py:47
  15.2 2.6 %collective-permute-start.3 = (bf16[128,1024]{1,0:T(8,128)(2,1)S(1)}, bf16[128,1024]{1,0:T(8,128)(2,1)S(1)}, u32[]{:S(2)}, u32[]{:S(2)}) collective-permute-start(bf16[128,1024]{1,0:T(8,128)(2,1)S(1)} %combine.8.refs_0_), channel_id=1, source_target_pairs={{0,2},{1,3},{2,0},{3,1},{4,6},{5,7},{6,4},{7,5},{8,10},{9,11},{10,... | collective-permute-start | bytes 786440 | tf_op jit(solution)/shard_map/z2a/ppermute | solution.py:47
  17.7 0.8 %collective-permute-done.2.received_ref = bf16[128,1024]{1,0:T(8,128)(2,1)S(1)} collective-permute-done((bf16[128,1024]{1,0:T(8,128)(2,1)S(1)}, bf16[128,1024]{1,0:T(8,128)(2,1)S(1)}, u32[]{:S(2)}, u32[]{:S(2)}) %collective-permute-start.2) | collective-permute-done | bytes 262176 | tf_op jit(solution)/shard_map/y2b/ppermute | solution.py:47
  18.6 2.1 %collective-permute-start.5 = (bf16[128,1024]{1,0:T(8,128)(2,1)S(1)}, bf16[128,1024]{1,0:T(8,128)(2,1)S(1)}, u32[]{:S(2)}, u32[]{:S(2)}) collective-permute-start(bf16[128,1024]{1,0:T(8,128)(2,1)S(1)} %get-tuple-element.38), channel_id=1, source_target_pairs={{0,16},{4,20},{8,24},{12,28},{16,0},{20,4},{24,8},{28,12},{1,17},{... | collective-permute-start | bytes 786440 | tf_op jit(solution)/shard_map/y1a/ppermute | solution.py:47
  20.9 1.9 %collective-permute-start.8 = (bf16[1024,128]{1,0:T(8,128)(2,1)S(1)}, bf16[1024,128]{1,0:T(8,128)(2,1)S(1)}, u32[]{:S(2)}, u32[]{:S(2)}) collective-permute-start(bf16[1024,128]{1,0:T(8,128)(2,1)S(1)} %copy-done), channel_id=1, source_target_pairs={{0,8},{4,12},{8,0},{12,4},{16,24},{20,28},{24,16},{28,20},{1,9},{5... | collective-permute-start | bytes 786440 | tf_op jit(solution)/shard_map/gather2/ppermute | solution.py:47
  22.8 1.4 %collective-permute-done.1.received_ref = bf16[128,1024]{1,0:T(8,128)(2,1)S(1)} collective-permute-done((bf16[128,1024]{1,0:T(8,128)(2,1)S(1)}, bf16[128,1024]{1,0:T(8,128)(2,1)S(1)}, u32[]{:S(2)}, u32[]{:S(2)}) %collective-permute-start.1) | collective-permute-done | bytes 262176 | tf_op jit(solution)/shard_map/y3a/ppermute | solution.py:47
  24.2 3.1 %collective-permute-start.7 = (bf16[128,1024]{1,0:T(8,128)(2,1)S(1)}, bf16[128,1024]{1,0:T(8,128)(2,1)S(1)}, u32[]{:S(2)}, u32[]{:S(2)}) collective-permute-start(bf16[128,1024]{1,0:T(8,128)(2,1)S(1)} %combine.9.refs_0_), channel_id=1, source_target_pairs={{0,2},{1,3},{2,0},{3,1},{4,6},{5,7},{6,4},{7,5},{8,10},{9,11},{10,... | collective-permute-start | bytes 786440 | tf_op jit(solution)/shard_map/z2b/ppermute | solution.py:47
  27.3 7.4 %collective-permute-done.3.refs_1_.refs_10_ = bf16[128,1024]{1,0:T(8,128)(2,1)S(1)} collective-permute-done((bf16[128,1024]{1,0:T(8,128)(2,1)S(1)}, bf16[128,1024]{1,0:T(8,128)(2,1)S(1)}, u32[]{:S(2)}, u32[]{:S(2)}) %collective-permute-start.3) | collective-permute-done | bytes 262176 | tf_op jit(solution)/shard_map/z2a/ppermute | solution.py:47
  35.0 2.0 %collective-permute-start.16 = (bf16[128,1024]{1,0:T(8,128)(2,1)S(1)}, bf16[128,1024]{1,0:T(8,128)(2,1)S(1)}, u32[]{:S(2)}, u32[]{:S(2)}) collective-permute-start(bf16[128,1024]{1,0:T(8,128)(2,1)S(1)} %get-tuple-element.49), channel_id=1, source_target_pairs={{0,16},{4,20},{8,24},{12,28},{16,0},{20,4},{24,8},{28,12},{1,17},{... | collective-permute-start | bytes 786440 | tf_op jit(solution)/shard_map/y3b/ppermute | solution.py:47
  37.0 1.5 %collective-permute-start.10 = (bf16[1024,128]{1,0:T(8,128)(2,1)S(1)}, bf16[1024,128]{1,0:T(8,128)(2,1)S(1)}, u32[]{:S(2)}, u32[]{:S(2)}) collective-permute-start(bf16[1024,128]{1,0:T(8,128)(2,1)S(1)} %collective-permute-done.6.refs_1_), channel_id=1, source_target_pairs={{0,8},{4,12},{8,0},{12,4},{16,24},{20,28},{24,16},{28,20},{1,9},{5... | collective-permute-start | bytes 786440 | tf_op jit(solution)/shard_map/gather2/ppermute | solution.py:47
  38.5 0.8 %collective-permute-done.7.refs_2_.refs_11_ = bf16[128,1024]{1,0:T(8,128)(2,1)S(1)} collective-permute-done((bf16[128,1024]{1,0:T(8,128)(2,1)S(1)}, bf16[128,1024]{1,0:T(8,128)(2,1)S(1)}, u32[]{:S(2)}, u32[]{:S(2)}) %collective-permute-start.7) | collective-permute-done | bytes 262176 | tf_op jit(solution)/shard_map/z2b/ppermute | solution.py:47
  39.3 3.4 %collective-permute-start.17 = (bf16[128,1024]{1,0:T(8,128)(2,1)S(1)}, bf16[128,1024]{1,0:T(8,128)(2,1)S(1)}, u32[]{:S(2)}, u32[]{:S(2)}) collective-permute-start(bf16[128,1024]{1,0:T(8,128)(2,1)S(1)} %combine.10.refs_0_), channel_id=1, source_target_pairs={{0,3},{1,2},{2,1},{3,0},{4,7},{5,6},{6,5},{7,4},{8,11},{9,10},{10,... | collective-permute-start | bytes 786440 | tf_op jit(solution)/shard_map/z3a/ppermute | solution.py:47
  42.7 0.3 collective-permute-done.4.received_ref
  43.1 1.2 %collective-permute-start.15 = (bf16[128,1024]{1,0:T(8,128)(2,1)S(1)}, bf16[128,1024]{1,0:T(8,128)(2,1)S(1)}, u32[]{:S(2)}, u32[]{:S(2)}) collective-permute-start(bf16[128,1024]{1,0:T(8,128)(2,1)S(1)} %get-tuple-element.47), channel_id=1, source_target_pairs={{0,16},{4,20},{8,24},{12,28},{16,0},{20,4},{24,8},{28,12},{1,17},{... | collective-permute-start | bytes 786440 | tf_op jit(solution)/shard_map/y0a/ppermute | solution.py:47
  44.3 2.7 %collective-permute-done.16.received_ref = bf16[128,1024]{1,0:T(8,128)(2,1)S(1)} collective-permute-done((bf16[128,1024]{1,0:T(8,128)(2,1)S(1)}, bf16[128,1024]{1,0:T(8,128)(2,1)S(1)}, u32[]{:S(2)}, u32[]{:S(2)}) %collective-permute-start.16) | collective-permute-done | bytes 262176 | tf_op jit(solution)/shard_map/y3b/ppermute | solution.py:47
  47.0 2.3 %collective-permute-start.18 = (bf16[128,1024]{1,0:T(8,128)(2,1)S(1)}, bf16[128,1024]{1,0:T(8,128)(2,1)S(1)}, u32[]{:S(2)}, u32[]{:S(2)}) collective-permute-start(bf16[128,1024]{1,0:T(8,128)(2,1)S(1)} %combine.12.refs_0_), channel_id=1, source_target_pairs={{0,1},{1,0},{2,3},{3,2},{4,5},{5,4},{6,7},{7,6},{8,9},{9,8},{10,11... | collective-permute-start | bytes 786440 | tf_op jit(solution)/shard_map/z1b/ppermute | solution.py:47
  49.3 2.9 %collective-permute-start.19 = (bf16[128,1024]{1,0:T(8,128)(2,1)S(1)}, bf16[128,1024]{1,0:T(8,128)(2,1)S(1)}, u32[]{:S(2)}, u32[]{:S(2)}) collective-permute-start(bf16[128,1024]{1,0:T(8,128)(2,1)S(1)} %combine.13.refs_0_), channel_id=1, source_target_pairs={{0,3},{1,2},{2,1},{3,0},{4,7},{5,6},{6,5},{7,4},{8,11},{9,10},{10,... | collective-permute-start | bytes 786440 | tf_op jit(solution)/shard_map/z3b/ppermute | solution.py:47
  52.2 0.8 %restrict.1 = (bf16[32,512]{1,0:T(8,128)(2,1)S(1)}, bf16[32,512]{1,0:T(8,128)(2,1)S(1)}) custom-call(s32[2,32]{1,0:T(2,128)S(1)} %bitcast.5, bf16[32,1024]{1,0:T(8,128)(2,1)S(1)} %copy-done.1, bf16[1024,128]{1,0:T(8,128)(2,1)S(1)} %copy-done, bf16[128,1024]{1,0:T(8,128)(2,1)S(1)} %combine.12.refs_0_), custom_call_target="tpu_custom_call" | custom-call | flops 1000 | bytes 1 | tf_op jit(solution)/shard_map/restrict/pallas_call | solution.py:304
  53.0 0.8 %collective-permute-start.9 = (bf16[32,512]{1,0:T(8,128)(2,1)S(1)}, bf16[32,512]{1,0:T(8,128)(2,1)S(1)}, u32[]{:S(2)}, u32[]{:S(2)}) collective-permute-start(bf16[32,512]{1,0:T(8,128)(2,1)S(1)} %get-tuple-element.41), channel_id=1, source_target_pairs={{0,16},{4,20},{8,24},{12,28},{16,0},{20,4},{24,8},{28,12},{1,17},{... | collective-permute-start | bytes 98312 | tf_op jit(solution)/shard_map/vectors/ppermute | solution.py:47
  53.8 1.5 %assemble.1 = (bf16[1024,128]{1,0:T(8,128)(2,1)S(1)}, bf16[1024,128]{1,0:T(8,128)(2,1)S(1)}, bf16[1024,128]{1,0:T(8,128)(2,1)S(1)}, bf16[1024,128]{1,0:T(8,128)(2,1)S(1)}) custom-call(s32[2,32]{1,0:T(2,128)} %bitcast.4, bf16[1024,128]{1,0:T(8,128)(2,1)S(1)} %copy-done, bf16[1024,128]{1,0:T(8,128)(2,1)S(1)} %collective-permute-done.6.refs_1_, ...), custom_call_target="tpu_custom_call" | custom-call | flops 1000 | bytes 1 | tf_op jit(solution)/shard_map/assemble/pallas_call | solution.py:193
  55.3 1.4 %collective-permute-start.20 = (bf16[128,1024]{1,0:T(8,128)(2,1)S(1)}, bf16[128,1024]{1,0:T(8,128)(2,1)S(1)}, u32[]{:S(2)}, u32[]{:S(2)}) collective-permute-start(bf16[128,1024]{1,0:T(8,128)(2,1)S(1)} %get-tuple-element.51), channel_id=1, source_target_pairs={{0,16},{4,20},{8,24},{12,28},{16,0},{20,4},{24,8},{28,12},{1,17},{... | collective-permute-start | bytes 786440 | tf_op jit(solution)/shard_map/y0b/ppermute | solution.py:47
  56.7 0.7 %collective-permute-done.9.refs_3_.far_ref = bf16[32,512]{1,0:T(8,128)(2,1)S(1)} collective-permute-done((bf16[32,512]{1,0:T(8,128)(2,1)S(1)}, bf16[32,512]{1,0:T(8,128)(2,1)S(1)}, u32[]{:S(2)}, u32[]{:S(2)}) %collective-permute-start.9) | collective-permute-done | bytes 32800 | tf_op jit(solution)/shard_map/vectors/ppermute | solution.py:47
  57.4 0.5 collective-permute-start.12
  57.9 0.7 %collective-permute-done.18.refs_2_.refs_13_ = bf16[128,1024]{1,0:T(8,128)(2,1)S(1)} collective-permute-done((bf16[128,1024]{1,0:T(8,128)(2,1)S(1)}, bf16[128,1024]{1,0:T(8,128)(2,1)S(1)}, u32[]{:S(2)}, u32[]{:S(2)}) %collective-permute-start.18) | collective-permute-done | bytes 262176 | tf_op jit(solution)/shard_map/z1b/ppermute | solution.py:47
  58.6 4.9 %collective-permute-done.19.refs_4_.refs_15_ = bf16[128,1024]{1,0:T(8,128)(2,1)S(1)} collective-permute-done((bf16[128,1024]{1,0:T(8,128)(2,1)S(1)}, bf16[128,1024]{1,0:T(8,128)(2,1)S(1)}, u32[]{:S(2)}, u32[]{:S(2)}) %collective-permute-start.19) | collective-permute-done | bytes 262176 | tf_op jit(solution)/shard_map/z3b/ppermute | solution.py:47
  63.7 1.4 %collective-permute-done.14.refs_7_ = bf16[1024,128]{1,0:T(8,128)(2,1)S(1)} collective-permute-done((bf16[1024,128]{1,0:T(8,128)(2,1)S(1)}, bf16[1024,128]{1,0:T(8,128)(2,1)S(1)}, u32[]{:S(2)}, u32[]{:S(2)}) %collective-permute-start.14) | collective-permute-done | bytes 262176 | tf_op jit(solution)/shard_map/core/ppermute | solution.py:47
  65.0 1.6 %finish.1 = (bf16[128,4096]{1,0:T(8,128)(2,1)}, bf16[32,512]{1,0:T(8,128)(2,1)}) custom-call(bf16[32,512]{1,0:T(8,128)(2,1)S(1)} %get-tuple-element.40.own_ref, bf16[32,512]{1,0:T(8,128)(2,1)S(1)} %collective-permute-done.9.refs_3_.far_ref, bf16[1024,128]{1,0:T(8,128)(2,1)S(1)} %get-tuple-element.42.refs_0_, ...), custom_call_target="tpu_custom_call" | custom-call | flops 1000 | bytes 1 | tf_op jit(solution)/shard_map/finish/pallas_call | solution.py:267
  (32 shorter events, 0.8 us)
Async XLA Ops:
  2.8 10.2 %collective-permute-start = (bf16[128,1024]{1,0:T(8,128)(2,1)S(1)}, bf16[128,1024]{1,0:T(8,128)(2,1)S(1)}, u32[]{:S(2)}, u32[]{:S(2)}) collective-permute-start(bf16[128,1024]{1,0:T(8,128)(2,1)S(1)} %get-tuple-element.27.refs_0_), channel_id=1, source_target_pairs={{0,16},{4,20},{8,24},{12,28},{16,0},{20,4},{24,8},{28,12},{1,17},{... | collective-permute-start | bytes 786440 | tf_op jit(solution)/shard_map/y2a/ppermute | solution.py:47
  5.8 12.8 %collective-permute-start.2 = (bf16[128,1024]{1,0:T(8,128)(2,1)S(1)}, bf16[128,1024]{1,0:T(8,128)(2,1)S(1)}, u32[]{:S(2)}, u32[]{:S(2)}) collective-permute-start(bf16[128,1024]{1,0:T(8,128)(2,1)S(1)} %get-tuple-element.35), channel_id=1, source_target_pairs={{0,16},{4,20},{8,24},{12,28},{16,0},{20,4},{24,8},{28,12},{1,17},{... | collective-permute-start | bytes 786440 | tf_op jit(solution)/shard_map/y2b/ppermute | solution.py:47
  8.8 12.0 %copy-start = (bf16[1024,128]{1,0:T(8,128)(2,1)S(1)}, bf16[1024,128]{1,0:T(8,128)(2,1)}, u32[]{:S(2)}) copy-start(bf16[1024,128]{1,0:T(8,128)(2,1)} %refs_0_) | copy-start | bytes 786436
  13.0 11.2 %collective-permute-start.1 = (bf16[128,1024]{1,0:T(8,128)(2,1)S(1)}, bf16[128,1024]{1,0:T(8,128)(2,1)S(1)}, u32[]{:S(2)}, u32[]{:S(2)}) collective-permute-start(bf16[128,1024]{1,0:T(8,128)(2,1)S(1)} %get-tuple-element.34.refs_0_), channel_id=1, source_target_pairs={{0,16},{4,20},{8,24},{12,28},{16,0},{20,4},{24,8},{28,12},{1,17},{... | collective-permute-start | bytes 786440 | tf_op jit(solution)/shard_map/y3a/ppermute | solution.py:47
  15.2 19.6 %collective-permute-start.3 = (bf16[128,1024]{1,0:T(8,128)(2,1)S(1)}, bf16[128,1024]{1,0:T(8,128)(2,1)S(1)}, u32[]{:S(2)}, u32[]{:S(2)}) collective-permute-start(bf16[128,1024]{1,0:T(8,128)(2,1)S(1)} %combine.8.refs_0_), channel_id=1, source_target_pairs={{0,2},{1,3},{2,0},{3,1},{4,6},{5,7},{6,4},{7,5},{8,10},{9,11},{10,... | collective-permute-start | bytes 786440 | tf_op jit(solution)/shard_map/z2a/ppermute | solution.py:47
  18.6 16.3 %collective-permute-start.5 = (bf16[128,1024]{1,0:T(8,128)(2,1)S(1)}, bf16[128,1024]{1,0:T(8,128)(2,1)S(1)}, u32[]{:S(2)}, u32[]{:S(2)}) collective-permute-start(bf16[128,1024]{1,0:T(8,128)(2,1)S(1)} %get-tuple-element.38), channel_id=1, source_target_pairs={{0,16},{4,20},{8,24},{12,28},{16,0},{20,4},{24,8},{28,12},{1,17},{... | collective-permute-start | bytes 786440 | tf_op jit(solution)/shard_map/y1a/ppermute | solution.py:47
  20.8 16.3 %collective-permute-start.6 = (bf16[1024,128]{1,0:T(8,128)(2,1)S(1)}, bf16[1024,128]{1,0:T(8,128)(2,1)S(1)}, u32[]{:S(2)}, u32[]{:S(2)}) collective-permute-start(bf16[1024,128]{1,0:T(8,128)(2,1)S(1)} %copy-done), channel_id=1, source_target_pairs={{0,16},{4,20},{8,24},{12,28},{16,0},{20,4},{24,8},{28,12},{1,17},{... | collective-permute-start | bytes 786440 | tf_op jit(solution)/shard_map/gather4/ppermute | solution.py:47
  20.9 17.7 %collective-permute-start.8 = (bf16[1024,128]{1,0:T(8,128)(2,1)S(1)}, bf16[1024,128]{1,0:T(8,128)(2,1)S(1)}, u32[]{:S(2)}, u32[]{:S(2)}) collective-permute-start(bf16[1024,128]{1,0:T(8,128)(2,1)S(1)} %copy-done), channel_id=1, source_target_pairs={{0,8},{4,12},{8,0},{12,4},{16,24},{20,28},{24,16},{28,20},{1,9},{5... | collective-permute-start | bytes 786440 | tf_op jit(solution)/shard_map/gather2/ppermute | solution.py:47
  24.2 15.1 %collective-permute-start.7 = (bf16[128,1024]{1,0:T(8,128)(2,1)S(1)}, bf16[128,1024]{1,0:T(8,128)(2,1)S(1)}, u32[]{:S(2)}, u32[]{:S(2)}) collective-permute-start(bf16[128,1024]{1,0:T(8,128)(2,1)S(1)} %combine.9.refs_0_), channel_id=1, source_target_pairs={{0,2},{1,3},{2,0},{3,1},{4,6},{5,7},{6,4},{7,5},{8,10},{9,11},{10,... | collective-permute-start | bytes 786440 | tf_op jit(solution)/shard_map/z2b/ppermute | solution.py:47
  34.7 17.5 %copy-start.1 = (bf16[32,1024]{1,0:T(8,128)(2,1)S(1)}, bf16[32,1024]{1,0:T(8,128)(2,1)}, u32[]{:S(2)}) copy-start(bf16[32,1024]{1,0:T(8,128)(2,1)} %vec_ref.1) | copy-start | bytes 196612
  34.7 17.5 %copy-start.2 = (s32[32,2]{0,1:T(2,128)S(1)}, s32[32,2]{0,1:T(2,128)}, u32[]{:S(2)}) copy-start(s32[32,2]{0,1:T(2,128)} %param.7) | copy-start | bytes 772
  34.8 8.2 %collective-permute-start.4 = (bf16[128,1024]{1,0:T(8,128)(2,1)S(1)}, bf16[128,1024]{1,0:T(8,128)(2,1)S(1)}, u32[]{:S(2)}, u32[]{:S(2)}) collective-permute-start(bf16[128,1024]{1,0:T(8,128)(2,1)S(1)} %get-tuple-element.36), channel_id=1, source_target_pairs={{0,16},{4,20},{8,24},{12,28},{16,0},{20,4},{24,8},{28,12},{1,17},{... | collective-permute-start | bytes 786440 | tf_op jit(solution)/shard_map/y1b/ppermute | solution.py:47
  35.0 12.0 %collective-permute-start.16 = (bf16[128,1024]{1,0:T(8,128)(2,1)S(1)}, bf16[128,1024]{1,0:T(8,128)(2,1)S(1)}, u32[]{:S(2)}, u32[]{:S(2)}) collective-permute-start(bf16[128,1024]{1,0:T(8,128)(2,1)S(1)} %get-tuple-element.49), channel_id=1, source_target_pairs={{0,16},{4,20},{8,24},{12,28},{16,0},{20,4},{24,8},{28,12},{1,17},{... | collective-permute-start | bytes 786440 | tf_op jit(solution)/shard_map/y3b/ppermute | solution.py:47
  37.0 12.3 %collective-permute-start.10 = (bf16[1024,128]{1,0:T(8,128)(2,1)S(1)}, bf16[1024,128]{1,0:T(8,128)(2,1)S(1)}, u32[]{:S(2)}, u32[]{:S(2)}) collective-permute-start(bf16[1024,128]{1,0:T(8,128)(2,1)S(1)} %collective-permute-done.6.refs_1_), channel_id=1, source_target_pairs={{0,8},{4,12},{8,0},{12,4},{16,24},{20,28},{24,16},{28,20},{1,9},{5... | collective-permute-start | bytes 786440 | tf_op jit(solution)/shard_map/gather2/ppermute | solution.py:47
  38.5 14.5 %collective-permute-start.21 = (bf16[128,1024]{1,0:T(8,128)(2,1)S(1)}, bf16[128,1024]{1,0:T(8,128)(2,1)S(1)}, u32[]{:S(2)}, u32[]{:S(2)}) collective-permute-start(bf16[128,1024]{1,0:T(8,128)(2,1)S(1)} %combine.11.refs_0_), channel_id=1, source_target_pairs={{0,1},{1,0},{2,3},{3,2},{4,5},{5,4},{6,7},{7,6},{8,9},{9,8},{10,11... | collective-permute-start | bytes 786440 | tf_op jit(solution)/shard_map/z1a/ppermute | solution.py:47
  39.3 16.0 %collective-permute-start.17 = (bf16[128,1024]{1,0:T(8,128)(2,1)S(1)}, bf16[128,1024]{1,0:T(8,128)(2,1)S(1)}, u32[]{:S(2)}, u32[]{:S(2)}) collective-permute-start(bf16[128,1024]{1,0:T(8,128)(2,1)S(1)} %combine.10.refs_0_), channel_id=1, source_target_pairs={{0,3},{1,2},{2,1},{3,0},{4,7},{5,6},{6,5},{7,4},{8,11},{9,10},{10,... | collective-permute-start | bytes 786440 | tf_op jit(solution)/shard_map/z3a/ppermute | solution.py:47
  43.1 14.3 %collective-permute-start.15 = (bf16[128,1024]{1,0:T(8,128)(2,1)S(1)}, bf16[128,1024]{1,0:T(8,128)(2,1)S(1)}, u32[]{:S(2)}, u32[]{:S(2)}) collective-permute-start(bf16[128,1024]{1,0:T(8,128)(2,1)S(1)} %get-tuple-element.47), channel_id=1, source_target_pairs={{0,16},{4,20},{8,24},{12,28},{16,0},{20,4},{24,8},{28,12},{1,17},{... | collective-permute-start | bytes 786440 | tf_op jit(solution)/shard_map/y0a/ppermute | solution.py:47
  47.0 11.6 %collective-permute-start.18 = (bf16[128,1024]{1,0:T(8,128)(2,1)S(1)}, bf16[128,1024]{1,0:T(8,128)(2,1)S(1)}, u32[]{:S(2)}, u32[]{:S(2)}) collective-permute-start(bf16[128,1024]{1,0:T(8,128)(2,1)S(1)} %combine.12.refs_0_), channel_id=1, source_target_pairs={{0,1},{1,0},{2,3},{3,2},{4,5},{5,4},{6,7},{7,6},{8,9},{9,8},{10,11... | collective-permute-start | bytes 786440 | tf_op jit(solution)/shard_map/z1b/ppermute | solution.py:47
  49.3 14.2 %collective-permute-start.19 = (bf16[128,1024]{1,0:T(8,128)(2,1)S(1)}, bf16[128,1024]{1,0:T(8,128)(2,1)S(1)}, u32[]{:S(2)}, u32[]{:S(2)}) collective-permute-start(bf16[128,1024]{1,0:T(8,128)(2,1)S(1)} %combine.13.refs_0_), channel_id=1, source_target_pairs={{0,3},{1,2},{2,1},{3,0},{4,7},{5,6},{6,5},{7,4},{8,11},{9,10},{10,... | collective-permute-start | bytes 786440 | tf_op jit(solution)/shard_map/z3b/ppermute | solution.py:47
  53.0 4.4 %collective-permute-start.9 = (bf16[32,512]{1,0:T(8,128)(2,1)S(1)}, bf16[32,512]{1,0:T(8,128)(2,1)S(1)}, u32[]{:S(2)}, u32[]{:S(2)}) collective-permute-start(bf16[32,512]{1,0:T(8,128)(2,1)S(1)} %get-tuple-element.41), channel_id=1, source_target_pairs={{0,16},{4,20},{8,24},{12,28},{16,0},{20,4},{24,8},{28,12},{1,17},{... | collective-permute-start | bytes 98312 | tf_op jit(solution)/shard_map/vectors/ppermute | solution.py:47
  55.3 8.3 %collective-permute-start.20 = (bf16[128,1024]{1,0:T(8,128)(2,1)S(1)}, bf16[128,1024]{1,0:T(8,128)(2,1)S(1)}, u32[]{:S(2)}, u32[]{:S(2)}) collective-permute-start(bf16[128,1024]{1,0:T(8,128)(2,1)S(1)} %get-tuple-element.51), channel_id=1, source_target_pairs={{0,16},{4,20},{8,24},{12,28},{16,0},{20,4},{24,8},{28,12},{1,17},{... | collective-permute-start | bytes 786440 | tf_op jit(solution)/shard_map/y0b/ppermute | solution.py:47
  57.4 6.2 %collective-permute-start.11 = (bf16[1024,128]{1,0:T(8,128)(2,1)S(1)}, bf16[1024,128]{1,0:T(8,128)(2,1)S(1)}, u32[]{:S(2)}, u32[]{:S(2)}) collective-permute-start(bf16[1024,128]{1,0:T(8,128)(2,1)S(1)} %get-tuple-element.42.refs_0_), channel_id=1, source_target_pairs={{0,4},{4,0},{8,12},{12,8},{16,20},{20,16},{24,28},{28,24},{1,5},{5... | collective-permute-start | bytes 786440 | tf_op jit(solution)/shard_map/core/ppermute | solution.py:47
  57.4 6.2 %collective-permute-start.12 = (bf16[1024,128]{1,0:T(8,128)(2,1)S(1)}, bf16[1024,128]{1,0:T(8,128)(2,1)S(1)}, u32[]{:S(2)}, u32[]{:S(2)}) collective-permute-start(bf16[1024,128]{1,0:T(8,128)(2,1)S(1)} %get-tuple-element.43.refs_1_), channel_id=1, source_target_pairs={{0,4},{4,0},{8,12},{12,8},{16,20},{20,16},{24,28},{28,24},{1,5},{5... | collective-permute-start | bytes 786440 | tf_op jit(solution)/shard_map/core/ppermute | solution.py:47
  58.6 5.0 %collective-permute-start.13 = (bf16[1024,128]{1,0:T(8,128)(2,1)S(1)}, bf16[1024,128]{1,0:T(8,128)(2,1)S(1)}, u32[]{:S(2)}, u32[]{:S(2)}) collective-permute-start(bf16[1024,128]{1,0:T(8,128)(2,1)S(1)} %get-tuple-element.44.refs_2_), channel_id=1, source_target_pairs={{0,4},{4,0},{8,12},{12,8},{16,20},{20,16},{24,28},{28,24},{1,5},{5... | collective-permute-start | bytes 786440 | tf_op jit(solution)/shard_map/core/ppermute | solution.py:47
  63.5 1.5 %collective-permute-start.14 = (bf16[1024,128]{1,0:T(8,128)(2,1)S(1)}, bf16[1024,128]{1,0:T(8,128)(2,1)S(1)}, u32[]{:S(2)}, u32[]{:S(2)}) collective-permute-start(bf16[1024,128]{1,0:T(8,128)(2,1)S(1)} %get-tuple-element.45.refs_3_), channel_id=1, source_target_pairs={{0,4},{4,0},{8,12},{12,8},{16,20},{20,16},{24,28},{28,24},{1,5},{5... | collective-permute-start | bytes 786440 | tf_op jit(solution)/shard_map/core/ppermute | solution.py:47

commit v5 on v4

--- a/solution.py
+++ b/solution.py
@@ -7,7 +7,7 @@
 
 
 YAFTER = {'3a': ['2a'], '1a': ['2b'], '1b': ['3a'], '3b': ['1a'], '0a': ['1b'], '0b': ['3b']}
-HEAD = 1
+FIRST = 2
 CORE_PARTS = 4
 GATHER = '2b'
 VECTORS = '1b'
@@ -16,7 +16,7 @@
 PFLOPS = (1000, 1000)
 CFLOPS = 1000
 ASSEMBLE = 1000
-WAITS = {'3a': ['z2a'], '1b': ['g1', 'z2b', 'g2'], '0a': ['z3a', 'z1b', 'v', 'z3b'], '0b': ['g3', 'z1a']}
+WAITS = {'3a': ['z2a'], '1b': ['g1', 'z2b', 'g2'], '0a': ['z3a', 'z1b', 'v', 'z3b'], '0b': ['z1a', 'p0', 'p1', 'p2', 'p3']}
 
 
 TOKENS = [('h', 0, 8), ('h', 8, 16), ('f', 0, 8), ('n', 0, 8), ('n', 8, 16), ('f', 8, 16), ('0', 0, 8), ('0', 8, 16)]
@@ -334,14 +334,12 @@
         for step in steps
     }
     labels = [f"{step}{'abcdefgh'[spans[step].index((lo * cols // 16, hi * cols // 16))]}" for step, lo, hi in order]
-    head = HEAD
-    cut = sum(len(spans[step]) for step in steps[:head])
-    sent = project(
-        laplacian, interp, pairs, [(s, False, jnp.bfloat16, spans[s]) for s in steps[:head]]
-    )
-    sent += project(
-        laplacian, interp, pairs, [(s, False, jnp.bfloat16, spans[s]) for s in steps[head:]], sent[0], flops=PFLOPS[0]
-    )
+    first, rest = steps[0], steps[1:]
+    cut = len(spans[first])
+    sent = project(laplacian, interp, pairs, [(first, False, jnp.bfloat16, spans[first][:FIRST])])
+    jobs = [(first, False, jnp.bfloat16, spans[first][FIRST:])] if FIRST < cut else []
+    jobs += [(s, False, jnp.bfloat16, spans[s]) for s in rest]
+    sent += project(laplacian, interp, pairs, jobs, sent[0], flops=PFLOPS[0])
     grouped = [(step, span) for step in steps for span in spans[step]]
     sent = dict(zip(grouped, sent))
     kept = project(

time: 66.9 us -> 65.3 us (0.976)
  starting transfers between devices: 31.2 us -> 27.4 us
  waiting for transfers between devices: 22 us -> 24.2 us
    ppermute x22, starting transfers between devices: 31.2 us -> 27.4 us  [exchange(): return lax.ppermute(block, axis, [(i, i ^ flip) for i in range(count)])]
    ppermute x22, waiting for transfers between devices: 22 us -> 24.2 us  [exchange(): return lax.ppermute(block, axis, [(i, i ^ flip) for i in range(count)])]
  transfers between devices with their start and end apart: 22 -> 22, of which waited for: 11 -> 12; matrix products, arithmetic and copies ran while one was open for 0% -> 0% of each run, Pallas kernels for 13% -> 14%
where the time goes in v5:
time: 65.3 us; the launch traced here: 65.1 us
  starting transfers between devices  27.4 us (42%)
  waiting for transfers between devices  24.2 us (37%)
  Pallas kernels  12.7 us (19%)
  between operations  0.74 us (1%)
    ppermute x22, starting transfers between devices, exchange(): return lax.ppermute(block, axis, [(i, i ^ flip) for i in range(count)])  27.4 us
    ppermute x22, waiting for transfers between devices, exchange(): return lax.ppermute(block, axis, [(i, i ^ flip) for i in range(count)])  24.2 us
    pallas_call x3, Pallas kernels, project(): pl.pallas_call(body, out_shape=outs, in_specs=[pl.BlockSpec(memory_space=...  8.38 us
    pallas_call x1, Pallas kernels, finish(): pl.pallas_call(body, out_shape=(jax.ShapeDtypeStruct((count, total), jnp....  1.66 us
    pallas_call x1, Pallas kernels, assemble(): pl.pallas_call(body, out_shape=[jax.ShapeDtypeStruct((length * tile, tile...  1.49 us
  transfers between devices with their start and end apart: 22, of which 12 were waited for; matrix products, arithmetic and copies ran while one was open for 0% of the time, Pallas kernels for 14%

profile of v5, /device:TPU:0, one launch (start us, length us, event | category | flops | bytes accessed | tf_op | source)
XLA Modules:
  0.0 65.1 jit_solution(4096324612406397129)
XLA Ops:
  0.6 2.2 %project.3 = (bf16[128,1024]{1,0:T(8,128)(2,1)S(1)}, bf16[128,1024]{1,0:T(8,128)(2,1)S(1)}) custom-call(s32[2,32]{1,0:T(2,128)} %bitcast.1, bf16[1024,128]{1,0:T(8,128)(2,1)} %refs_0_, bf16[1024,2048]{1,0:T(8,128)(2,1)} %lap_ref.5), custom_call_target="tpu_custom_call" | custom-call | flops 1000 | bytes 1 | tf_op jit(solution)/shard_map/project/pallas_call | solution.py:110
  2.8 3.0 %collective-permute-start = (bf16[128,1024]{1,0:T(8,128)(2,1)S(1)}, bf16[128,1024]{1,0:T(8,128)(2,1)S(1)}, u32[]{:S(2)}, u32[]{:S(2)}) collective-permute-start(bf16[128,1024]{1,0:T(8,128)(2,1)S(1)} %get-tuple-element.27.refs_0_), channel_id=1, source_target_pairs={{0,16},{4,20},{8,24},{12,28},{16,0},{20,4},{24,8},{28,12},{1,17},{... | collective-permute-start | bytes 786440 | tf_op jit(solution)/shard_map/y2a/ppermute | solution.py:47
  5.9 2.9 %project.4 = (bf16[128,1024]{1,0:T(8,128)(2,1)S(1)}, bf16[128,1024]{1,0:T(8,128)(2,1)S(1)}, bf16[128,1024]{1,0:T(8,128)(2,1)S(1)}, bf16[128,1024]{1,0:T(8,128)(2...) custom-call(s32[2,32]{1,0:T(2,128)} %bitcast.2, bf16[1024,128]{1,0:T(8,128)(2,1)} %refs_0_, ...), custom_call_target="tpu_custom_call" | custom-call | flops 1000 | bytes 1 | tf_op jit(solution)/shard_map/project/pallas_call | solution.py:110
  8.8 3.3 %project.5 = (f32[128,2048]{1,0:T(8,128)S(1)}, f32[128,2048]{1,0:T(8,128)S(1)}, f32[128,2048]{1,0:T(8,128)S(1)}, f32[128,2048]{1,0:T(8,128)S(1)}) custom-call(s32[2,32]{1,0:T(2,128)} %bitcast.3, bf16[1024,128]{1,0:T(8,128)(2,1)} %refs_0_, bf16[1024,2048]{1,0:T(8,128)(2,1)} %lap_ref.5, bf16[128,1024]{1,0:T(8,128)(2,1)S(1)} %get-tuple-element.34.refs_0_), custom_call_target="tpu_custom_call" | custom-call | flops 1000 | bytes 1 | tf_op jit(solution)/shard_map/project/pallas_call | solution.py:110
  12.2 0.8 %collective-permute-done.received_ref = bf16[128,1024]{1,0:T(8,128)(2,1)S(1)} collective-permute-done((bf16[128,1024]{1,0:T(8,128)(2,1)S(1)}, bf16[128,1024]{1,0:T(8,128)(2,1)S(1)}, u32[]{:S(2)}, u32[]{:S(2)}) %collective-permute-start) | collective-permute-done | bytes 262176 | tf_op jit(solution)/shard_map/y2a/ppermute | solution.py:47
  13.0 3.2 %collective-permute-start.3 = (bf16[128,1024]{1,0:T(8,128)(2,1)S(1)}, bf16[128,1024]{1,0:T(8,128)(2,1)S(1)}, u32[]{:S(2)}, u32[]{:S(2)}) collective-permute-start(bf16[128,1024]{1,0:T(8,128)(2,1)S(1)} %combine.8.refs_0_), channel_id=1, source_target_pairs={{0,2},{1,3},{2,0},{3,1},{4,6},{5,7},{6,4},{7,5},{8,10},{9,11},{10,... | collective-permute-start | bytes 786440 | tf_op jit(solution)/shard_map/z2a/ppermute | solution.py:47
  16.2 1.5 %collective-permute-start.1 = (bf16[128,1024]{1,0:T(8,128)(2,1)S(1)}, bf16[128,1024]{1,0:T(8,128)(2,1)S(1)}, u32[]{:S(2)}, u32[]{:S(2)}) collective-permute-start(bf16[128,1024]{1,0:T(8,128)(2,1)S(1)} %get-tuple-element.34.refs_0_), channel_id=1, source_target_pairs={{0,16},{4,20},{8,24},{12,28},{16,0},{20,4},{24,8},{28,12},{1,17},{... | collective-permute-start | bytes 786440 | tf_op jit(solution)/shard_map/y3a/ppermute | solution.py:47
  17.7 0.8 %collective-permute-done.2.received_ref = bf16[128,1024]{1,0:T(8,128)(2,1)S(1)} collective-permute-done((bf16[128,1024]{1,0:T(8,128)(2,1)S(1)}, bf16[128,1024]{1,0:T(8,128)(2,1)S(1)}, u32[]{:S(2)}, u32[]{:S(2)}) %collective-permute-start.2) | collective-permute-done | bytes 262176 | tf_op jit(solution)/shard_map/y2b/ppermute | solution.py:47
  18.6 2.0 %collective-permute-start.5 = (bf16[128,1024]{1,0:T(8,128)(2,1)S(1)}, bf16[128,1024]{1,0:T(8,128)(2,1)S(1)}, u32[]{:S(2)}, u32[]{:S(2)}) collective-permute-start(bf16[128,1024]{1,0:T(8,128)(2,1)S(1)} %get-tuple-element.38), channel_id=1, source_target_pairs={{0,16},{4,20},{8,24},{12,28},{16,0},{20,4},{24,8},{28,12},{1,17},{... | collective-permute-start | bytes 786440 | tf_op jit(solution)/shard_map/y1a/ppermute | solution.py:47
  20.7 1.9 %collective-permute-start.8 = (bf16[1024,128]{1,0:T(8,128)(2,1)S(1)}, bf16[1024,128]{1,0:T(8,128)(2,1)S(1)}, u32[]{:S(2)}, u32[]{:S(2)}) collective-permute-start(bf16[1024,128]{1,0:T(8,128)(2,1)S(1)} %copy-done), channel_id=1, source_target_pairs={{0,8},{4,12},{8,0},{12,4},{16,24},{20,28},{24,16},{28,20},{1,9},{5... | collective-permute-start | bytes 786440 | tf_op jit(solution)/shard_map/gather2/ppermute | solution.py:47
  22.6 2.8 %collective-permute-done.1.received_ref = bf16[128,1024]{1,0:T(8,128)(2,1)S(1)} collective-permute-done((bf16[128,1024]{1,0:T(8,128)(2,1)S(1)}, bf16[128,1024]{1,0:T(8,128)(2,1)S(1)}, u32[]{:S(2)}, u32[]{:S(2)}) %collective-permute-start.1) | collective-permute-done | bytes 262176 | tf_op jit(solution)/shard_map/y3a/ppermute | solution.py:47
  25.5 1.9 %collective-permute-start.7 = (bf16[128,1024]{1,0:T(8,128)(2,1)S(1)}, bf16[128,1024]{1,0:T(8,128)(2,1)S(1)}, u32[]{:S(2)}, u32[]{:S(2)}) collective-permute-start(bf16[128,1024]{1,0:T(8,128)(2,1)S(1)} %combine.9.refs_0_), channel_id=1, source_target_pairs={{0,2},{1,3},{2,0},{3,1},{4,6},{5,7},{6,4},{7,5},{8,10},{9,11},{10,... | collective-permute-start | bytes 786440 | tf_op jit(solution)/shard_map/z2b/ppermute | solution.py:47
  27.3 2.7 %collective-permute-done.3.refs_1_.refs_10_ = bf16[128,1024]{1,0:T(8,128)(2,1)S(1)} collective-permute-done((bf16[128,1024]{1,0:T(8,128)(2,1)S(1)}, bf16[128,1024]{1,0:T(8,128)(2,1)S(1)}, u32[]{:S(2)}, u32[]{:S(2)}) %collective-permute-start.3) | collective-permute-done | bytes 262176 | tf_op jit(solution)/shard_map/z2a/ppermute | solution.py:47
  30.1 0.9 %collective-permute-done.5.received_ref = bf16[128,1024]{1,0:T(8,128)(2,1)S(1)} collective-permute-done((bf16[128,1024]{1,0:T(8,128)(2,1)S(1)}, bf16[128,1024]{1,0:T(8,128)(2,1)S(1)}, u32[]{:S(2)}, u32[]{:S(2)}) %collective-permute-start.5) | collective-permute-done | bytes 262176 | tf_op jit(solution)/shard_map/y1a/ppermute | solution.py:47
  31.2 1.6 %collective-permute-start.4 = (bf16[128,1024]{1,0:T(8,128)(2,1)S(1)}, bf16[128,1024]{1,0:T(8,128)(2,1)S(1)}, u32[]{:S(2)}, u32[]{:S(2)}) collective-permute-start(bf16[128,1024]{1,0:T(8,128)(2,1)S(1)} %get-tuple-element.36), channel_id=1, source_target_pairs={{0,16},{4,20},{8,24},{12,28},{16,0},{20,4},{24,8},{28,12},{1,17},{... | collective-permute-start | bytes 786440 | tf_op jit(solution)/shard_map/y1b/ppermute | solution.py:47
  32.7 0.5 collective-permute-start.16
  33.2 3.5 %collective-permute-done.6.refs_1_ = bf16[1024,128]{1,0:T(8,128)(2,1)S(1)} collective-permute-done((bf16[1024,128]{1,0:T(8,128)(2,1)S(1)}, bf16[1024,128]{1,0:T(8,128)(2,1)S(1)}, u32[]{:S(2)}, u32[]{:S(2)}) %collective-permute-start.6) | collective-permute-done | bytes 262176 | tf_op jit(solution)/shard_map/gather4/ppermute | solution.py:47
  36.7 1.7 %collective-permute-start.17 = (bf16[128,1024]{1,0:T(8,128)(2,1)S(1)}, bf16[128,1024]{1,0:T(8,128)(2,1)S(1)}, u32[]{:S(2)}, u32[]{:S(2)}) collective-permute-start(bf16[128,1024]{1,0:T(8,128)(2,1)S(1)} %combine.10.refs_0_), channel_id=1, source_target_pairs={{0,3},{1,2},{2,1},{3,0},{4,7},{5,6},{6,5},{7,4},{8,11},{9,10},{10,... | collective-permute-start | bytes 786440 | tf_op jit(solution)/shard_map/z3a/ppermute | solution.py:47
  38.4 1.5 %collective-permute-start.10 = (bf16[1024,128]{1,0:T(8,128)(2,1)S(1)}, bf16[1024,128]{1,0:T(8,128)(2,1)S(1)}, u32[]{:S(2)}, u32[]{:S(2)}) collective-permute-start(bf16[1024,128]{1,0:T(8,128)(2,1)S(1)} %collective-permute-done.6.refs_1_), channel_id=1, source_target_pairs={{0,8},{4,12},{8,0},{12,4},{16,24},{20,28},{24,16},{28,20},{1,9},{5... | collective-permute-start | bytes 786440 | tf_op jit(solution)/shard_map/gather2/ppermute | solution.py:47
  39.9 1.4 %collective-permute-done.7.refs_2_.refs_11_ = bf16[128,1024]{1,0:T(8,128)(2,1)S(1)} collective-permute-done((bf16[128,1024]{1,0:T(8,128)(2,1)S(1)}, bf16[128,1024]{1,0:T(8,128)(2,1)S(1)}, u32[]{:S(2)}, u32[]{:S(2)}) %collective-permute-start.7) | collective-permute-done | bytes 262176 | tf_op jit(solution)/shard_map/z2b/ppermute | solution.py:47
  41.3 1.0 %collective-permute-done.4.received_ref = bf16[128,1024]{1,0:T(8,128)(2,1)S(1)} collective-permute-done((bf16[128,1024]{1,0:T(8,128)(2,1)S(1)}, bf16[128,1024]{1,0:T(8,128)(2,1)S(1)}, u32[]{:S(2)}, u32[]{:S(2)}) %collective-permute-start.4) | collective-permute-done | bytes 262176 | tf_op jit(solution)/shard_map/y1b/ppermute | solution.py:47
  42.4 3.5 %collective-permute-done.16.received_ref = bf16[128,1024]{1,0:T(8,128)(2,1)S(1)} collective-permute-done((bf16[128,1024]{1,0:T(8,128)(2,1)S(1)}, bf16[128,1024]{1,0:T(8,128)(2,1)S(1)}, u32[]{:S(2)}, u32[]{:S(2)}) %collective-permute-start.16) | collective-permute-done | bytes 262176 | tf_op jit(solution)/shard_map/y3b/ppermute | solution.py:47
  45.9 4.1 %collective-permute-start.19 = (bf16[128,1024]{1,0:T(8,128)(2,1)S(1)}, bf16[128,1024]{1,0:T(8,128)(2,1)S(1)}, u32[]{:S(2)}, u32[]{:S(2)}) collective-permute-start(bf16[128,1024]{1,0:T(8,128)(2,1)S(1)} %combine.13.refs_0_), channel_id=1, source_target_pairs={{0,3},{1,2},{2,1},{3,0},{4,7},{5,6},{6,5},{7,4},{8,11},{9,10},{10,... | collective-permute-start | bytes 786440 | tf_op jit(solution)/shard_map/z3b/ppermute | solution.py:47
  50.0 1.5 %collective-permute-start.15 = (bf16[128,1024]{1,0:T(8,128)(2,1)S(1)}, bf16[128,1024]{1,0:T(8,128)(2,1)S(1)}, u32[]{:S(2)}, u32[]{:S(2)}) collective-permute-start(bf16[128,1024]{1,0:T(8,128)(2,1)S(1)} %get-tuple-element.47), channel_id=1, source_target_pairs={{0,16},{4,20},{8,24},{12,28},{16,0},{20,4},{24,8},{28,12},{1,17},{... | collective-permute-start | bytes 786440 | tf_op jit(solution)/shard_map/y0a/ppermute | solution.py:47
  51.5 0.8 %restrict.1 = (bf16[32,512]{1,0:T(8,128)(2,1)S(1)}, bf16[32,512]{1,0:T(8,128)(2,1)S(1)}) custom-call(s32[2,32]{1,0:T(2,128)S(1)} %bitcast.5, bf16[32,1024]{1,0:T(8,128)(2,1)S(1)} %copy-done.1, bf16[1024,128]{1,0:T(8,128)(2,1)S(1)} %copy-done, bf16[128,1024]{1,0:T(8,128)(2,1)S(1)} %combine.12.refs_0_), custom_call_target="tpu_custom_call" | custom-call | flops 1000 | bytes 1 | tf_op jit(solution)/shard_map/restrict/pallas_call | solution.py:304
  52.3 0.6 collective-permute-start.9
  52.9 1.5 %assemble.1 = (bf16[1024,128]{1,0:T(8,128)(2,1)S(1)}, bf16[1024,128]{1,0:T(8,128)(2,1)S(1)}, bf16[1024,128]{1,0:T(8,128)(2,1)S(1)}, bf16[1024,128]{1,0:T(8,128)(2,1)S(1)}) custom-call(s32[2,32]{1,0:T(2,128)} %bitcast.4, bf16[1024,128]{1,0:T(8,128)(2,1)S(1)} %copy-done, bf16[1024,128]{1,0:T(8,128)(2,1)S(1)} %collective-permute-done.6.refs_1_, ...), custom_call_target="tpu_custom_call" | custom-call | flops 1000 | bytes 1 | tf_op jit(solution)/shard_map/assemble/pallas_call | solution.py:193
  54.4 1.6 %collective-permute-start.20 = (bf16[128,1024]{1,0:T(8,128)(2,1)S(1)}, bf16[128,1024]{1,0:T(8,128)(2,1)S(1)}, u32[]{:S(2)}, u32[]{:S(2)}) collective-permute-start(bf16[128,1024]{1,0:T(8,128)(2,1)S(1)} %get-tuple-element.51), channel_id=1, source_target_pairs={{0,16},{4,20},{8,24},{12,28},{16,0},{20,4},{24,8},{28,12},{1,17},{... | collective-permute-start | bytes 786440 | tf_op jit(solution)/shard_map/y0b/ppermute | solution.py:47
  56.0 4.0 %collective-permute-done.9.refs_3_.far_ref = bf16[32,512]{1,0:T(8,128)(2,1)S(1)} collective-permute-done((bf16[32,512]{1,0:T(8,128)(2,1)S(1)}, bf16[32,512]{1,0:T(8,128)(2,1)S(1)}, u32[]{:S(2)}, u32[]{:S(2)}) %collective-permute-start.9) | collective-permute-done | bytes 32800 | tf_op jit(solution)/shard_map/vectors/ppermute | solution.py:47
  60.5 1.3 %collective-permute-done.18.refs_2_.refs_13_ = bf16[128,1024]{1,0:T(8,128)(2,1)S(1)} collective-permute-done((bf16[128,1024]{1,0:T(8,128)(2,1)S(1)}, bf16[128,1024]{1,0:T(8,128)(2,1)S(1)}, u32[]{:S(2)}, u32[]{:S(2)}) %collective-permute-start.18) | collective-permute-done | bytes 262176 | tf_op jit(solution)/shard_map/z1b/ppermute | solution.py:47
  61.9 1.4 %collective-permute-done.20.received_ref = bf16[128,1024]{1,0:T(8,128)(2,1)S(1)} collective-permute-done((bf16[128,1024]{1,0:T(8,128)(2,1)S(1)}, bf16[128,1024]{1,0:T(8,128)(2,1)S(1)}, u32[]{:S(2)}, u32[]{:S(2)}) %collective-permute-start.20) | collective-permute-done | bytes 262176 | tf_op jit(solution)/shard_map/y0b/ppermute | solution.py:47
  63.4 1.7 %finish.1 = (bf16[128,4096]{1,0:T(8,128)(2,1)}, bf16[32,512]{1,0:T(8,128)(2,1)}) custom-call(bf16[32,512]{1,0:T(8,128)(2,1)S(1)} %get-tuple-element.40.own_ref, bf16[32,512]{1,0:T(8,128)(2,1)S(1)} %collective-permute-done.9.refs_3_.far_ref, bf16[1024,128]{1,0:T(8,128)(2,1)S(1)} %get-tuple-element.42.refs_0_, ...), custom_call_target="tpu_custom_call" | custom-call | flops 1000 | bytes 1 | tf_op jit(solution)/shard_map/finish/pallas_call | solution.py:267
  (32 shorter events, 1.3 us)
Async XLA Ops:
  2.8 10.2 %collective-permute-start = (bf16[128,1024]{1,0:T(8,128)(2,1)S(1)}, bf16[128,1024]{1,0:T(8,128)(2,1)S(1)}, u32[]{:S(2)}, u32[]{:S(2)}) collective-permute-start(bf16[128,1024]{1,0:T(8,128)(2,1)S(1)} %get-tuple-element.27.refs_0_), channel_id=1, source_target_pairs={{0,16},{4,20},{8,24},{12,28},{16,0},{20,4},{24,8},{28,12},{1,17},{... | collective-permute-start | bytes 786440 | tf_op jit(solution)/shard_map/y2a/ppermute | solution.py:47
  5.8 12.8 %collective-permute-start.2 = (bf16[128,1024]{1,0:T(8,128)(2,1)S(1)}, bf16[128,1024]{1,0:T(8,128)(2,1)S(1)}, u32[]{:S(2)}, u32[]{:S(2)}) collective-permute-start(bf16[128,1024]{1,0:T(8,128)(2,1)S(1)} %get-tuple-element.35), channel_id=1, source_target_pairs={{0,16},{4,20},{8,24},{12,28},{16,0},{20,4},{24,8},{28,12},{1,17},{... | collective-permute-start | bytes 786440 | tf_op jit(solution)/shard_map/y2b/ppermute | solution.py:47
  8.8 11.9 %copy-start = (bf16[1024,128]{1,0:T(8,128)(2,1)S(1)}, bf16[1024,128]{1,0:T(8,128)(2,1)}, u32[]{:S(2)}) copy-start(bf16[1024,128]{1,0:T(8,128)(2,1)} %refs_0_) | copy-start | bytes 786436
  13.0 17.0 %collective-permute-start.3 = (bf16[128,1024]{1,0:T(8,128)(2,1)S(1)}, bf16[128,1024]{1,0:T(8,128)(2,1)S(1)}, u32[]{:S(2)}, u32[]{:S(2)}) collective-permute-start(bf16[128,1024]{1,0:T(8,128)(2,1)S(1)} %combine.8.refs_0_), channel_id=1, source_target_pairs={{0,2},{1,3},{2,0},{3,1},{4,6},{5,7},{6,4},{7,5},{8,10},{9,11},{10,... | collective-permute-start | bytes 786440 | tf_op jit(solution)/shard_map/z2a/ppermute | solution.py:47
  16.2 9.2 %collective-permute-start.1 = (bf16[128,1024]{1,0:T(8,128)(2,1)S(1)}, bf16[128,1024]{1,0:T(8,128)(2,1)S(1)}, u32[]{:S(2)}, u32[]{:S(2)}) collective-permute-start(bf16[128,1024]{1,0:T(8,128)(2,1)S(1)} %get-tuple-element.34.refs_0_), channel_id=1, source_target_pairs={{0,16},{4,20},{8,24},{12,28},{16,0},{20,4},{24,8},{28,12},{1,17},{... | collective-permute-start | bytes 786440 | tf_op jit(solution)/shard_map/y3a/ppermute | solution.py:47
  18.6 12.4 %collective-permute-start.5 = (bf16[128,1024]{1,0:T(8,128)(2,1)S(1)}, bf16[128,1024]{1,0:T(8,128)(2,1)S(1)}, u32[]{:S(2)}, u32[]{:S(2)}) collective-permute-start(bf16[128,1024]{1,0:T(8,128)(2,1)S(1)} %get-tuple-element.38), channel_id=1, source_target_pairs={{0,16},{4,20},{8,24},{12,28},{16,0},{20,4},{24,8},{28,12},{1,17},{... | collective-permute-start | bytes 786440 | tf_op jit(solution)/shard_map/y1a/ppermute | solution.py:47
  20.6 16.1 %collective-permute-start.6 = (bf16[1024,128]{1,0:T(8,128)(2,1)S(1)}, bf16[1024,128]{1,0:T(8,128)(2,1)S(1)}, u32[]{:S(2)}, u32[]{:S(2)}) collective-permute-start(bf16[1024,128]{1,0:T(8,128)(2,1)S(1)} %copy-done), channel_id=1, source_target_pairs={{0,16},{4,20},{8,24},{12,28},{16,0},{20,4},{24,8},{28,12},{1,17},{... | collective-permute-start | bytes 786440 | tf_op jit(solution)/shard_map/gather4/ppermute | solution.py:47
  20.7 17.7 %collective-permute-start.8 = (bf16[1024,128]{1,0:T(8,128)(2,1)S(1)}, bf16[1024,128]{1,0:T(8,128)(2,1)S(1)}, u32[]{:S(2)}, u32[]{:S(2)}) collective-permute-start(bf16[1024,128]{1,0:T(8,128)(2,1)S(1)} %copy-done), channel_id=1, source_target_pairs={{0,8},{4,12},{8,0},{12,4},{16,24},{20,28},{24,16},{28,20},{1,9},{5... | collective-permute-start | bytes 786440 | tf_op jit(solution)/shard_map/gather2/ppermute | solution.py:47
  25.5 15.8 %collective-permute-start.7 = (bf16[128,1024]{1,0:T(8,128)(2,1)S(1)}, bf16[128,1024]{1,0:T(8,128)(2,1)S(1)}, u32[]{:S(2)}, u32[]{:S(2)}) collective-permute-start(bf16[128,1024]{1,0:T(8,128)(2,1)S(1)} %combine.9.refs_0_), channel_id=1, source_target_pairs={{0,2},{1,3},{2,0},{3,1},{4,6},{5,7},{6,4},{7,5},{8,10},{9,11},{10,... | collective-permute-start | bytes 786440 | tf_op jit(solution)/shard_map/z2b/ppermute | solution.py:47
  30.1 21.4 %copy-start.1 = (bf16[32,1024]{1,0:T(8,128)(2,1)S(1)}, bf16[32,1024]{1,0:T(8,128)(2,1)}, u32[]{:S(2)}) copy-start(bf16[32,1024]{1,0:T(8,128)(2,1)} %vec_ref.1) | copy-start | bytes 196612
  30.1 21.4 %copy-start.2 = (s32[32,2]{0,1:T(2,128)S(1)}, s32[32,2]{0,1:T(2,128)}, u32[]{:S(2)}) copy-start(s32[32,2]{0,1:T(2,128)} %param.7) | copy-start | bytes 772
  31.2 11.2 %collective-permute-start.4 = (bf16[128,1024]{1,0:T(8,128)(2,1)S(1)}, bf16[128,1024]{1,0:T(8,128)(2,1)S(1)}, u32[]{:S(2)}, u32[]{:S(2)}) collective-permute-start(bf16[128,1024]{1,0:T(8,128)(2,1)S(1)} %get-tuple-element.36), channel_id=1, source_target_pairs={{0,16},{4,20},{8,24},{12,28},{16,0},{20,4},{24,8},{28,12},{1,17},{... | collective-permute-start | bytes 786440 | tf_op jit(solution)/shard_map/y1b/ppermute | solution.py:47
  32.7 13.1 %collective-permute-start.16 = (bf16[128,1024]{1,0:T(8,128)(2,1)S(1)}, bf16[128,1024]{1,0:T(8,128)(2,1)S(1)}, u32[]{:S(2)}, u32[]{:S(2)}) collective-permute-start(bf16[128,1024]{1,0:T(8,128)(2,1)S(1)} %get-tuple-element.49), channel_id=1, source_target_pairs={{0,16},{4,20},{8,24},{12,28},{16,0},{20,4},{24,8},{28,12},{1,17},{... | collective-permute-start | bytes 786440 | tf_op jit(solution)/shard_map/y3b/ppermute | solution.py:47
  36.7 14.8 %collective-permute-start.17 = (bf16[128,1024]{1,0:T(8,128)(2,1)S(1)}, bf16[128,1024]{1,0:T(8,128)(2,1)S(1)}, u32[]{:S(2)}, u32[]{:S(2)}) collective-permute-start(bf16[128,1024]{1,0:T(8,128)(2,1)S(1)} %combine.10.refs_0_), channel_id=1, source_target_pairs={{0,3},{1,2},{2,1},{3,0},{4,7},{5,6},{6,5},{7,4},{8,11},{9,10},{10,... | collective-permute-start | bytes 786440 | tf_op jit(solution)/shard_map/z3a/ppermute | solution.py:47
  38.4 13.9 %collective-permute-start.10 = (bf16[1024,128]{1,0:T(8,128)(2,1)S(1)}, bf16[1024,128]{1,0:T(8,128)(2,1)S(1)}, u32[]{:S(2)}, u32[]{:S(2)}) collective-permute-start(bf16[1024,128]{1,0:T(8,128)(2,1)S(1)} %collective-permute-done.6.refs_1_), channel_id=1, source_target_pairs={{0,8},{4,12},{8,0},{12,4},{16,24},{20,28},{24,16},{28,20},{1,9},{5... | collective-permute-start | bytes 786440 | tf_op jit(solution)/shard_map/gather2/ppermute | solution.py:47
  41.3 13.0 %collective-permute-start.21 = (bf16[128,1024]{1,0:T(8,128)(2,1)S(1)}, bf16[128,1024]{1,0:T(8,128)(2,1)S(1)}, u32[]{:S(2)}, u32[]{:S(2)}) collective-permute-start(bf16[128,1024]{1,0:T(8,128)(2,1)S(1)} %combine.11.refs_0_), channel_id=1, source_target_pairs={{0,1},{1,0},{2,3},{3,2},{4,5},{5,4},{6,7},{7,6},{8,9},{9,8},{10,11... | collective-permute-start | bytes 786440 | tf_op jit(solution)/shard_map/z1a/ppermute | solution.py:47
  45.9 14.0 %collective-permute-start.19 = (bf16[128,1024]{1,0:T(8,128)(2,1)S(1)}, bf16[128,1024]{1,0:T(8,128)(2,1)S(1)}, u32[]{:S(2)}, u32[]{:S(2)}) collective-permute-start(bf16[128,1024]{1,0:T(8,128)(2,1)S(1)} %combine.13.refs_0_), channel_id=1, source_target_pairs={{0,3},{1,2},{2,1},{3,0},{4,7},{5,6},{6,5},{7,4},{8,11},{9,10},{10,... | collective-permute-start | bytes 786440 | tf_op jit(solution)/shard_map/z3b/ppermute | solution.py:47
  50.0 10.5 %collective-permute-start.15 = (bf16[128,1024]{1,0:T(8,128)(2,1)S(1)}, bf16[128,1024]{1,0:T(8,128)(2,1)S(1)}, u32[]{:S(2)}, u32[]{:S(2)}) collective-permute-start(bf16[128,1024]{1,0:T(8,128)(2,1)S(1)} %get-tuple-element.47), channel_id=1, source_target_pairs={{0,16},{4,20},{8,24},{12,28},{16,0},{20,4},{24,8},{28,12},{1,17},{... | collective-permute-start | bytes 786440 | tf_op jit(solution)/shard_map/y0a/ppermute | solution.py:47
  51.5 10.3 %collective-permute-start.18 = (bf16[128,1024]{1,0:T(8,128)(2,1)S(1)}, bf16[128,1024]{1,0:T(8,128)(2,1)S(1)}, u32[]{:S(2)}, u32[]{:S(2)}) collective-permute-start(bf16[128,1024]{1,0:T(8,128)(2,1)S(1)} %combine.12.refs_0_), channel_id=1, source_target_pairs={{0,1},{1,0},{2,3},{3,2},{4,5},{5,4},{6,7},{7,6},{8,9},{9,8},{10,11... | collective-permute-start | bytes 786440 | tf_op jit(solution)/shard_map/z1b/ppermute | solution.py:47
  52.3 7.6 %collective-permute-start.9 = (bf16[32,512]{1,0:T(8,128)(2,1)S(1)}, bf16[32,512]{1,0:T(8,128)(2,1)S(1)}, u32[]{:S(2)}, u32[]{:S(2)}) collective-permute-start(bf16[32,512]{1,0:T(8,128)(2,1)S(1)} %get-tuple-element.41), channel_id=1, source_target_pairs={{0,16},{4,20},{8,24},{12,28},{16,0},{20,4},{24,8},{28,12},{1,17},{... | collective-permute-start | bytes 98312 | tf_op jit(solution)/shard_map/vectors/ppermute | solution.py:47
  54.4 8.9 %collective-permute-start.20 = (bf16[128,1024]{1,0:T(8,128)(2,1)S(1)}, bf16[128,1024]{1,0:T(8,128)(2,1)S(1)}, u32[]{:S(2)}, u32[]{:S(2)}) collective-permute-start(bf16[128,1024]{1,0:T(8,128)(2,1)S(1)} %get-tuple-element.51), channel_id=1, source_target_pairs={{0,16},{4,20},{8,24},{12,28},{16,0},{20,4},{24,8},{28,12},{1,17},{... | collective-permute-start | bytes 786440 | tf_op jit(solution)/shard_map/y0b/ppermute | solution.py:47
  59.9 3.4 %collective-permute-start.11 = (bf16[1024,128]{1,0:T(8,128)(2,1)S(1)}, bf16[1024,128]{1,0:T(8,128)(2,1)S(1)}, u32[]{:S(2)}, u32[]{:S(2)}) collective-permute-start(bf16[1024,128]{1,0:T(8,128)(2,1)S(1)} %get-tuple-element.42.refs_0_), channel_id=1, source_target_pairs={{0,4},{4,0},{8,12},{12,8},{16,20},{20,16},{24,28},{28,24},{1,5},{5... | collective-permute-start | bytes 786440 | tf_op jit(solution)/shard_map/core/ppermute | solution.py:47
  59.9 3.4 %collective-permute-start.12 = (bf16[1024,128]{1,0:T(8,128)(2,1)S(1)}, bf16[1024,128]{1,0:T(8,128)(2,1)S(1)}, u32[]{:S(2)}, u32[]{:S(2)}) collective-permute-start(bf16[1024,128]{1,0:T(8,128)(2,1)S(1)} %get-tuple-element.43.refs_1_), channel_id=1, source_target_pairs={{0,4},{4,0},{8,12},{12,8},{16,20},{20,16},{24,28},{28,24},{1,5},{5... | collective-permute-start | bytes 786440 | tf_op jit(solution)/shard_map/core/ppermute | solution.py:47
  60.5 2.9 %collective-permute-start.13 = (bf16[1024,128]{1,0:T(8,128)(2,1)S(1)}, bf16[1024,128]{1,0:T(8,128)(2,1)S(1)}, u32[]{:S(2)}, u32[]{:S(2)}) collective-permute-start(bf16[1024,128]{1,0:T(8,128)(2,1)S(1)} %get-tuple-element.44.refs_2_), channel_id=1, source_target_pairs={{0,4},{4,0},{8,12},{12,8},{16,20},{20,16},{24,28},{28,24},{1,5},{5... | collective-permute-start | bytes 786440 | tf_op jit(solution)/shard_map/core/ppermute | solution.py:47
  61.8 1.5 %collective-permute-start.14 = (bf16[1024,128]{1,0:T(8,128)(2,1)S(1)}, bf16[1024,128]{1,0:T(8,128)(2,1)S(1)}, u32[]{:S(2)}, u32[]{:S(2)}) collective-permute-start(bf16[1024,128]{1,0:T(8,128)(2,1)S(1)} %get-tuple-element.45.refs_3_), channel_id=1, source_target_pairs={{0,4},{4,0},{8,12},{12,8},{16,20},{20,16},{24,28},{28,24},{1,5},{5... | collective-permute-start | bytes 786440 | tf_op jit(solution)/shard_map/core/ppermute | solution.py:47

commit v6 on v5

--- a/solution.py
+++ b/solution.py
@@ -6,29 +6,33 @@
 from jax.sharding import PartitionSpec as P
 
 
-YAFTER = {'3a': ['2a'], '1a': ['2b'], '1b': ['3a'], '3b': ['1a'], '0a': ['1b'], '0b': ['3b']}
-FIRST = 2
+CHUNKS = [
+    ("h", 0, 8),
+    ("h", 8, 16),
+    ("f", 0, 8),
+    ("n", 0, 8),
+    ("n", 8, 16),
+    ("f", 8, 16),
+    ("0", 0, 8),
+    ("0", 8, 16),
+]
+ROW_AFTER = {"3a": "2a", "1a": "2b", "1b": "3a", "3b": "1a", "0a": "1b", "0b": "3b"}
+WAITS = {
+    "3a": ["z2a"],
+    "1b": ["z2b", "g2"],
+    "0a": ["z3a", "z1b", "v", "z3b"],
+    "0b": ["z1a", "p1", "p2", "p3"],
+}
+GATHER, VECTORS = "2b", "1b"
 CORE_PARTS = 4
-GATHER = '2b'
-VECTORS = '1b'
-ZAFTER = {}
-FINISH = 1000
-PFLOPS = (1000, 1000)
-CFLOPS = 1000
-ASSEMBLE = 1000
-WAITS = {'3a': ['z2a'], '1b': ['g1', 'z2b', 'g2'], '0a': ['z3a', 'z1b', 'v', 'z3b'], '0b': ['z1a', 'p0', 'p1', 'p2', 'p3']}
-
-
-TOKENS = [('h', 0, 8), ('h', 8, 16), ('f', 0, 8), ('n', 0, 8), ('n', 8, 16), ('f', 8, 16), ('0', 0, 8), ('0', 8, 16)]
 
 
 def chunks_of(half, count):
     kinds = {"h": [half], "f": range(half + 1, count), "n": range(1, half), "0": [0]}
-    return [(step, lo, hi) for kind, lo, hi in TOKENS for step in kinds[kind]]
-
-
-def estimate(flops=1000):
-    return pl.CostEstimate(flops=flops, bytes_accessed=flops // 1000, transcendentals=0)
+    return [(step, lo, hi) for kind, lo, hi in CHUNKS for step in kinds[kind]]
+
+
+ESTIMATE = pl.CostEstimate(flops=1000, bytes_accessed=1, transcendentals=0)
 
 
 def in_hbm(value):
@@ -41,18 +45,17 @@
     )
 
 
-def exchange(block, axis, flip, name="p"):
+def exchange(block, axis, flip, name):
     count = lax.axis_size(axis)
     with jax.named_scope(name):
         return lax.ppermute(block, axis, [(i, i ^ flip) for i in range(count)])
-    return lax.ppermute(block, axis, [(i, i ^ flip) for i in range(count)])
 
 
 def after(value, *earlier):
     return lax.optimization_barrier((value, *earlier))[0]
 
 
-def project(laplacian, interp, pairs, jobs, *earlier, flops=1000):
+def project(laplacian, interp, pairs, jobs, *earlier):
     tile = interp.shape[1]
     fine_rows = interp.shape[0] // tile
     coarse_rows = fine_rows // 2
@@ -120,12 +123,12 @@
             pltpu.SemaphoreType.DMA((2, len(jobs))),
         ],
         compiler_params=pltpu.CompilerParams(vmem_limit_bytes=size + 4 * 1024 * 1024),
-        cost_estimate=estimate(flops),
+        cost_estimate=ESTIMATE,
         name="project",
     )(in_hbm(pairs), in_hbm(interp), in_hbm(laplacian), *earlier)
 
 
-def combine(own, begin, received, *earlier, flops=1000):
+def combine(own, begin, received, *earlier):
     end = begin + received.shape[1]
 
     def body(own_ref, received_ref, *refs):
@@ -139,7 +142,7 @@
         + [pl.BlockSpec(memory_space=pl.ANY)] * len(earlier),
         out_specs=pl.BlockSpec(memory_space=pltpu.VMEM),
         compiler_params=pltpu.CompilerParams(vmem_limit_bytes=8 * 1024 * 1024),
-        cost_estimate=estimate(flops),
+        cost_estimate=ESTIMATE,
         name="combine",
     )(own, received, *earlier)
 
@@ -200,7 +203,7 @@
             pltpu.VMEM((len(blocks) * rows, tile), blocks[0].dtype),
             pltpu.SemaphoreType.DMA((len(blocks),)),
         ],
-        cost_estimate=estimate(ASSEMBLE),
+        cost_estimate=ESTIMATE,
         compiler_params=pltpu.CompilerParams(
             vmem_limit_bytes=len(blocks) * rows * tile * 4 + 4 * 1024 * 1024
         ),
@@ -225,7 +228,8 @@
             begin -= ref.shape[1]
 
     def body(own_ref, far_ref, *refs):
-        paired_refs, other_refs, refs = refs[:CORE_PARTS], refs[CORE_PARTS : 2 * CORE_PARTS], refs[2 * CORE_PARTS :]
+        paired_refs, other_refs = refs[:CORE_PARTS], refs[CORE_PARTS : 2 * CORE_PARTS]
+        refs = refs[2 * CORE_PARTS :]
         out_ref, vec_ref, buf, vec_buf, sem = refs[-5:]
         row, col = lax.axis_index("row"), lax.axis_index("col")
         vec = own_ref[...].astype(jnp.float32) + far_ref[...].astype(jnp.float32)
@@ -277,7 +281,7 @@
             pltpu.VMEM(own_vec.shape, jnp.bfloat16),
             pltpu.SemaphoreType.DMA((1 + 2 * len(jobs),)),
         ],
-        cost_estimate=estimate(FINISH),
+        cost_estimate=ESTIMATE,
         compiler_params=pltpu.CompilerParams(vmem_limit_bytes=size + 4 * 1024 * 1024),
         name="finish",
     )(*operands)
@@ -312,7 +316,7 @@
         + [pl.BlockSpec(memory_space=pl.ANY)] * len(earlier),
         out_specs=(pl.BlockSpec(memory_space=pltpu.VMEM),) * 2,
         compiler_params=pltpu.CompilerParams(vmem_limit_bytes=4 * 1024 * 1024),
-        cost_estimate=estimate(),
+        cost_estimate=ESTIMATE,
         name="restrict",
     )(pairs, vectors, interp, *earlier)
 
@@ -333,34 +337,32 @@
         step: [(lo * cols // 16, hi * cols // 16) for other, lo, hi in order if other == step]
         for step in steps
     }
-    labels = [f"{step}{'abcdefgh'[spans[step].index((lo * cols // 16, hi * cols // 16))]}" for step, lo, hi in order]
     first, rest = steps[0], steps[1:]
     cut = len(spans[first])
-    sent = project(laplacian, interp, pairs, [(first, False, jnp.bfloat16, spans[first][:FIRST])])
-    jobs = [(first, False, jnp.bfloat16, spans[first][FIRST:])] if FIRST < cut else []
-    jobs += [(s, False, jnp.bfloat16, spans[s]) for s in rest]
-    sent += project(laplacian, interp, pairs, jobs, sent[0], flops=PFLOPS[0])
+    sent = project(laplacian, interp, pairs, [(first, False, jnp.bfloat16, spans[first])])
+    jobs = [(s, False, jnp.bfloat16, spans[s]) for s in rest]
+    sent += project(laplacian, interp, pairs, jobs, sent[0])
     grouped = [(step, span) for step in steps for span in spans[step]]
     sent = dict(zip(grouped, sent))
     kept = project(
-        laplacian, interp, pairs, [(s, True, jnp.float32, whole) for s in steps], sent[grouped[cut]], flops=PFLOPS[1]
+        laplacian, interp, pairs, [(s, True, jnp.float32, whole) for s in steps], sent[grouped[cut]]
     )
     kept = dict(zip(steps, kept))
     named, totals, held = {}, [kept[0]], {step: [] for step in steps}
     paired = keep = None
     for k, (step, lo, hi) in enumerate(order):
-        name, span = labels[k], (lo * cols // 16, hi * cols // 16)
+        span = (lo * cols // 16, hi * cols // 16)
+        name = f"{step}{'abcdefgh'[spans[step].index(span)]}"
         block = sent[step, span]
-        if name in YAFTER:
-            block = after(block, *(named["t" + w] for w in YAFTER[name] if "t" + w in named))
+        if "t" + ROW_AFTER.get(name, "") in named:
+            block = after(block, named["t" + ROW_AFTER[name]])
         block = exchange(block, "row", row_half, "y" + name)
         waits = totals[-1:] + [named[w] for w in WAITS.get(name, ()) if w in named]
-        total = combine(kept[step], span[0], block, *waits, flops=CFLOPS)
+        total = combine(kept[step], span[0], block, *waits)
         totals.append(total)
         named["t" + name] = total
         if step:
-            later = [named[w] for w in ZAFTER.get(name, ()) if w in named]
-            total = exchange(after(total, *later) if later else total, "col", step, "z" + name)
+            total = exchange(total, "col", step, "z" + name)
         named["z" + name] = total
         held[step].append(total)
         if name == GATHER or (k + 1 == len(order) and paired is None):

time: 65.3 us -> 65.3 us (level)
  waiting for transfers between devices: 24.2 us -> 21 us
  starting transfers between devices: 27.4 us -> 30.5 us
    ppermute x22, waiting for transfers between devices: 24.2 us -> 21 us  [exchange(): return lax.ppermute(block, axis, [(i, i ^ flip) for i in range(count)])]
    ppermute x22, starting transfers between devices: 27.4 us -> 30.5 us  [exchange(): return lax.ppermute(block, axis, [(i, i ^ flip) for i in range(count)])]
  transfers between devices with their start and end apart: 22 -> 22, of which waited for: 12 -> 10; matrix products, arithmetic and copies ran while one was open for 0% -> 0% of each run, Pallas kernels for 14% -> 14%
where the time goes in v6:
time: 65.3 us; the launch traced here: 65 us
  starting transfers between devices  30.5 us (47%)
  waiting for transfers between devices  21 us (32%)
  Pallas kernels  12.7 us (19%)
  between operations  0.77 us (1%)
    ppermute x22, starting transfers between devices, exchange(): return lax.ppermute(block, axis, [(i, i ^ flip) for i in range(count)])  30.5 us
    ppermute x22, waiting for transfers between devices, exchange(): return lax.ppermute(block, axis, [(i, i ^ flip) for i in range(count)])  21 us
    pallas_call x3, Pallas kernels, project(): pl.pallas_call(body, out_shape=outs, in_specs=[pl.BlockSpec(memory_space=...  8.37 us
    pallas_call x1, Pallas kernels, finish(): pl.pallas_call(body, out_shape=(jax.ShapeDtypeStruct((count, total), jnp....  1.65 us
    pallas_call x1, Pallas kernels, assemble(): pl.pallas_call(body, out_shape=[jax.ShapeDtypeStruct((length * tile, tile...  1.49 us
  transfers between devices with their start and end apart: 22, of which 10 were waited for; matrix products, arithmetic and copies ran while one was open for 0% of the time, Pallas kernels for 14%

profile of v6, /device:TPU:0, one launch (start us, length us, event | category | flops | bytes accessed | tf_op | source)
XLA Modules:
  0.0 65.0 jit_solution(7167062606106091223)
XLA Ops:
  0.6 2.2 %project.3 = (bf16[128,1024]{1,0:T(8,128)(2,1)S(1)}, bf16[128,1024]{1,0:T(8,128)(2,1)S(1)}) custom-call(s32[2,32]{1,0:T(2,128)} %bitcast.1, bf16[1024,128]{1,0:T(8,128)(2,1)} %refs_0_, bf16[1024,2048]{1,0:T(8,128)(2,1)} %lap_ref.5), custom_call_target="tpu_custom_call" | custom-call | flops 1000 | bytes 1 | tf_op jit(solution)/shard_map/project/pallas_call | solution.py:113
  2.8 3.0 %collective-permute-start = (bf16[128,1024]{1,0:T(8,128)(2,1)S(1)}, bf16[128,1024]{1,0:T(8,128)(2,1)S(1)}, u32[]{:S(2)}, u32[]{:S(2)}) collective-permute-start(bf16[128,1024]{1,0:T(8,128)(2,1)S(1)} %get-tuple-element.27.refs_0_), channel_id=1, source_target_pairs={{0,16},{4,20},{8,24},{12,28},{16,0},{20,4},{24,8},{28,12},{1,17},{... | collective-permute-start | bytes 786440 | tf_op jit(solution)/shard_map/y2a/ppermute | solution.py:51
  5.9 2.9 %project.4 = (bf16[128,1024]{1,0:T(8,128)(2,1)S(1)}, bf16[128,1024]{1,0:T(8,128)(2,1)S(1)}, bf16[128,1024]{1,0:T(8,128)(2,1)S(1)}, bf16[128,1024]{1,0:T(8,128)(2...) custom-call(s32[2,32]{1,0:T(2,128)} %bitcast.2, bf16[1024,128]{1,0:T(8,128)(2,1)} %refs_0_, ...), custom_call_target="tpu_custom_call" | custom-call | flops 1000 | bytes 1 | tf_op jit(solution)/shard_map/project/pallas_call | solution.py:113
  8.8 3.3 %project.5 = (f32[128,2048]{1,0:T(8,128)S(1)}, f32[128,2048]{1,0:T(8,128)S(1)}, f32[128,2048]{1,0:T(8,128)S(1)}, f32[128,2048]{1,0:T(8,128)S(1)}) custom-call(s32[2,32]{1,0:T(2,128)} %bitcast.3, bf16[1024,128]{1,0:T(8,128)(2,1)} %refs_0_, bf16[1024,2048]{1,0:T(8,128)(2,1)} %lap_ref.5, bf16[128,1024]{1,0:T(8,128)(2,1)S(1)} %get-tuple-element.34.refs_0_), custom_call_target="tpu_custom_call" | custom-call | flops 1000 | bytes 1 | tf_op jit(solution)/shard_map/project/pallas_call | solution.py:113
  12.1 0.8 %collective-permute-done.received_ref = bf16[128,1024]{1,0:T(8,128)(2,1)S(1)} collective-permute-done((bf16[128,1024]{1,0:T(8,128)(2,1)S(1)}, bf16[128,1024]{1,0:T(8,128)(2,1)S(1)}, u32[]{:S(2)}, u32[]{:S(2)}) %collective-permute-start) | collective-permute-done | bytes 262176 | tf_op jit(solution)/shard_map/y2a/ppermute | solution.py:51
  13.0 3.2 %collective-permute-start.3 = (bf16[128,1024]{1,0:T(8,128)(2,1)S(1)}, bf16[128,1024]{1,0:T(8,128)(2,1)S(1)}, u32[]{:S(2)}, u32[]{:S(2)}) collective-permute-start(bf16[128,1024]{1,0:T(8,128)(2,1)S(1)} %combine.8.refs_0_), channel_id=1, source_target_pairs={{0,2},{1,3},{2,0},{3,1},{4,6},{5,7},{6,4},{7,5},{8,10},{9,11},{10,... | collective-permute-start | bytes 786440 | tf_op jit(solution)/shard_map/z2a/ppermute | solution.py:51
  16.2 1.5 %collective-permute-start.1 = (bf16[128,1024]{1,0:T(8,128)(2,1)S(1)}, bf16[128,1024]{1,0:T(8,128)(2,1)S(1)}, u32[]{:S(2)}, u32[]{:S(2)}) collective-permute-start(bf16[128,1024]{1,0:T(8,128)(2,1)S(1)} %get-tuple-element.34.refs_0_), channel_id=1, source_target_pairs={{0,16},{4,20},{8,24},{12,28},{16,0},{20,4},{24,8},{28,12},{1,17},{... | collective-permute-start | bytes 786440 | tf_op jit(solution)/shard_map/y3a/ppermute | solution.py:51
  17.7 0.8 %collective-permute-done.2.received_ref = bf16[128,1024]{1,0:T(8,128)(2,1)S(1)} collective-permute-done((bf16[128,1024]{1,0:T(8,128)(2,1)S(1)}, bf16[128,1024]{1,0:T(8,128)(2,1)S(1)}, u32[]{:S(2)}, u32[]{:S(2)}) %collective-permute-start.2) | collective-permute-done | bytes 262176 | tf_op jit(solution)/shard_map/y2b/ppermute | solution.py:51
  18.7 2.0 %collective-permute-start.5 = (bf16[128,1024]{1,0:T(8,128)(2,1)S(1)}, bf16[128,1024]{1,0:T(8,128)(2,1)S(1)}, u32[]{:S(2)}, u32[]{:S(2)}) collective-permute-start(bf16[128,1024]{1,0:T(8,128)(2,1)S(1)} %get-tuple-element.38), channel_id=1, source_target_pairs={{0,16},{4,20},{8,24},{12,28},{16,0},{20,4},{24,8},{28,12},{1,17},{... | collective-permute-start | bytes 786440 | tf_op jit(solution)/shard_map/y1a/ppermute | solution.py:51
  20.7 1.5 %collective-permute-start.7 = (bf16[1024,128]{1,0:T(8,128)(2,1)S(1)}, bf16[1024,128]{1,0:T(8,128)(2,1)S(1)}, u32[]{:S(2)}, u32[]{:S(2)}) collective-permute-start(bf16[1024,128]{1,0:T(8,128)(2,1)S(1)} %copy-done), channel_id=1, source_target_pairs={{0,8},{4,12},{8,0},{12,4},{16,24},{20,28},{24,16},{28,20},{1,9},{5... | collective-permute-start | bytes 786440 | tf_op jit(solution)/shard_map/gather2/ppermute | solution.py:51
  22.2 0.5 collective-permute-start.9
  22.7 2.8 %collective-permute-done.1.received_ref = bf16[128,1024]{1,0:T(8,128)(2,1)S(1)} collective-permute-done((bf16[128,1024]{1,0:T(8,128)(2,1)S(1)}, bf16[128,1024]{1,0:T(8,128)(2,1)S(1)}, u32[]{:S(2)}, u32[]{:S(2)}) %collective-permute-start.1) | collective-permute-done | bytes 262176 | tf_op jit(solution)/shard_map/y3a/ppermute | solution.py:51
  25.5 1.9 %collective-permute-start.6 = (bf16[128,1024]{1,0:T(8,128)(2,1)S(1)}, bf16[128,1024]{1,0:T(8,128)(2,1)S(1)}, u32[]{:S(2)}, u32[]{:S(2)}) collective-permute-start(bf16[128,1024]{1,0:T(8,128)(2,1)S(1)} %combine.9.refs_0_), channel_id=1, source_target_pairs={{0,2},{1,3},{2,0},{3,1},{4,6},{5,7},{6,4},{7,5},{8,10},{9,11},{10,... | collective-permute-start | bytes 786440 | tf_op jit(solution)/shard_map/z2b/ppermute | solution.py:51
  27.3 2.7 %collective-permute-done.3.refs_1_.refs_10_ = bf16[128,1024]{1,0:T(8,128)(2,1)S(1)} collective-permute-done((bf16[128,1024]{1,0:T(8,128)(2,1)S(1)}, bf16[128,1024]{1,0:T(8,128)(2,1)S(1)}, u32[]{:S(2)}, u32[]{:S(2)}) %collective-permute-start.3) | collective-permute-done | bytes 262176 | tf_op jit(solution)/shard_map/z2a/ppermute | solution.py:51
  30.1 1.0 %collective-permute-done.5.received_ref = bf16[128,1024]{1,0:T(8,128)(2,1)S(1)} collective-permute-done((bf16[128,1024]{1,0:T(8,128)(2,1)S(1)}, bf16[128,1024]{1,0:T(8,128)(2,1)S(1)}, u32[]{:S(2)}, u32[]{:S(2)}) %collective-permute-start.5) | collective-permute-done | bytes 262176 | tf_op jit(solution)/shard_map/y1a/ppermute | solution.py:51
  31.2 1.6 %collective-permute-start.4 = (bf16[128,1024]{1,0:T(8,128)(2,1)S(1)}, bf16[128,1024]{1,0:T(8,128)(2,1)S(1)}, u32[]{:S(2)}, u32[]{:S(2)}) collective-permute-start(bf16[128,1024]{1,0:T(8,128)(2,1)S(1)} %get-tuple-element.36), channel_id=1, source_target_pairs={{0,16},{4,20},{8,24},{12,28},{16,0},{20,4},{24,8},{28,12},{1,17},{... | collective-permute-start | bytes 786440 | tf_op jit(solution)/shard_map/y1b/ppermute | solution.py:51
  32.7 0.5 collective-permute-start.16
  33.2 4.9 %collective-permute-start.17 = (bf16[128,1024]{1,0:T(8,128)(2,1)S(1)}, bf16[128,1024]{1,0:T(8,128)(2,1)S(1)}, u32[]{:S(2)}, u32[]{:S(2)}) collective-permute-start(bf16[128,1024]{1,0:T(8,128)(2,1)S(1)} %combine.10.refs_0_), channel_id=1, source_target_pairs={{0,3},{1,2},{2,1},{3,0},{4,7},{5,6},{6,5},{7,4},{8,11},{9,10},{10,... | collective-permute-start | bytes 786440 | tf_op jit(solution)/shard_map/z3a/ppermute | solution.py:51
  38.1 1.5 %collective-permute-start.10 = (bf16[1024,128]{1,0:T(8,128)(2,1)S(1)}, bf16[1024,128]{1,0:T(8,128)(2,1)S(1)}, u32[]{:S(2)}, u32[]{:S(2)}) collective-permute-start(bf16[1024,128]{1,0:T(8,128)(2,1)S(1)} %collective-permute-done.9.refs_1_), channel_id=1, source_target_pairs={{0,8},{4,12},{8,0},{12,4},{16,24},{20,28},{24,16},{28,20},{1,9},{5... | collective-permute-start | bytes 786440 | tf_op jit(solution)/shard_map/gather2/ppermute | solution.py:51
  39.6 3.4 %collective-permute-done.6.refs_1_.refs_11_ = bf16[128,1024]{1,0:T(8,128)(2,1)S(1)} collective-permute-done((bf16[128,1024]{1,0:T(8,128)(2,1)S(1)}, bf16[128,1024]{1,0:T(8,128)(2,1)S(1)}, u32[]{:S(2)}, u32[]{:S(2)}) %collective-permute-start.6) | collective-permute-done | bytes 262176 | tf_op jit(solution)/shard_map/z2b/ppermute | solution.py:51
  43.1 2.8 %collective-permute-done.16.received_ref = bf16[128,1024]{1,0:T(8,128)(2,1)S(1)} collective-permute-done((bf16[128,1024]{1,0:T(8,128)(2,1)S(1)}, bf16[128,1024]{1,0:T(8,128)(2,1)S(1)}, u32[]{:S(2)}, u32[]{:S(2)}) %collective-permute-start.16) | collective-permute-done | bytes 262176 | tf_op jit(solution)/shard_map/y3b/ppermute | solution.py:51
  45.9 4.1 %collective-permute-start.19 = (bf16[128,1024]{1,0:T(8,128)(2,1)S(1)}, bf16[128,1024]{1,0:T(8,128)(2,1)S(1)}, u32[]{:S(2)}, u32[]{:S(2)}) collective-permute-start(bf16[128,1024]{1,0:T(8,128)(2,1)S(1)} %combine.13.refs_0_), channel_id=1, source_target_pairs={{0,3},{1,2},{2,1},{3,0},{4,7},{5,6},{6,5},{7,4},{8,11},{9,10},{10,... | collective-permute-start | bytes 786440 | tf_op jit(solution)/shard_map/z3b/ppermute | solution.py:51
  50.0 1.5 %collective-permute-start.15 = (bf16[128,1024]{1,0:T(8,128)(2,1)S(1)}, bf16[128,1024]{1,0:T(8,128)(2,1)S(1)}, u32[]{:S(2)}, u32[]{:S(2)}) collective-permute-start(bf16[128,1024]{1,0:T(8,128)(2,1)S(1)} %get-tuple-element.47), channel_id=1, source_target_pairs={{0,16},{4,20},{8,24},{12,28},{16,0},{20,4},{24,8},{28,12},{1,17},{... | collective-permute-start | bytes 786440 | tf_op jit(solution)/shard_map/y0a/ppermute | solution.py:51
  51.5 0.8 %restrict.1 = (bf16[32,512]{1,0:T(8,128)(2,1)S(1)}, bf16[32,512]{1,0:T(8,128)(2,1)S(1)}) custom-call(s32[2,32]{1,0:T(2,128)S(1)} %bitcast.5, bf16[32,1024]{1,0:T(8,128)(2,1)S(1)} %copy-done.1, bf16[1024,128]{1,0:T(8,128)(2,1)S(1)} %copy-done, bf16[128,1024]{1,0:T(8,128)(2,1)S(1)} %combine.12.refs_0_), custom_call_target="tpu_custom_call" | custom-call | flops 1000 | bytes 1 | tf_op jit(solution)/shard_map/restrict/pallas_call | solution.py:308
  52.3 0.6 collective-permute-start.8
  52.9 1.5 %assemble.1 = (bf16[1024,128]{1,0:T(8,128)(2,1)S(1)}, bf16[1024,128]{1,0:T(8,128)(2,1)S(1)}, bf16[1024,128]{1,0:T(8,128)(2,1)S(1)}, bf16[1024,128]{1,0:T(8,128)(2,1)S(1)}) custom-call(s32[2,32]{1,0:T(2,128)} %bitcast.4, bf16[1024,128]{1,0:T(8,128)(2,1)S(1)} %copy-done, bf16[1024,128]{1,0:T(8,128)(2,1)S(1)} %collective-permute-done.9.refs_1_, ...), custom_call_target="tpu_custom_call" | custom-call | flops 1000 | bytes 1 | tf_op jit(solution)/shard_map/assemble/pallas_call | solution.py:196
  54.4 1.6 %collective-permute-start.20 = (bf16[128,1024]{1,0:T(8,128)(2,1)S(1)}, bf16[128,1024]{1,0:T(8,128)(2,1)S(1)}, u32[]{:S(2)}, u32[]{:S(2)}) collective-permute-start(bf16[128,1024]{1,0:T(8,128)(2,1)S(1)} %get-tuple-element.51), channel_id=1, source_target_pairs={{0,16},{4,20},{8,24},{12,28},{16,0},{20,4},{24,8},{28,12},{1,17},{... | collective-permute-start | bytes 786440 | tf_op jit(solution)/shard_map/y0b/ppermute | solution.py:51
  56.0 3.5 %collective-permute-done.8.refs_3_.far_ref = bf16[32,512]{1,0:T(8,128)(2,1)S(1)} collective-permute-done((bf16[32,512]{1,0:T(8,128)(2,1)S(1)}, bf16[32,512]{1,0:T(8,128)(2,1)S(1)}, u32[]{:S(2)}, u32[]{:S(2)}) %collective-permute-start.8) | collective-permute-done | bytes 32800 | tf_op jit(solution)/shard_map/vectors/ppermute | solution.py:51
  59.5 0.5 collective-permute-start.13
  60.0 1.2 %collective-permute-done.18.refs_2_.refs_13_ = bf16[128,1024]{1,0:T(8,128)(2,1)S(1)} collective-permute-done((bf16[128,1024]{1,0:T(8,128)(2,1)S(1)}, bf16[128,1024]{1,0:T(8,128)(2,1)S(1)}, u32[]{:S(2)}, u32[]{:S(2)}) %collective-permute-start.18) | collective-permute-done | bytes 262176 | tf_op jit(solution)/shard_map/z1b/ppermute | solution.py:51
  61.3 2.0 %collective-permute-done.20.received_ref = bf16[128,1024]{1,0:T(8,128)(2,1)S(1)} collective-permute-done((bf16[128,1024]{1,0:T(8,128)(2,1)S(1)}, bf16[128,1024]{1,0:T(8,128)(2,1)S(1)}, u32[]{:S(2)}, u32[]{:S(2)}) %collective-permute-start.20) | collective-permute-done | bytes 262176 | tf_op jit(solution)/shard_map/y0b/ppermute | solution.py:51
  63.4 1.7 %finish.1 = (bf16[128,4096]{1,0:T(8,128)(2,1)}, bf16[32,512]{1,0:T(8,128)(2,1)}) custom-call(bf16[32,512]{1,0:T(8,128)(2,1)S(1)} %get-tuple-element.40.own_ref, bf16[32,512]{1,0:T(8,128)(2,1)S(1)} %collective-permute-done.8.refs_3_.far_ref, bf16[1024,128]{1,0:T(8,128)(2,1)S(1)} %get-tuple-element.42.refs_0_, ...), custom_call_target="tpu_custom_call" | custom-call | flops 1000 | bytes 1 | tf_op jit(solution)/shard_map/finish/pallas_call | solution.py:271
  (32 shorter events, 0.7 us)
Async XLA Ops:
  2.8 10.2 %collective-permute-start = (bf16[128,1024]{1,0:T(8,128)(2,1)S(1)}, bf16[128,1024]{1,0:T(8,128)(2,1)S(1)}, u32[]{:S(2)}, u32[]{:S(2)}) collective-permute-start(bf16[128,1024]{1,0:T(8,128)(2,1)S(1)} %get-tuple-element.27.refs_0_), channel_id=1, source_target_pairs={{0,16},{4,20},{8,24},{12,28},{16,0},{20,4},{24,8},{28,12},{1,17},{... | collective-permute-start | bytes 786440 | tf_op jit(solution)/shard_map/y2a/ppermute | solution.py:51
  5.8 12.8 %collective-permute-start.2 = (bf16[128,1024]{1,0:T(8,128)(2,1)S(1)}, bf16[128,1024]{1,0:T(8,128)(2,1)S(1)}, u32[]{:S(2)}, u32[]{:S(2)}) collective-permute-start(bf16[128,1024]{1,0:T(8,128)(2,1)S(1)} %get-tuple-element.35), channel_id=1, source_target_pairs={{0,16},{4,20},{8,24},{12,28},{16,0},{20,4},{24,8},{28,12},{1,17},{... | collective-permute-start | bytes 786440 | tf_op jit(solution)/shard_map/y2b/ppermute | solution.py:51
  8.8 11.9 %copy-start = (bf16[1024,128]{1,0:T(8,128)(2,1)S(1)}, bf16[1024,128]{1,0:T(8,128)(2,1)}, u32[]{:S(2)}) copy-start(bf16[1024,128]{1,0:T(8,128)(2,1)} %refs_0_) | copy-start | bytes 786436
  13.0 17.0 %collective-permute-start.3 = (bf16[128,1024]{1,0:T(8,128)(2,1)S(1)}, bf16[128,1024]{1,0:T(8,128)(2,1)S(1)}, u32[]{:S(2)}, u32[]{:S(2)}) collective-permute-start(bf16[128,1024]{1,0:T(8,128)(2,1)S(1)} %combine.8.refs_0_), channel_id=1, source_target_pairs={{0,2},{1,3},{2,0},{3,1},{4,6},{5,7},{6,4},{7,5},{8,10},{9,11},{10,... | collective-permute-start | bytes 786440 | tf_op jit(solution)/shard_map/z2a/ppermute | solution.py:51
  16.2 9.2 %collective-permute-start.1 = (bf16[128,1024]{1,0:T(8,128)(2,1)S(1)}, bf16[128,1024]{1,0:T(8,128)(2,1)S(1)}, u32[]{:S(2)}, u32[]{:S(2)}) collective-permute-start(bf16[128,1024]{1,0:T(8,128)(2,1)S(1)} %get-tuple-element.34.refs_0_), channel_id=1, source_target_pairs={{0,16},{4,20},{8,24},{12,28},{16,0},{20,4},{24,8},{28,12},{1,17},{... | collective-permute-start | bytes 786440 | tf_op jit(solution)/shard_map/y3a/ppermute | solution.py:51
  18.6 32.9 %copy-start.1 = (bf16[32,1024]{1,0:T(8,128)(2,1)S(1)}, bf16[32,1024]{1,0:T(8,128)(2,1)}, u32[]{:S(2)}) copy-start(bf16[32,1024]{1,0:T(8,128)(2,1)} %vec_ref.1) | copy-start | bytes 196612
  18.7 32.9 %copy-start.2 = (s32[32,2]{0,1:T(2,128)S(1)}, s32[32,2]{0,1:T(2,128)}, u32[]{:S(2)}) copy-start(s32[32,2]{0,1:T(2,128)} %param.7) | copy-start | bytes 772
  18.7 12.4 %collective-permute-start.5 = (bf16[128,1024]{1,0:T(8,128)(2,1)S(1)}, bf16[128,1024]{1,0:T(8,128)(2,1)S(1)}, u32[]{:S(2)}, u32[]{:S(2)}) collective-permute-start(bf16[128,1024]{1,0:T(8,128)(2,1)S(1)} %get-tuple-element.38), channel_id=1, source_target_pairs={{0,16},{4,20},{8,24},{12,28},{16,0},{20,4},{24,8},{28,12},{1,17},{... | collective-permute-start | bytes 786440 | tf_op jit(solution)/shard_map/y1a/ppermute | solution.py:51
  20.7 12.6 %collective-permute-start.7 = (bf16[1024,128]{1,0:T(8,128)(2,1)S(1)}, bf16[1024,128]{1,0:T(8,128)(2,1)S(1)}, u32[]{:S(2)}, u32[]{:S(2)}) collective-permute-start(bf16[1024,128]{1,0:T(8,128)(2,1)S(1)} %copy-done), channel_id=1, source_target_pairs={{0,8},{4,12},{8,0},{12,4},{16,24},{20,28},{24,16},{28,20},{1,9},{5... | collective-permute-start | bytes 786440 | tf_op jit(solution)/shard_map/gather2/ppermute | solution.py:51
  22.2 16.0 %collective-permute-start.9 = (bf16[1024,128]{1,0:T(8,128)(2,1)S(1)}, bf16[1024,128]{1,0:T(8,128)(2,1)S(1)}, u32[]{:S(2)}, u32[]{:S(2)}) collective-permute-start(bf16[1024,128]{1,0:T(8,128)(2,1)S(1)} %copy-done), channel_id=1, source_target_pairs={{0,16},{4,20},{8,24},{12,28},{16,0},{20,4},{24,8},{28,12},{1,17},{... | collective-permute-start | bytes 786440 | tf_op jit(solution)/shard_map/gather4/ppermute | solution.py:51
  25.5 17.5 %collective-permute-start.6 = (bf16[128,1024]{1,0:T(8,128)(2,1)S(1)}, bf16[128,1024]{1,0:T(8,128)(2,1)S(1)}, u32[]{:S(2)}, u32[]{:S(2)}) collective-permute-start(bf16[128,1024]{1,0:T(8,128)(2,1)S(1)} %combine.9.refs_0_), channel_id=1, source_target_pairs={{0,2},{1,3},{2,0},{3,1},{4,6},{5,7},{6,4},{7,5},{8,10},{9,11},{10,... | collective-permute-start | bytes 786440 | tf_op jit(solution)/shard_map/z2b/ppermute | solution.py:51
  31.2 11.9 %collective-permute-start.4 = (bf16[128,1024]{1,0:T(8,128)(2,1)S(1)}, bf16[128,1024]{1,0:T(8,128)(2,1)S(1)}, u32[]{:S(2)}, u32[]{:S(2)}) collective-permute-start(bf16[128,1024]{1,0:T(8,128)(2,1)S(1)} %get-tuple-element.36), channel_id=1, source_target_pairs={{0,16},{4,20},{8,24},{12,28},{16,0},{20,4},{24,8},{28,12},{1,17},{... | collective-permute-start | bytes 786440 | tf_op jit(solution)/shard_map/y1b/ppermute | solution.py:51
  32.7 13.1 %collective-permute-start.16 = (bf16[128,1024]{1,0:T(8,128)(2,1)S(1)}, bf16[128,1024]{1,0:T(8,128)(2,1)S(1)}, u32[]{:S(2)}, u32[]{:S(2)}) collective-permute-start(bf16[128,1024]{1,0:T(8,128)(2,1)S(1)} %get-tuple-element.49), channel_id=1, source_target_pairs={{0,16},{4,20},{8,24},{12,28},{16,0},{20,4},{24,8},{28,12},{1,17},{... | collective-permute-start | bytes 786440 | tf_op jit(solution)/shard_map/y3b/ppermute | solution.py:51
  33.2 18.3 %collective-permute-start.17 = (bf16[128,1024]{1,0:T(8,128)(2,1)S(1)}, bf16[128,1024]{1,0:T(8,128)(2,1)S(1)}, u32[]{:S(2)}, u32[]{:S(2)}) collective-permute-start(bf16[128,1024]{1,0:T(8,128)(2,1)S(1)} %combine.10.refs_0_), channel_id=1, source_target_pairs={{0,3},{1,2},{2,1},{3,0},{4,7},{5,6},{6,5},{7,4},{8,11},{9,10},{10,... | collective-permute-start | bytes 786440 | tf_op jit(solution)/shard_map/z3a/ppermute | solution.py:51
  38.1 14.1 %collective-permute-start.10 = (bf16[1024,128]{1,0:T(8,128)(2,1)S(1)}, bf16[1024,128]{1,0:T(8,128)(2,1)S(1)}, u32[]{:S(2)}, u32[]{:S(2)}) collective-permute-start(bf16[1024,128]{1,0:T(8,128)(2,1)S(1)} %collective-permute-done.9.refs_1_), channel_id=1, source_target_pairs={{0,8},{4,12},{8,0},{12,4},{16,24},{20,28},{24,16},{28,20},{1,9},{5... | collective-permute-start | bytes 786440 | tf_op jit(solution)/shard_map/gather2/ppermute | solution.py:51
  43.0 11.4 %collective-permute-start.21 = (bf16[128,1024]{1,0:T(8,128)(2,1)S(1)}, bf16[128,1024]{1,0:T(8,128)(2,1)S(1)}, u32[]{:S(2)}, u32[]{:S(2)}) collective-permute-start(bf16[128,1024]{1,0:T(8,128)(2,1)S(1)} %combine.11.refs_0_), channel_id=1, source_target_pairs={{0,1},{1,0},{2,3},{3,2},{4,5},{5,4},{6,7},{7,6},{8,9},{9,8},{10,11... | collective-permute-start | bytes 786440 | tf_op jit(solution)/shard_map/z1a/ppermute | solution.py:51
  45.9 13.6 %collective-permute-start.19 = (bf16[128,1024]{1,0:T(8,128)(2,1)S(1)}, bf16[128,1024]{1,0:T(8,128)(2,1)S(1)}, u32[]{:S(2)}, u32[]{:S(2)}) collective-permute-start(bf16[128,1024]{1,0:T(8,128)(2,1)S(1)} %combine.13.refs_0_), channel_id=1, source_target_pairs={{0,3},{1,2},{2,1},{3,0},{4,7},{5,6},{6,5},{7,4},{8,11},{9,10},{10,... | collective-permute-start | bytes 786440 | tf_op jit(solution)/shard_map/z3b/ppermute | solution.py:51
  50.0 10.0 %collective-permute-start.15 = (bf16[128,1024]{1,0:T(8,128)(2,1)S(1)}, bf16[128,1024]{1,0:T(8,128)(2,1)S(1)}, u32[]{:S(2)}, u32[]{:S(2)}) collective-permute-start(bf16[128,1024]{1,0:T(8,128)(2,1)S(1)} %get-tuple-element.47), channel_id=1, source_target_pairs={{0,16},{4,20},{8,24},{12,28},{16,0},{20,4},{24,8},{28,12},{1,17},{... | collective-permute-start | bytes 786440 | tf_op jit(solution)/shard_map/y0a/ppermute | solution.py:51
  51.5 9.7 %collective-permute-start.18 = (bf16[128,1024]{1,0:T(8,128)(2,1)S(1)}, bf16[128,1024]{1,0:T(8,128)(2,1)S(1)}, u32[]{:S(2)}, u32[]{:S(2)}) collective-permute-start(bf16[128,1024]{1,0:T(8,128)(2,1)S(1)} %combine.12.refs_0_), channel_id=1, source_target_pairs={{0,1},{1,0},{2,3},{3,2},{4,5},{5,4},{6,7},{7,6},{8,9},{9,8},{10,11... | collective-permute-start | bytes 786440 | tf_op jit(solution)/shard_map/z1b/ppermute | solution.py:51
  52.3 7.2 %collective-permute-start.8 = (bf16[32,512]{1,0:T(8,128)(2,1)S(1)}, bf16[32,512]{1,0:T(8,128)(2,1)S(1)}, u32[]{:S(2)}, u32[]{:S(2)}) collective-permute-start(bf16[32,512]{1,0:T(8,128)(2,1)S(1)} %get-tuple-element.41), channel_id=1, source_target_pairs={{0,16},{4,20},{8,24},{12,28},{16,0},{20,4},{24,8},{28,12},{1,17},{... | collective-permute-start | bytes 98312 | tf_op jit(solution)/shard_map/vectors/ppermute | solution.py:51
  54.4 8.9 %collective-permute-start.20 = (bf16[128,1024]{1,0:T(8,128)(2,1)S(1)}, bf16[128,1024]{1,0:T(8,128)(2,1)S(1)}, u32[]{:S(2)}, u32[]{:S(2)}) collective-permute-start(bf16[128,1024]{1,0:T(8,128)(2,1)S(1)} %get-tuple-element.51), channel_id=1, source_target_pairs={{0,16},{4,20},{8,24},{12,28},{16,0},{20,4},{24,8},{28,12},{1,17},{... | collective-permute-start | bytes 786440 | tf_op jit(solution)/shard_map/y0b/ppermute | solution.py:51
  59.5 3.8 %collective-permute-start.12 = (bf16[1024,128]{1,0:T(8,128)(2,1)S(1)}, bf16[1024,128]{1,0:T(8,128)(2,1)S(1)}, u32[]{:S(2)}, u32[]{:S(2)}) collective-permute-start(bf16[1024,128]{1,0:T(8,128)(2,1)S(1)} %get-tuple-element.43.refs_1_), channel_id=1, source_target_pairs={{0,4},{4,0},{8,12},{12,8},{16,20},{20,16},{24,28},{28,24},{1,5},{5... | collective-permute-start | bytes 786440 | tf_op jit(solution)/shard_map/core/ppermute | solution.py:51
  59.5 3.8 %collective-permute-start.13 = (bf16[1024,128]{1,0:T(8,128)(2,1)S(1)}, bf16[1024,128]{1,0:T(8,128)(2,1)S(1)}, u32[]{:S(2)}, u32[]{:S(2)}) collective-permute-start(bf16[1024,128]{1,0:T(8,128)(2,1)S(1)} %get-tuple-element.44.refs_2_), channel_id=1, source_target_pairs={{0,4},{4,0},{8,12},{12,8},{16,20},{20,16},{24,28},{28,24},{1,5},{5... | collective-permute-start | bytes 786440 | tf_op jit(solution)/shard_map/core/ppermute | solution.py:51
  60.0 3.3 %collective-permute-start.14 = (bf16[1024,128]{1,0:T(8,128)(2,1)S(1)}, bf16[1024,128]{1,0:T(8,128)(2,1)S(1)}, u32[]{:S(2)}, u32[]{:S(2)}) collective-permute-start(bf16[1024,128]{1,0:T(8,128)(2,1)S(1)} %get-tuple-element.45.refs_3_), channel_id=1, source_target_pairs={{0,4},{4,0},{8,12},{12,8},{16,20},{20,16},{24,28},{28,24},{1,5},{5... | collective-permute-start | bytes 786440 | tf_op jit(solution)/shard_map/core/ppermute | solution.py:51
  61.2 2.1 %collective-permute-start.11 = (bf16[1024,128]{1,0:T(8,128)(2,1)S(1)}, bf16[1024,128]{1,0:T(8,128)(2,1)S(1)}, u32[]{:S(2)}, u32[]{:S(2)}) collective-permute-start(bf16[1024,128]{1,0:T(8,128)(2,1)S(1)} %get-tuple-element.42.refs_0_), channel_id=1, source_target_pairs={{0,4},{4,0},{8,12},{12,8},{16,20},{20,16},{24,28},{28,24},{1,5},{5... | collective-permute-start | bytes 786440 | tf_op jit(solution)/shard_map/core/ppermute | solution.py:51
